TPU v7x, 32 devices: a whole 2x2x4 slice. The times are simulated.
32 devices in a mesh: doc: 4 (over y, x), blk: 8 (over z, core).
Axes of the slice: x: 2, y: 2, z: 4, core: 2. Of those that a mesh axis runs over, the one named last changes fastest.
Arguments:
- byte_embed: bfloat16 [32, 2048, 768], P('doc', 'blk'), may hold values from -6 to 6
- doc_lengths: int32 [32], P('doc'), may hold values from 200 to 2048, as said below
- key_mask: int32 [32, 2048], P('doc', 'blk'), may hold values from 0 to 1, as said below
- latents: float32 [256, 1280], P('blk'), may hold values from -6 to 6
- gain_query: float32 [1280], replicated, may hold values from 0.1 to 1.9
- gain_bytes: float32 [768], replicated, may hold values from 0.1 to 1.9
- gain_mlp: float32 [1280], replicated, may hold values from 0.1 to 1.9
- w_query: bfloat16 [1280, 256], replicated, may hold values from -0.25 to 0.25
- w_key: bfloat16 [768, 256], replicated, may hold values from -0.21875 to 0.21875
- w_value: bfloat16 [768, 1280], replicated, may hold values from -0.21875 to 0.21875
- w_out: bfloat16 [1280, 1280], replicated, may hold values from -1.25 to 1.25
- w_up: bfloat16 [1280, 1280], replicated, may hold values from -0.15625 to 0.15625
- w_down: bfloat16 [1280, 1280], replicated, may hold values from -0.15625 to 0.15625
- cotangent: float32 [32, 256, 1280], P('doc', 'blk'), may hold values from -6 to 6
Outputs:
- latents_out: float32 [32, 256, 1280], P('doc', 'blk')
- byte_grad: float32 [32, 2048, 768], P('doc', 'blk')
- latents_grad: float32 [256, 1280], P('blk')
- gain_query_grad: float32 [1280], P('blk')
- gain_bytes_grad: float32 [768], P('blk')
- gain_mlp_grad: float32 [1280], P('blk')
- w_query_grad: float32 [1280, 256], P('blk')
- w_key_grad: float32 [768, 256], P('blk')
- w_value_grad: float32 [768, 1280], P('blk')
- w_out_grad: float32 [1280, 1280], P('blk')
- w_up_grad: float32 [1280, 1280], P('blk')
- w_down_grad: float32 [1280, 1280], P('blk')
Inputs may be any that keep to these rules, and one draw needn't show every extreme that they name: `doc_lengths`: every group of 8 documents on one index of doc holds one document of length 2048, which one drawn from the seed. `key_mask`: slot 0 of every document is 1.
All inputs are finite; a program needn't handle non-finite values.
Results may differ from a plain program's by a relative error of at most 0.029.
Values may be sent and summed in bfloat16 or wider, within the bound.
A program may use at most 192 MiB of HBM per device.

v0:
```python
import jax
import jax.numpy as jnp
from jax import lax
from jax.sharding import PartitionSpec as P

LAT = 256
HEADS = 8
QK_HEAD = 32
V_HEAD = 160


epsilon = 1e-05
masked_score = -1e30


def layer_norm(matrix, gain_vec):
    centered = matrix - jnp.mean(matrix, axis=-1, keepdims=True)
    spread = jnp.mean(centered * centered, axis=-1, keepdims=True)
    return centered * lax.rsqrt(spread + epsilon) * gain_vec


def body(
    byte_embed,
    doc_lengths,
    key_mask,
    latents,
    gain_query,
    gain_bytes,
    gain_mlp,
    w_query,
    w_key,
    w_value,
    w_out,
    w_up,
    w_down,
    cotangent,
):
    doc_count, key_count, in_width = byte_embed.shape
    row_count, model_width = latents.shape
    qk_width = HEADS * QK_HEAD
    v_width = HEADS * V_HEAD
    score_scale = QK_HEAD ** (-0.5)
    positions = lax.axis_index("blk") * key_count + jnp.arange(key_count, dtype=jnp.int32)
    usable = (positions[None, :] < doc_lengths[:, None]) & (key_mask == 1)
    normed_lat, latent_back = jax.vjp(layer_norm, latents, gain_query)
    normed_lat_low = normed_lat.astype(jnp.bfloat16)
    query_own = jnp.dot(normed_lat_low, w_query, preferred_element_type=jnp.float32).astype(
        jnp.bfloat16
    )
    query_all = lax.all_gather(query_own, "blk", axis=0, tiled=True)
    heads_q = query_all.reshape(LAT, HEADS, QK_HEAD)
    normed_bytes, bytes_back = jax.vjp(layer_norm, byte_embed.astype(jnp.float32), gain_bytes)
    flat_bytes = normed_bytes.astype(jnp.bfloat16).reshape(doc_count * key_count, in_width)
    key_rows = jnp.dot(flat_bytes, w_key, preferred_element_type=jnp.float32).astype(jnp.bfloat16)
    key_rows = key_rows.reshape(doc_count, key_count, HEADS, QK_HEAD)
    value_rows = jnp.dot(flat_bytes, w_value, preferred_element_type=jnp.float32).astype(
        jnp.bfloat16
    )
    value_rows = value_rows.reshape(doc_count, key_count, HEADS, V_HEAD)

    def masked_scores():
        scores = (
            jnp.einsum("qhd,nkhd->nhqk", heads_q, key_rows, preferred_element_type=jnp.float32)
            * score_scale
        )
        return jnp.where(usable[:, None, None, :], scores, masked_score)

    masked = masked_scores()
    row_top = lax.pmax(jnp.max(masked, axis=-1).astype(jnp.bfloat16), "blk").astype(jnp.float32)
    numerator = jnp.exp(masked - row_top[..., None])
    part_totals = jnp.sum(numerator, axis=-1).transpose(0, 2, 1)
    part_weighted = jnp.einsum(
        "nhqk,nkhd->nqhd",
        numerator.astype(jnp.bfloat16),
        value_rows,
        preferred_element_type=jnp.float32,
    ).reshape(doc_count, LAT, v_width)
    weighted, totals = (
        lax.psum_scatter(
            part_weighted.astype(jnp.bfloat16), "blk", scatter_dimension=1, tiled=True
        ).astype(jnp.float32),
        lax.psum_scatter(
            part_totals.astype(jnp.bfloat16), "blk", scatter_dimension=1, tiled=True
        ).astype(jnp.float32),
    )
    attended_heads = weighted.reshape(doc_count, row_count, HEADS, V_HEAD) / totals[..., None]
    attended = attended_heads.reshape(doc_count * row_count, v_width)
    attended_low = attended.astype(jnp.bfloat16)
    branch = jnp.dot(attended_low, w_out, preferred_element_type=jnp.float32)
    middle = (latents[None] + branch.reshape(doc_count, row_count, model_width)).reshape(
        doc_count * row_count, model_width
    )
    normed_mid, mid_back = jax.vjp(layer_norm, middle, gain_mlp)
    normed_mid_low = normed_mid.astype(jnp.bfloat16)
    up_proj = jnp.dot(normed_mid_low, w_up, preferred_element_type=jnp.float32)
    activated, gelu_back = jax.vjp(jax.nn.gelu, up_proj)
    activated_low = activated.astype(jnp.bfloat16)
    latents_out = middle + jnp.dot(activated_low, w_down, preferred_element_type=jnp.float32)
    grad_out = cotangent.reshape(doc_count * row_count, model_width)
    grad_mlp = grad_out.astype(jnp.bfloat16)
    grad_w_down = jnp.dot(activated_low.T, grad_mlp, preferred_element_type=jnp.float32)
    grad_act = jnp.dot(grad_mlp, w_down.T, preferred_element_type=jnp.float32)
    (grad_up,) = gelu_back(grad_act)
    grad_up_low = grad_up.astype(jnp.bfloat16)
    grad_w_up = jnp.dot(normed_mid_low.T, grad_up_low, preferred_element_type=jnp.float32)
    grad_norm_mid = jnp.dot(grad_up_low, w_up.T, preferred_element_type=jnp.float32)
    grad_mid_norm, grad_gain_mlp = mid_back(grad_norm_mid)
    grad_middle = grad_out + grad_mid_norm
    grad_branch = grad_middle.astype(jnp.bfloat16)
    grad_w_out = jnp.dot(attended_low.T, grad_branch, preferred_element_type=jnp.float32)
    grad_attended = jnp.dot(grad_branch, w_out.T, preferred_element_type=jnp.float32)
    grad_attended = grad_attended.reshape(doc_count, row_count, HEADS, V_HEAD)
    grad_weighted = (
        (grad_attended / totals[..., None])
        .astype(jnp.bfloat16)
        .reshape(doc_count, row_count, v_width)
    )
    grad_totals = -jnp.sum(grad_attended * attended_heads, axis=-1) / totals
    grad_weighted_all = lax.all_gather(grad_weighted, "blk", axis=1, tiled=True).reshape(
        doc_count, LAT, HEADS, V_HEAD
    )
    grad_totals_all = lax.all_gather(grad_totals, "blk", axis=1, tiled=True).transpose(0, 2, 1)
    numerator = jnp.exp(masked_scores() - row_top[..., None])
    grad_numerator = jnp.einsum(
        "nqhd,nkhd->nhqk", grad_weighted_all, value_rows, preferred_element_type=jnp.float32
    )
    grad_scores = (numerator * (grad_numerator + grad_totals_all[..., None])).astype(jnp.bfloat16)
    grad_keys = (
        jnp.einsum("nhqk,qhd->nkhd", grad_scores, heads_q, preferred_element_type=jnp.float32)
        * score_scale
    )
    grad_keys = grad_keys.astype(jnp.bfloat16).reshape(doc_count * key_count, qk_width)
    grad_values = jnp.einsum(
        "nhqk,nqhd->nkhd",
        numerator.astype(jnp.bfloat16),
        grad_weighted_all,
        preferred_element_type=jnp.float32,
    )
    grad_values = grad_values.astype(jnp.bfloat16).reshape(doc_count * key_count, v_width)
    query_part = jnp.einsum(
        "nhqk,nkhd->qhd", grad_scores, key_rows, preferred_element_type=jnp.float32
    )
    grad_query_part = lax.psum_scatter(
        (query_part * score_scale)
        .reshape(lax.axis_size("blk") * row_count, qk_width)
        .astype(jnp.bfloat16),
        "blk",
        scatter_dimension=0,
        tiled=True,
    )
    grad_w_key = jnp.dot(flat_bytes.T, grad_keys, preferred_element_type=jnp.float32)
    grad_w_value = jnp.dot(flat_bytes.T, grad_values, preferred_element_type=jnp.float32)
    grad_normed_bytes = jnp.dot(grad_keys, w_key.T, preferred_element_type=jnp.float32)
    grad_normed_bytes = grad_normed_bytes + jnp.dot(
        grad_values, w_value.T, preferred_element_type=jnp.float32
    )
    byte_grad, grad_gain_bytes = bytes_back(
        grad_normed_bytes.reshape(doc_count, key_count, in_width)
    )
    direct = jnp.sum(grad_middle.reshape(doc_count, row_count, model_width), axis=0)
    direct_total, query_total = (
        lax.psum(direct.astype(jnp.bfloat16), "doc").astype(jnp.float32),
        lax.psum(grad_query_part, "doc").astype(jnp.float32),
    )
    grad_query_low = query_total.astype(jnp.bfloat16)
    lead_doc = (lax.axis_index("doc") == 0).astype(jnp.float32)
    grad_w_query = (
        jnp.dot(normed_lat_low.T, grad_query_low, preferred_element_type=jnp.float32) * lead_doc
    )
    grad_latent_norm, grad_gain_query = latent_back(
        jnp.dot(grad_query_low, w_query.T, preferred_element_type=jnp.float32)
    )
    latents_grad = direct_total + grad_latent_norm
    grad_gain_query = grad_gain_query * lead_doc
    summed = (
        lax.psum(grad_w_query.astype(jnp.bfloat16), "doc").astype(jnp.float32),
        lax.psum(grad_w_key.astype(jnp.bfloat16), "doc").astype(jnp.float32),
        lax.psum(grad_w_value.astype(jnp.bfloat16), "doc").astype(jnp.float32),
        lax.psum(grad_w_out.astype(jnp.bfloat16), "doc").astype(jnp.float32),
        lax.psum(grad_w_up.astype(jnp.bfloat16), "doc").astype(jnp.float32),
        lax.psum(grad_w_down.astype(jnp.bfloat16), "doc").astype(jnp.float32),
        lax.psum(grad_gain_query.astype(jnp.bfloat16), "doc").astype(jnp.float32),
        lax.psum(grad_gain_bytes.astype(jnp.bfloat16), "doc").astype(jnp.float32),
        lax.psum(grad_gain_mlp.astype(jnp.bfloat16), "doc").astype(jnp.float32),
    )
    sum_query, sum_key, sum_value, sum_out, sum_up, sum_down, sum_gq, sum_gb, sum_gm = summed
    shards = (
        lax.psum_scatter(
            sum_query.astype(jnp.bfloat16), "blk", scatter_dimension=0, tiled=True
        ).astype(jnp.float32),
        lax.psum_scatter(
            sum_key.astype(jnp.bfloat16), "blk", scatter_dimension=0, tiled=True
        ).astype(jnp.float32),
        lax.psum_scatter(
            sum_value.astype(jnp.bfloat16), "blk", scatter_dimension=0, tiled=True
        ).astype(jnp.float32),
        lax.psum_scatter(
            sum_out.astype(jnp.bfloat16), "blk", scatter_dimension=0, tiled=True
        ).astype(jnp.float32),
        lax.psum_scatter(
            sum_up.astype(jnp.bfloat16), "blk", scatter_dimension=0, tiled=True
        ).astype(jnp.float32),
        lax.psum_scatter(
            sum_down.astype(jnp.bfloat16), "blk", scatter_dimension=0, tiled=True
        ).astype(jnp.float32),
        lax.psum_scatter(
            sum_gq.astype(jnp.bfloat16), "blk", scatter_dimension=0, tiled=True
        ).astype(jnp.float32),
        lax.psum_scatter(
            sum_gb.astype(jnp.bfloat16), "blk", scatter_dimension=0, tiled=True
        ).astype(jnp.float32),
        lax.psum_scatter(
            sum_gm.astype(jnp.bfloat16), "blk", scatter_dimension=0, tiled=True
        ).astype(jnp.float32),
    )
    return (
        latents_out.reshape(doc_count, row_count, model_width),
        byte_grad,
        latents_grad,
        shards[6],
        shards[7],
        shards[8],
        shards[0],
        shards[1],
        shards[2],
        shards[3],
        shards[4],
        shards[5],
    )


def solution(mesh):
    in_specs = (
        P("doc", "blk", None),
        P("doc"),
        P("doc", "blk"),
        P("blk", None),
        P(),
        P(),
        P(),
        P(),
        P(),
        P(),
        P(),
        P(),
        P(),
        P("doc", "blk", None),
    )
    out_specs = (
        P("doc", "blk", None),
        P("doc", "blk", None),
        P("blk", None),
        P("blk"),
        P("blk"),
        P("blk"),
        P("blk", None),
        P("blk", None),
        P("blk", None),
        P("blk", None),
        P("blk", None),
        P("blk", None),
    )
    return jax.shard_map(body, mesh=mesh, in_specs=in_specs, out_specs=out_specs, check_vma=False)
```

profile of v0, /device:TPU:0, one launch (start us, length us, event | category | flops | bytes accessed | tf_op | source)
XLA Modules:
  0.0 653.6 jit_solution(11242711443529006404)
XLA Ops:
  10.2 2.5 convert_reduce_fusion
  14.4 16.8 %all_gather.9 = bf16[256,256]{1,0:T(8,128)(2,1)} all-gather(bf16[32,256]{1,0:T(8,128)(2,1)S(1)} %convolution_convert_fusion.7), channel_id=1, replica_groups=mesh['doc'=4,'blk'=8] {'blk'}, dimensions={0}, use_global_device_ids=true | all-gather | bytes 147456 | tf_op jit(solution)/shard_map/all_gather | solution.py:50
  32.8 2.6 fusion.13
  43.0 8.9 %bitcast_reduce_fusion = (bf16[8,8,256]{2,0,1:T(8,128)(2,1)S(1)}, f32[8,8,256,256]{3,2,1,0:T(8,128)}) fusion(pred[8,256]{1,0:T(8,128)(4,1)S(1)} %compare_and_fusion, bf16[256,8,32,1]{0,2,3,1:T(8,128)(2,1)} %bitcast.160, bf16[8,256,8,32]{1,0,3,2:T(8,128)(2,1)S(1)} %bitcast.139), kind=kOutput, calls=%fused_computation.1 | convolution fusion | flops 281001984 | bytes 17991680 | tf_op jit(solution)/shard_map/qhd,nkhd->nhqk/dot_general | solution.py:63
  51.9 29.6 %pmax.7 = bf16[8,8,256]{2,0,1:T(8,128)(2,1)} all-reduce(bf16[8,8,256]{2,0,1:T(8,128)(2,1)S(1)} %get-tuple-element.37), channel_id=1, replica_groups=mesh['doc'=4,'blk'=8] {'blk'}, use_global_device_ids=true, to_apply=%region_5.6 | all-reduce | flops 16384 | bytes 65536 | tf_op jit(solution)/shard_map/pmax | solution.py:69
  82.3 11.4 %fusion.2 = (bf16[8,8,256,256]{2,3,0,1:T(8,128)(2,1)}, bf16[8,8,256]{2,0,1:T(8,128)(2,1)}) fusion(f32[8,8,256,256]{3,2,1,0:T(8,128)} %get-tuple-element.38, f32[8,8,256]{2,0,1:T(8,128)S(1)} %convert_element_type.188, pred[8,256]{1,0:T(8,128)(4,1)S(1)} %compare_and_fusion), kind=kLoop, calls=%fused_computation.7 | loop fusion | flops 20955136 | bytes 25266176 | tf_op jit(solution)/shard_map/convert_element_type | solution.py:74
  98.0 9.1 %convolution_convert_fusion.3 = bf16[2048,1280]{1,0:T(8,128)(2,1)} fusion(bf16[2048,768]{1,0:T(8,128)(2,1)} %bitcast.156, bf16[768,1280]{1,0:T(8,128)(2,1)} %param.23), kind=kOutput, calls=%fused_computation.17 | convolution fusion | flops 4029153280 | bytes 10354688 | tf_op jit(solution)/shard_map/dot_general | solution.py:56
  107.1 8.0 %copy.76 = bf16[2048,1280]{0,1:T(8,128)(2,1)} copy(bf16[2048,1280]{1,0:T(8,128)(2,1)} %convolution_convert_fusion.3) | data formatting | bytes 10485760 | tf_op jit(solution)/shard_map/convert_element_type | solution.py:56
  115.1 7.1 %copy.114 = bf16[160,8,8,256]{3,2,1,0:T(8,128)(2,1)} copy(bf16[160,8,8,256]{3,1,2,0:T(8,128)(2,1)} %bitcast.136) | data formatting | bytes 10485760
  122.2 9.4 %fusion.22 = bf16[8,8,160,256]{3,2,1,0:T(8,128)(2,1)} fusion(bf16[8,8,256,256]{2,3,0,1:T(8,128)(2,1)} %get-tuple-element.35, bf16[8,256,8,160]{1,0,3,2:T(8,128)(2,1)} %bitcast.143), kind=kOutput, calls=%fused_computation.37 | convolution fusion | flops 1344798720 | bytes 18874368 | tf_op jit(solution)/shard_map/nhqk,nkhd->nqhd/dot_general | solution.py:72
  131.5 7.9 %copy.82 = bf16[8,256,1280]{2,1,0:T(8,128)(2,1)} copy(bf16[8,256,1280]{1,2,0:T(8,128)(2,1)} %bitcast.149) | data formatting | bytes 10485760 | tf_op jit(solution)/shard_map/convert_element_type | solution.py:80
  142.2 4.4 fusion.57
  149.8 2.6 div.88
  152.4 3.1 div.89
  155.5 42.2 %reduce-scatter.14.cloned.1.call-done = bf16[8,32,1280]{2,1,0:T(8,128)(2,1)} async-done(((bf16[8,256,1280]{2,1,0:T(8,128)(2,1)}), bf16[8,32,1280]{2,1,0:T(8,128)(2,1)}) %reduce-scatter.14.cloned.1.call-update) | async-done | bytes 655376 | tf_op jit(solution)/shard_map/reduce_scatter | solution.py:79
  197.7 4.6 fusion.56
  210.0 4.2 fusion.41
  220.9 2.4 reshape.205
  223.3 2.5 reshape.206
  225.8 3.2 multiply_reduce_fusion
  229.2 22.2 %all_gather.11 = f32[8,256,8]{2,0,1:T(8,128)S(1)} all-gather(f32[8,32,8]{2,0,1:T(8,128)S(1)} %copy.88), channel_id=1, replica_groups=mesh['doc'=4,'blk'=8] {'blk'}, dimensions={1}, use_global_device_ids=true | all-gather | bytes 73728 | tf_op jit(solution)/shard_map/all_gather | solution.py:122
  251.9 31.9 %all-gather.2.cloned.1.call-done = bf16[8,256,1280]{2,1,0:T(8,128)(2,1)} async-done(((bf16[8,32,1280]{2,1,0:T(8,128)(2,1)}), bf16[8,256,1280]{2,1,0:T(8,128)(2,1)}) %all-gather.2.cloned.1.call-update) | async-done | bytes 5242896 | tf_op jit(solution)/shard_map/all_gather | solution.py:119
  283.7 7.8 %copy.85 = bf16[8,256,1280]{1,2,0:T(8,128)(2,1)} copy(bf16[8,256,1280]{2,1,0:T(8,128)(2,1)} %all-gather.2.cloned.1.call-done) | data formatting | bytes 10485760 | tf_op jit(solution)/shard_map/all_gather | solution.py:119
  291.5 17.5 %multiply_convert_fusion = bf16[8,8,256,256]{2,3,0,1:T(8,128)(2,1)} fusion(f32[8,8,256,256]{3,2,1,0:T(8,128)} %get-tuple-element.38, f32[8,8,256]{2,0,1:T(8,128)S(1)} %copy.89, f32[8,8,256]{2,0,1:T(8,128)S(1)} %convert_element_type.188, pred[8,256]{1,0:T(8,128)(4,1)S(1)} %copy-done.37, bf16[8,256,8,160]{1,0,3,2:T(8,128)(2,1)} %bitcast.144, ...), kind=kOutput, calls=%fused_computation.3 | convolution fusion | flops 1367343104 | bytes 35784704 | tf_op jit(solution)/shard_map/nqhd,nkhd->nhqk/dot_general | solution.py:124
  309.0 4.7 fusion.44
  314.5 4.4 convolution_convert_fusion
  319.1 2.3 div.106
  322.7 2.8 convolution_convert_fusion.2
  326.7 2.7 convolution_convert_fusion.1
  329.6 13.9 %reduce-scatter.30.cloned.1.call-done = bf16[32,256]{1,0:T(8,128)(2,1)} async-done(((bf16[256,256]{1,0:T(8,128)(2,1)}), bf16[32,256]{1,0:T(8,128)(2,1)}) %reduce-scatter.30.cloned.1.call-update) | async-done | bytes 16400
  344.4 16.9 %psum.78 = bf16[32,256]{0,1:T(8,128)(2,1)S(1)} all-reduce(bf16[32,256]{0,1:T(8,128)(2,1)S(1)} %copy.112), channel_id=1, replica_groups=mesh['doc'=4,'blk'=8] {'doc'}, use_global_device_ids=true, to_apply=%region_19.20 | all-reduce | flops 8192 | bytes 32768 | tf_op jit(solution)/shard_map/psum | solution.py:163
  362.6 10.4 %convert_bitcast_fusion = bf16[8,256,8,160]{1,3,2,0:T(8,128)(2,1)} fusion(bf16[8,256,8,160]{1,3,2,0:T(8,128)(2,1)} %bitcast.135, bf16[8,8,256,256]{2,3,0,1:T(8,128)(2,1)} %get-tuple-element.35), kind=kOutput, calls=%fused_computation.31 | convolution fusion | flops 1344798720 | bytes 18874368 | tf_op jit(solution)/shard_map/nhqk,nqhd->nkhd/dot_general | solution.py:133
  373.0 5.8 copy.94
  378.8 2.3 copy.117
  381.1 2.3 copy-done.11
  383.4 5.6 convolution_convert_fusion.4
  392.1 4.8 convolution_add_fusion.1
  396.9 6.1 fusion.34
  404.6 4.5 fusion.58
  416.4 6.3 fusion.14
  422.7 4.9 reduce-scatter.22.cloned.1.call-done
  427.6 42.5 %reduce-scatter.24.cloned.1.call-done = bf16[160,1280]{1,0:T(8,128)(2,1)} async-done(((bf16[1280,1280]{1,0:T(8,128)(2,1)}), bf16[160,1280]{1,0:T(8,128)(2,1)}) %reduce-scatter.24.cloned.1.call-update) | async-done | bytes 409616 | tf_op jit(solution)/shard_map/reduce_scatter | solution.py:200
  470.1 33.1 %reduce-scatter.16.cloned.1.call-done = bf16[160,256]{1,0:T(8,128)(2,1)} async-done(((bf16[1280,256]{1,0:T(8,128)(2,1)}), bf16[160,256]{1,0:T(8,128)(2,1)}) %reduce-scatter.16.cloned.1.call-update) | async-done | bytes 81936 | tf_op jit(solution)/shard_map/reduce_scatter | solution.py:188
  503.2 36.1 %reduce-scatter.20.cloned.1.call-done = bf16[96,1280]{1,0:T(8,128)(2,1)} async-done(((bf16[768,1280]{1,0:T(8,128)(2,1)}), bf16[96,1280]{1,0:T(8,128)(2,1)}) %reduce-scatter.20.cloned.1.call-update) | async-done | bytes 245776 | tf_op jit(solution)/shard_map/reduce_scatter | solution.py:194
  539.3 5.6 broadcast_add_fusion
  546.1 26.6 %all-reduce.3 = (bf16[1280]{0:T(1024)(128)(2,1)S(1)}, bf16[768]{0:T(1024)(128)(2,1)S(1)}, bf16[1280]{0:T(1024)(128)(2,1)S(1)}) all-reduce(bf16[1280]{0:T(1024)(128)(2,1)S(1)} %multiply_convert_fusion.5, bf16[768]{0:T(1024)(128)(2,1)S(1)} %get-tuple-element.12, ...), channel_id=5, replica_groups=mesh['doc'=4,'blk'=8] {'blk'}, use_global_device_ids=true, to_apply=%region_24.25.clone | all-reduce | flops 3328 | bytes 13312
  575.5 19.2 %all-reduce.4 = (bf16[160]{0:T(256)(128)(2,1)S(1)}, bf16[96]{0:T(256)(128)(2,1)S(1)}, bf16[160]{0:T(256)(128)(2,1)S(1)}, bf16[96,256]{1,0:T(8,128)(2,1)S(1)}) all-reduce(bf16[160]{0:T(256)(128)(2,1)S(1)} %dynamic-slice.1, bf16[96]{0:T(256)(128)(2,1)S(1)} %dynamic-slice.3, ...), channel_id=1, replica_groups=mesh['doc'=4,'blk'=8] {'doc'}, use_global_device_ids=true, to_apply=%region_23.24 | all-reduce | flops 24992 | bytes 99968 | tf_op jit(solution)/shard_map/psum | solution.py:182
  597.0 40.9 %all-reduce.8.cloned.1.call-done = (bf16[32,1280]{1,0:T(8,128)(2,1)}, bf16[160,256]{1,0:T(8,128)(2,1)}, bf16[96,1280]{1,0:T(8,128)(2,1)}, bf16[160,1280]{1,0:T(8...) async-done(((bf16[32,1280]{1,0:T(8,128)(2,1)}, bf16[160,256]{1,0:T(8,128)(2,1)}, bf16[96,1280]{1,0:T(8,128)(2,1)}, bf16[160,1280]{1,0:T(8,128)(2,1)}, ...) | async-done | bytes 1638416 | tf_op jit(solution)/shard_map/psum | solution.py:162
  (199 shorter events, 70.9 us)
Async XLA Ops:
  7.2 202.8 %copy-start = (bf16[1280,1280]{1,0:T(8,128)(2,1)S(1)}, bf16[1280,1280]{1,0:T(8,128)(2,1)}, u32[]{:S(2)}) copy-start(bf16[1280,1280]{1,0:T(8,128)(2,1)} %param.25) | copy-start | bytes 9830404
  7.2 139.5 %reduce-scatter.28.cloned.1.call-start = ((), (), s32[]{:S(2)}) async-start(), calls=%async_computation.17 | async-start | bytes 73728
  8.4 5.6 copy-start.38
  10.2 3.9 copy-start.43
  10.2 2.8 copy-start.3
  10.2 3.9 copy-start.9
  10.2 3.9 copy-start.19
  10.2 3.9 copy-start.31
  10.2 22.6 %copy-start.33 = (f32[768]{0:T(1024)S(1)}, f32[768]{0:T(1024)}, u32[]{:S(2)}) copy-start(f32[768]{0:T(1024)} %param.19) | copy-start | bytes 9220
  32.8 4.2 copy-start.29
  39.0 3.8 copy-start.42
  39.0 3.8 copy-start.47
  42.9 9.0 %copy-start.5 = (bf16[32,8,8,256]{3,2,1,0:T(8,128)(2,1)}, bf16[32,8,8,256]{3,2,1,0:T(8,128)(2,1)S(1)}, u32[]{:S(2)}) copy-start(bf16[32,8,8,256]{3,2,1,0:T(8,128)(2,1)S(1)} %copy.115) | copy-start | bytes 3145732
  43.0 39.3 %copy-start.36 = (pred[8,256]{1,0:T(8,128)(4,1)}, pred[8,256]{1,0:T(8,128)(4,1)S(1)}, u32[]{:S(2)}) copy-start(pred[8,256]{1,0:T(8,128)(4,1)S(1)} %compare_and_fusion) | copy-start | bytes 6148
  97.6 100.0 %reduce-scatter.14.cloned.1.call-start = ((), (), s32[]{:S(2)}) async-start(), calls=%async_computation.9 | async-start | bytes 5898240 | tf_op jit(solution)/shard_map/reduce_scatter | solution.py:79
  139.4 144.3 %all-gather.2.cloned.1.call-start = ((), (), s32[]{:S(2)}) async-start(), calls=%async_computation.10 | async-start | bytes 5898240 | tf_op jit(solution)/shard_map/all_gather | solution.py:119
  210.0 4.3 copy-start.13
  210.0 4.2 copy-start.7
  210.0 4.2 copy-start.35
  210.0 4.2 copy-start.40
  219.7 3.6 copy-start.21
  220.8 122.7 %reduce-scatter.30.cloned.1.call-start = ((), (), s32[]{:S(2)}) async-start(), calls=%async_computation.18 | async-start | bytes 147456
  251.8 39.7 %copy-start.37 = (pred[8,256]{1,0:T(8,128)(4,1)S(1)}, pred[8,256]{1,0:T(8,128)(4,1)}, u32[]{:S(2)}) copy-start(pred[8,256]{1,0:T(8,128)(4,1)} %copy-done.36) | copy-start | bytes 6148
  291.5 17.5 %copy-start.6 = (bf16[32,8,8,256]{3,2,1,0:T(8,128)(2,1)S(1)}, bf16[32,8,8,256]{3,2,1,0:T(8,128)(2,1)}, u32[]{:S(2)}) copy-start(bf16[32,8,8,256]{3,2,1,0:T(8,128)(2,1)} %copy-done.5) | copy-start | bytes 3145732
  309.0 5.5 copy-start.25
  314.5 108.3 %reduce-scatter.26.cloned.1.call-start = ((), (), s32[]{:S(2)}) async-start(), calls=%async_computation.16 | async-start | bytes 3686400 | tf_op jit(solution)/shard_map/reduce_scatter | solution.py:203
  319.0 108.6 %reduce-scatter.22.cloned.1.call-start = ((), (), s32[]{:S(2)}) async-start(), calls=%async_computation.14 | async-start | bytes 3686400 | tf_op jit(solution)/shard_map/reduce_scatter | solution.py:197
  325.5 144.6 %reduce-scatter.24.cloned.1.call-start = ((), (), s32[]{:S(2)}) async-start(), calls=%async_computation.15 | async-start | bytes 3686400 | tf_op jit(solution)/shard_map/reduce_scatter | solution.py:200
  329.5 31.7 %copy-start.39 = (f32[32]{0:T(128)S(1)}, f32[32]{0:T(128)}, u32[]{:S(2)}) copy-start(f32[32]{0:T(128)} %copy-done.38) | copy-start | bytes 388
  329.5 31.8 %copy-start.44 = (f32[32]{0:T(128)S(1)}, f32[32]{0:T(128)}, u32[]{:S(2)}) copy-start(f32[32]{0:T(128)} %copy-done.43) | copy-start | bytes 388
  329.5 173.7 %reduce-scatter.16.cloned.1.call-start = ((), (), s32[]{:S(2)}) async-start(), calls=%async_computation.11 | async-start | bytes 737280 | tf_op jit(solution)/shard_map/reduce_scatter | solution.py:188
  362.6 176.7 %reduce-scatter.20.cloned.1.call-start = ((), (), s32[]{:S(2)}) async-start(), calls=%async_computation.13 | async-start | bytes 2211840 | tf_op jit(solution)/shard_map/reduce_scatter | solution.py:194
  378.7 4.7 copy-start.17
  383.4 6.1 copy-start.49
  389.0 3.1 copy-start.8
  389.1 186.4 %reduce-scatter.18.cloned.1.call-start = ((), (), s32[]{:S(2)}) async-start(), calls=%async_computation.12 | async-start | bytes 442368 | tf_op jit(solution)/shard_map/reduce_scatter | solution.py:191
  392.1 4.8 copy-start.22
  392.1 11.9 %slice-start = ((s8[5242880]{0:T(1024)(128)(4,1)}), s8[4194304]{0:T(1024)(128)(4,1)S(1)}, s32[]{:S(2)}) async-start(s8[5242880]{0:T(1024)(128)(4,1)} %bitcast.146), calls=%async_computation.20 | async-start | bytes 8388608
  396.9 7.1 %slice-start.1 = ((s8[5242880]{0:T(1024)(128)(4,1)}), s8[1048576]{0:T(1024)(128)(4,1)S(1)}, s32[]{:S(2)}) async-start(s8[5242880]{0:T(1024)(128)(4,1)} %bitcast.146), calls=%async_computation.21 | async-start | bytes 2097152
  404.6 4.5 copy-start.30
  411.1 3.3 copy-start.18
  416.2 221.7 %all-reduce.8.cloned.1.call-start = ((), (), s32[]{:S(2)}) async-start(), calls=%async_computation.19 | async-start | bytes 3276800 | tf_op jit(solution)/shard_map/psum | solution.py:162
  539.3 5.7 copy-start.20
  539.3 5.7 copy-start.45
  545.0 101.9 %copy-start.1 = (bf16[1280,1280]{1,0:T(8,128)(2,1)S(1)}, bf16[1280,1280]{1,0:T(8,128)(2,1)}, u32[]{:S(2)}) copy-start(bf16[1280,1280]{1,0:T(8,128)(2,1)} %param.25) | copy-start | bytes 9830404
  575.4 70.7 %copy-start.23 = (f32[32,1280]{1,0:T(8,128)S(1)}, f32[32,1280]{1,0:T(8,128)}, u32[]{:S(2)}) copy-start(f32[32,1280]{1,0:T(8,128)} %get-tuple-element.32) | copy-start | bytes 491524
  637.9 7.3 %copy-start.28 = (bf16[160,1280]{1,0:T(8,128)(2,1)S(1)}, bf16[160,1280]{1,0:T(8,128)(2,1)}, u32[]{:S(2)}) copy-start(bf16[160,1280]{1,0:T(8,128)(2,1)} %get-tuple-element.30) | copy-start | bytes 1228804
  638.0 8.2 %copy-start.32 = (bf16[32,1280]{1,0:T(8,128)(2,1)S(1)}, bf16[32,1280]{1,0:T(8,128)(2,1)}, u32[]{:S(2)}) copy-start(bf16[32,1280]{1,0:T(8,128)(2,1)} %get-tuple-element.25) | copy-start | bytes 245764
  (15 other events, 24.7 us)
Sparse Core Ops, SparseCore 0:
  97.8 28.2 reduce-scatter.27
  139.5 58.0 reduce-scatter.13
  220.9 62.7 all-gather.1
  314.6 28.8 reduce-scatter.29
  345.7 39.4 reduce-scatter.25
  387.5 40.1 reduce-scatter.21
  430.0 40.1 reduce-scatter.23
  473.1 30.1 reduce-scatter.15
  505.7 33.5 reduce-scatter.19
  542.0 28.9 reduce-scatter.17
  575.7 62.2 all-reduce.7
where the time goes:
time: 662 us; the launch traced here: 654 us
  waiting for transfers between devices  246 us (37%)
  blocking collectives  131 us (20%)
  matrix products  114 us (17%)
  local copies, waits for them, and re-layouts  83.4 us (13%)
  other arithmetic  60.6 us (9%)
  between operations  16 us (2%)
    reduce_scatter x1, waiting for transfers between devices, body(): lax.psum_scatter(sum_up.astype(jnp.bfloat16), 'blk', scatter_dimension=0,...  42.5 us
    reduce_scatter x1, waiting for transfers between devices, body(): lax.psum_scatter(part_weighted.astype(jnp.bfloat16), 'blk', scatter_dimen...  42.2 us
    psum x1, waiting for transfers between devices, body(): lax.psum(direct.astype(jnp.bfloat16), 'doc').astype(jnp.float32)  40.9 us
    reduce_scatter x1, waiting for transfers between devices, body(): lax.psum_scatter(sum_value.astype(jnp.bfloat16), 'blk', scatter_dimension...  36.1 us
    reduce_scatter x1, waiting for transfers between devices, body(): lax.psum_scatter(sum_query.astype(jnp.bfloat16), 'blk', scatter_dimension...  33.1 us
    all_gather x1, waiting for transfers between devices, body(): lax.all_gather(grad_weighted, 'blk', axis=1, tiled=True)  31.9 us
    unnamed x117, local copies, waits for them, and re-layouts  30.8 us
    pmax x1, blocking collectives, body(): lax.pmax(jnp.max(masked, axis=-1).astype(jnp.bfloat16), 'blk')  29.6 us
  transfers between devices with their start and end apart: 11, of which 8 were waited for; matrix products, arithmetic and copies ran while one was open for 22% of the time, Pallas kernels for 0%

commit v1 on v0

--- a/solution.py
+++ b/solution.py
@@ -1,17 +1,324 @@
+import functools
+import math
+
 import jax
 import jax.numpy as jnp
 from jax import lax
+from jax.experimental import pallas as pl
+from jax.experimental.pallas import tpu as pltpu
 from jax.sharding import PartitionSpec as P
 
 LAT = 256
 HEADS = 8
 QK_HEAD = 32
 V_HEAD = 160
-
+DQK = HEADS * QK_HEAD
+DV = HEADS * V_HEAD
+MESH = pl.DeviceIdType.MESH
+F32 = jnp.float32
+BF16 = jnp.bfloat16
 
 epsilon = 1e-05
 masked_score = -1e30
-
+LOG2E = math.log2(math.e)
+SCORE2 = QK_HEAD ** (-0.5) * LOG2E
+SCORE_SCALE = QK_HEAD ** (-0.5)
+
+
+def dot_nn(a, b):
+    return jnp.dot(a, b, preferred_element_type=F32)
+
+
+def dot_nt(a, b):
+    return lax.dot_general(a, b, (((1,), (1,)), ((), ())), preferred_element_type=F32)
+
+
+def norm_parts(v):
+    centered = v - jnp.mean(v, axis=-1, keepdims=True)
+    spread = jnp.mean(centered * centered, axis=-1, keepdims=True)
+    inv = lax.rsqrt(spread + epsilon)
+    return centered * inv, inv
+
+
+def window(h):
+    return V_HEAD * h // 128 * 128
+
+
+def value_mask(h, rows):
+    lane = lax.broadcasted_iota(jnp.int32, (rows, 256), 1) + window(h)
+    keep = (lane >= V_HEAD * h) & (lane < V_HEAD * (h + 1))
+    return jnp.where(keep, 1.0, 0.0).astype(BF16)
+
+
+def query_mask(h, rows):
+    lane = lax.broadcasted_iota(jnp.int32, (rows, DQK), 1)
+    keep = (lane >= QK_HEAD * h) & (lane < QK_HEAD * (h + 1))
+    return jnp.where(keep, 1.0, 0.0).astype(BF16)
+
+
+def row_to_lanes(row):
+    return jnp.transpose(jnp.broadcast_to(row, (128, row.shape[1])))
+
+
+def wide(col, n):
+    return jnp.concatenate([col] * (n // 128), axis=1) if n > 128 else col
+
+
+def remote(src, dst, send, recv, doc, blk):
+    return pltpu.make_async_remote_copy(
+        src_ref=src, dst_ref=dst, send_sem=send, recv_sem=recv,
+        device_id=(doc, blk), device_id_type=MESH,
+    )
+
+
+def forward_kernel(
+    nb,
+    x_ref, bias_ref, lat_ref, gq_ref, gb_ref, wq_ref, wk_ref, wv_ref,
+    att_ref, lse_ref, k_ref, v_ref, nl_ref, qall_ref,
+    normed, qm, lloc, lmate, lz, acc, part, mate_in, rin, lin,
+    q_s, q_r, l_s, l_r, mate_s, mate_r, rs_s, rs_r, ls_s, ls_r,
+):
+    D, kc, din = x_ref.shape
+    rq = lat_ref.shape[0]
+    pos = nb // 2
+    doc, blk = lax.axis_index("doc"), lax.axis_index("blk")
+    p, c = blk // 2, blk % 2
+    mate = 2 * p + 1 - c
+    barrier = pltpu.get_barrier_semaphore()
+    for i in range(1, nb):
+        pl.semaphore_signal(
+            barrier, inc=1, device_id=(doc, lax.rem(blk + i, nb)), device_id_type=MESH
+        )
+
+    xhat, _ = norm_parts(lat_ref[...])
+    nl = (xhat * gq_ref[...]).astype(BF16)
+    nl_ref[...] = nl
+    own = pl.ds(pl.multiple_of(blk * rq, rq), rq)
+    qall_ref[own, :] = dot_nn(nl, wq_ref[...]).astype(BF16)
+    pl.semaphore_wait(barrier, nb - 1)
+
+    def q_copy(i, slot):
+        return remote(
+            qall_ref.at[own, :], qall_ref.at[slot, :], q_s.at[i - 1], q_r.at[i - 1],
+            doc, lax.rem(blk + i, nb),
+        )
+
+    for i in range(1, nb):
+        q_copy(i, own).start()
+
+    @pl.loop(0, D)
+    def _(n):
+        xh, _ = norm_parts(x_ref[n].astype(F32))
+        normed[n] = (xh * gb_ref[...]).astype(BF16)
+        k_ref[n] = dot_nn(normed[n], wk_ref[...]).astype(BF16)
+
+    for i in range(1, nb):
+        src = lax.rem(blk + nb - i, nb)
+        q_copy(i, pl.ds(pl.multiple_of(src * rq, rq), rq)).wait_recv()
+    for h in range(HEADS):
+        qm[h] = qall_ref[...] * query_mask(h, LAT)
+
+    @pl.loop(0, D)
+    def _(n):
+        bias = wide(row_to_lanes(bias_ref[pl.ds(n, 1), :]), LAT)
+        kn = k_ref[n]
+        rows = []
+        for h in range(HEADS):
+            s = dot_nt(kn, qm[h]) * SCORE2 + bias
+            top = jnp.max(s, axis=0, keepdims=True)
+            tot = jnp.sum(jnp.exp2(s - top), axis=0, keepdims=True)
+            rows.append(top + jnp.log(tot) * LOG2E)
+        lloc[n] = jnp.concatenate(rows, axis=0)
+
+    half = D // 2
+    mine, other = pl.ds(c * half, half), pl.ds((1 - c) * half, half)
+
+    def merge(a, b):
+        top = jnp.maximum(a, b)
+        return top + jnp.log(jnp.exp2(a - top) + jnp.exp2(b - top)) * LOG2E
+
+    first = remote(lloc.at[other], lmate, l_s.at[0], l_r.at[0], doc, mate)
+    first.start()
+
+    def values(lo, hi):
+        @pl.loop(lo, hi)
+        def _(n):
+            v_ref[n] = dot_nn(normed[n], wv_ref[...]).astype(BF16)
+
+    values(0, D // 4)
+    first.wait_recv()
+    lz[p] = merge(lloc[mine], lmate[...])
+
+    def z_copy(i, slot):
+        return remote(
+            lz.at[p], lz.at[slot], l_s.at[i], l_r.at[i],
+            doc, 2 * lax.rem(p + i, pos) + c,
+        )
+
+    for i in range(1, pos):
+        z_copy(i, p).start()
+    values(D // 4, 3 * D // 4)
+    for i in range(1, pos):
+        z_copy(i, lax.rem(p + pos - i, pos)).wait_recv()
+    total = lz[0]
+    for i in range(1, pos):
+        total = merge(total, lz[i])
+    lse_ref[mine] = total
+    last = remote(lse_ref.at[mine], lse_ref.at[mine], l_s.at[pos], l_r.at[pos], doc, mate)
+    last.start()
+    values(3 * D // 4, D)
+    remote(
+        lse_ref.at[other], lse_ref.at[other], l_s.at[pos], l_r.at[pos], doc, mate
+    ).wait_recv()
+
+    def mate_copy(n):
+        return remote(
+            part.at[n, 1 - c], mate_in.at[n], mate_s.at[n], mate_r.at[n], doc, mate
+        )
+
+    def right_copy(n, j, src):
+        return remote(
+            src, rin.at[n, j], rs_s.at[n, j], rs_r.at[n, j],
+            doc, 2 * jnp.minimum(p + 1, pos - 1) + c,
+        )
+
+    def left_copy(n, j, src):
+        return remote(
+            src, lin.at[n, j], ls_s.at[n, j], ls_r.at[n, j],
+            doc, 2 * jnp.maximum(p - 1, 0) + c,
+        )
+
+    def chip_sum(n):
+        mate_copy(n).wait_recv()
+        for j in range(pos):
+            both = part[n, c, j].astype(F32) + mate_in[n, j].astype(F32)
+            part[n, c, j] = both.astype(BF16)
+
+            @pl.when((p == 0) & (j > 0))
+            def _():
+                right_copy(n, j, part.at[n, c, j]).start()
+
+            @pl.when((p == pos - 1) & (j < pos - 1))
+            def _():
+                left_copy(n, j, part.at[n, c, j]).start()
+
+    @pl.loop(0, D)
+    def _(n):
+        logs = lse_ref[n]
+        logs_t = jnp.transpose(jnp.concatenate([logs] * (128 // HEADS), axis=0))
+        bias = bias_ref[pl.ds(n, 1), :]
+        kn = k_ref[n]
+        acc[...] = jnp.zeros_like(acc)
+        for h in range(HEADS):
+            s = dot_nt(qm[h], kn) * SCORE2 + bias
+            prob = jnp.exp2(s - logs_t[:, h : h + 1]).astype(BF16)
+            cols = slice(window(h), window(h) + 256)
+            acc[:, cols] += dot_nn(prob, v_ref[n, :, cols] * value_mask(h, kc))
+        for j in range(nb):
+            part[n, j % 2, j // 2] = acc[rq * j : rq * (j + 1), :].astype(BF16)
+        mate_copy(n).start()
+
+        @pl.when(n > 0)
+        def _():
+            chip_sum(n - 1)
+
+    chip_sum(D - 1)
+
+    @pl.loop(0, D)
+    def _(n):
+        for j in range(1, pos):
+            @pl.when((p > 0) & (j >= p))
+            def _():
+                right_copy(n, j, part.at[n, c, j]).wait_recv()
+
+            @pl.when((p > 0) & (j > p))
+            def _():
+                both = rin[n, j].astype(F32) + part[n, c, j].astype(F32)
+                part[n, c, j] = both.astype(BF16)
+                right_copy(n, j, part.at[n, c, j]).start()
+
+        for j in range(pos - 2, -1, -1):
+            @pl.when((p < pos - 1) & (j <= p))
+            def _():
+                left_copy(n, j, part.at[n, c, j]).wait_recv()
+
+            @pl.when((p < pos - 1) & (j < p))
+            def _():
+                both = lin[n, j].astype(F32) + part[n, c, j].astype(F32)
+                part[n, c, j] = both.astype(BF16)
+                left_copy(n, j, part.at[n, c, j]).start()
+
+        att_ref[n] = part[n, c, p].astype(F32)
+
+        @pl.when(p > 0)
+        def _():
+            att_ref[n] += rin[n, p].astype(F32)
+
+        @pl.when(p < pos - 1)
+        def _():
+            att_ref[n] += lin[n, p].astype(F32)
+
+    for i in range(1, nb):
+        q_copy(i, own).wait_send()
+    first.wait_send()
+    for i in range(1, pos):
+        z_copy(i, p).wait_send()
+    last.wait_send()
+
+    @pl.loop(0, D)
+    def _(n):
+        mate_copy(n).wait_send()
+        for j in range(pos):
+            @pl.when((j > p) & (p < pos - 1))
+            def _():
+                right_copy(n, j, part.at[n, c, j]).wait_send()
+
+            @pl.when((j < p) & (p > 0))
+            def _():
+                left_copy(n, j, part.at[n, c, j]).wait_send()
+
+
+def forward(nb, byte_embed, bias, latents, gain_query, gain_bytes, w_query, w_key, w_value):
+    D, kc, din = byte_embed.shape
+    rq, dl = latents.shape
+    pos = nb // 2
+    vmem = pl.BlockSpec(memory_space=pltpu.VMEM)
+    dma = pltpu.SemaphoreType.DMA
+    return pl.pallas_call(
+        functools.partial(forward_kernel, nb),
+        out_shape=(
+            jax.ShapeDtypeStruct((D, rq, DV), F32),
+            jax.ShapeDtypeStruct((D, HEADS, LAT), F32),
+            jax.ShapeDtypeStruct((D, kc, DQK), BF16),
+            jax.ShapeDtypeStruct((D, kc, DV), BF16),
+            jax.ShapeDtypeStruct((rq, dl), BF16),
+            jax.ShapeDtypeStruct((LAT, DQK), BF16),
+        ),
+        in_specs=[vmem] * 8,
+        out_specs=(vmem,) * 6,
+        scratch_shapes=[
+            pltpu.VMEM((D, kc, din), BF16),
+            pltpu.VMEM((HEADS, LAT, DQK), BF16),
+            pltpu.VMEM((D, HEADS, LAT), F32),
+            pltpu.VMEM((D // 2, HEADS, LAT), F32),
+            pltpu.VMEM((pos, D // 2, HEADS, LAT), F32),
+            pltpu.VMEM((LAT, DV), F32),
+            pltpu.VMEM((D, 2, pos, rq, DV), BF16),
+            pltpu.VMEM((D, pos, rq, DV), BF16),
+            pltpu.VMEM((D, pos, rq, DV), BF16),
+            pltpu.VMEM((D, pos, rq, DV), BF16),
+            dma((nb - 1,)), dma((nb - 1,)), dma((pos + 1,)), dma((pos + 1,)),
+            dma((D,)), dma((D,)),
+            dma((D, pos)), dma((D, pos)), dma((D, pos)), dma((D, pos)),
+        ],
+        compiler_params=pltpu.CompilerParams(
+            collective_id=0, has_side_effects=True, vmem_limit_bytes=56 * 2**20
+        ),
+        name="forward",
+    )(
+        byte_embed, bias, latents, gain_query.reshape(1, -1), gain_bytes.reshape(1, -1),
+        w_query, w_key, w_value,
+    )
 
 def layer_norm(matrix, gain_vec):
     centered = matrix - jnp.mean(matrix, axis=-1, keepdims=True)
@@ -42,22 +349,16 @@
     score_scale = QK_HEAD ** (-0.5)
     positions = lax.axis_index("blk") * key_count + jnp.arange(key_count, dtype=jnp.int32)
     usable = (positions[None, :] < doc_lengths[:, None]) & (key_mask == 1)
+    bias = jnp.where(usable, 0.0, masked_score).astype(jnp.float32)
+    nb = lax.axis_size("blk")
+    att, lse, key_rows, value_rows, _, query_all = forward(nb, byte_embed, bias, latents, gain_query, gain_bytes, w_query, w_key, w_value)
     normed_lat, latent_back = jax.vjp(layer_norm, latents, gain_query)
     normed_lat_low = normed_lat.astype(jnp.bfloat16)
-    query_own = jnp.dot(normed_lat_low, w_query, preferred_element_type=jnp.float32).astype(
-        jnp.bfloat16
-    )
-    query_all = lax.all_gather(query_own, "blk", axis=0, tiled=True)
     heads_q = query_all.reshape(LAT, HEADS, QK_HEAD)
     normed_bytes, bytes_back = jax.vjp(layer_norm, byte_embed.astype(jnp.float32), gain_bytes)
     flat_bytes = normed_bytes.astype(jnp.bfloat16).reshape(doc_count * key_count, in_width)
-    key_rows = jnp.dot(flat_bytes, w_key, preferred_element_type=jnp.float32).astype(jnp.bfloat16)
     key_rows = key_rows.reshape(doc_count, key_count, HEADS, QK_HEAD)
-    value_rows = jnp.dot(flat_bytes, w_value, preferred_element_type=jnp.float32).astype(
-        jnp.bfloat16
-    )
     value_rows = value_rows.reshape(doc_count, key_count, HEADS, V_HEAD)
-
     def masked_scores():
         scores = (
             jnp.einsum("qhd,nkhd->nhqk", heads_q, key_rows, preferred_element_type=jnp.float32)
@@ -66,24 +367,7 @@
         return jnp.where(usable[:, None, None, :], scores, masked_score)
 
     masked = masked_scores()
-    row_top = lax.pmax(jnp.max(masked, axis=-1).astype(jnp.bfloat16), "blk").astype(jnp.float32)
-    numerator = jnp.exp(masked - row_top[..., None])
-    part_totals = jnp.sum(numerator, axis=-1).transpose(0, 2, 1)
-    part_weighted = jnp.einsum(
-        "nhqk,nkhd->nqhd",
-        numerator.astype(jnp.bfloat16),
-        value_rows,
-        preferred_element_type=jnp.float32,
-    ).reshape(doc_count, LAT, v_width)
-    weighted, totals = (
-        lax.psum_scatter(
-            part_weighted.astype(jnp.bfloat16), "blk", scatter_dimension=1, tiled=True
-        ).astype(jnp.float32),
-        lax.psum_scatter(
-            part_totals.astype(jnp.bfloat16), "blk", scatter_dimension=1, tiled=True
-        ).astype(jnp.float32),
-    )
-    attended_heads = weighted.reshape(doc_count, row_count, HEADS, V_HEAD) / totals[..., None]
+    attended_heads = att.reshape(doc_count, row_count, HEADS, V_HEAD)
     attended = attended_heads.reshape(doc_count * row_count, v_width)
     attended_low = attended.astype(jnp.bfloat16)
     branch = jnp.dot(attended_low, w_out, preferred_element_type=jnp.float32)
@@ -111,16 +395,16 @@
     grad_attended = jnp.dot(grad_branch, w_out.T, preferred_element_type=jnp.float32)
     grad_attended = grad_attended.reshape(doc_count, row_count, HEADS, V_HEAD)
     grad_weighted = (
-        (grad_attended / totals[..., None])
+        grad_attended
         .astype(jnp.bfloat16)
         .reshape(doc_count, row_count, v_width)
     )
-    grad_totals = -jnp.sum(grad_attended * attended_heads, axis=-1) / totals
+    grad_totals = -jnp.sum(grad_attended * attended_heads, axis=-1)
     grad_weighted_all = lax.all_gather(grad_weighted, "blk", axis=1, tiled=True).reshape(
         doc_count, LAT, HEADS, V_HEAD
     )
     grad_totals_all = lax.all_gather(grad_totals, "blk", axis=1, tiled=True).transpose(0, 2, 1)
-    numerator = jnp.exp(masked_scores() - row_top[..., None])
+    numerator = jnp.exp2(masked_scores()*LOG2E - lse[..., None])
     grad_numerator = jnp.einsum(
         "nqhd,nkhd->nhqk", grad_weighted_all, value_rows, preferred_element_type=jnp.float32
     )

time: 662 us -> 591 us (0.89)
  Pallas kernels: 0 us -> 122 us
  waiting for transfers between devices: 246 us -> 174 us
  blocking collectives: 131 us -> 84 us
  local copies, waits for them, and re-layouts: 83.4 us -> 44.8 us
  other arithmetic: 60.6 us -> 38 us
  matrix products: 114 us -> 94 us
  starting transfers between devices: 2.06 us -> 9.63 us
    pallas_call x0 -> x1, Pallas kernels: none -> 122 us  [forward(): pl.pallas_call(functools.partial(forward_kernel, nb), out_shape=(jax.Shap...]
    reduce_scatter x1 -> x0, waiting for transfers between devices: 42.2 us -> none  [body(): lax.psum_scatter(part_weighted.astype(jnp.bfloat16), 'blk', scatter_dimen...]
    reduce_scatter x1, waiting for transfers between devices: 4.9 us -> 42.4 us  [body(): lax.psum_scatter(sum_out.astype(jnp.bfloat16), 'blk', scatter_dimension=0...]
    reduce_scatter x1, waiting for transfers between devices: 42.5 us -> 12.2 us  [body(): lax.psum_scatter(sum_up.astype(jnp.bfloat16), 'blk', scatter_dimension=0,...]
    pmax x1 -> x0, blocking collectives: 29.6 us -> none  [body(): lax.pmax(jnp.max(masked, axis=-1).astype(jnp.bfloat16), 'blk')]
    all_gather x1, waiting for transfers between devices: 31.9 us -> 9.57 us  [body(): lax.all_gather(grad_weighted, 'blk', axis=1, tiled=True)]
    dot_general x4 -> x0, matrix products: 20.7 us -> none  [the longest x1 9.35 us: body(): jnp.einsum('nhqk,nkhd->nqhd', numerator.astype(jnp.bfloat16), value_rows,...]
    unnamed x117 -> x82, local copies, waits for them, and re-layouts: 30.8 us -> 11.9 us
  transfers between devices with their start and end apart: 11 -> 9, of which waited for: 8 -> 6; matrix products, arithmetic and copies ran while one was open for 22% -> 19% of each run, Pallas kernels for 0% -> 0%
where the time goes in v1:
time: 591 us; the launch traced here: 582 us
  waiting for transfers between devices  174 us (29%)
  Pallas kernels  122 us (21%)
  matrix products  94 us (16%)
  blocking collectives  84 us (14%)
  local copies, waits for them, and re-layouts  44.8 us (8%)
  other arithmetic  38 us (6%)
  between operations  16.2 us (3%)
  starting transfers between devices  9.63 us (2%)
    pallas_call x1, Pallas kernels, forward(): pl.pallas_call(functools.partial(forward_kernel, nb), out_shape=(jax.Shap...  122 us
    reduce_scatter x1, waiting for transfers between devices, body(): lax.psum_scatter(sum_out.astype(jnp.bfloat16), 'blk', scatter_dimension=0...  42.4 us
    psum x1, waiting for transfers between devices, body(): lax.psum(direct.astype(jnp.bfloat16), 'doc').astype(jnp.float32)  40.6 us
    reduce_scatter x1, waiting for transfers between devices, body(): lax.psum_scatter(sum_value.astype(jnp.bfloat16), 'blk', scatter_dimension...  36.1 us
    reduce_scatter x1, waiting for transfers between devices, body(): lax.psum_scatter(sum_query.astype(jnp.bfloat16), 'blk', scatter_dimension...  32.9 us
    unnamed x1, blocking collectives  26.5 us
    all_gather x1, blocking collectives, body(): lax.all_gather(grad_totals, 'blk', axis=1, tiled=True).transpose(0, 2, 1)  21.8 us
    psum x1, blocking collectives, body(): lax.psum(grad_gain_query.astype(jnp.bfloat16), 'doc').astype(jnp.float32)  18.7 us
  transfers between devices with their start and end apart: 9, of which 6 were waited for; matrix products, arithmetic and copies ran while one was open for 19% of the time, Pallas kernels for 0%

profile of v1, /device:TPU:0, one launch (start us, length us, event | category | flops | bytes accessed | tf_op | source)
XLA Modules:
  0.0 582.2 jit_solution(6758706641200011175)
XLA Ops:
  7.3 1.4 reshape.193.gb_ref
  10.0 2.2 bitcast_convert_fusion
  13.6 121.6 %forward.1 = (f32[8,32,1280]{2,1,0:T(8,128)}, f32[8,8,256]{2,1,0:T(8,128)}, bf16[8,256,256]{2,1,0:T(8,128)(2,1)}, bf16[8,256,1280]{2,1,0:T(8,128)(2,1)}, bf16[32...) custom-call(bf16[8,256,768]{2,1,0:T(8,128)(2,1)} %x_ref.1, f32[8,256]{1,0:T(8,128)} %get-tuple-element.47.bias_ref, ...), custom_call_target="tpu_custom_call" | custom-call | tf_op jit(solution)/shard_map/forward/pallas_call | solution.py:287
  136.6 2.1 fusion.57
  138.8 1.6 multiply_reduce_fusion.3
  140.5 3.3 fusion.59
  144.0 2.6 fusion.35
  150.3 2.4 fusion.58
  153.0 2.5 reshape.202
  155.6 2.3 copy.65
  158.0 2.5 reshape.201
  160.4 2.6 multiply_reduce_fusion
  163.2 21.8 %all_gather.7 = f32[8,256,8]{2,0,1:T(8,128)S(1)} all-gather(f32[8,32,8]{2,0,1:T(8,128)S(1)} %copy.71), channel_id=1, replica_groups=mesh['doc'=4,'blk'=8] {'blk'}, dimensions={1}, use_global_device_ids=true | all-gather | bytes 73728 | tf_op jit(solution)/shard_map/all_gather | solution.py:406
  185.4 7.9 %copy.69 = bf16[8,256,1280]{1,2,0:T(8,128)(2,1)} copy(bf16[8,256,1280]{2,1,0:T(8,128)(2,1)} %get-tuple-element.21) | data formatting | bytes 10485760 | tf_op jit(solution)/shard_map/forward/pallas_call | solution.py:287
  193.4 11.6 %fusion.2 = (bf16[8,8,256,256]{2,3,0,1:T(8,128)(2,1)}, f32[8,8,256,256]{3,2,1,0:T(8,128)}) fusion(f32[8,8,256]{2,0,1:T(8,128)S(1)} %copy.67, pred[8,256]{1,0:T(8,128)(4,1)S(1)} %get-tuple-element.48, bf16[256,8,32,1]{0,2,3,1:T(8,128)(2,1)S(1)} %bitcast.122, bf16[8,256,8,32]{1,3,2,0:T(8,128)(2,1)S(1)} %bitcast.120), kind=kOutput, calls=%fused_computation.4 | convolution fusion | flops 293601280 | bytes 26413056 | tf_op jit(solution)/shard_map/qhd,nkhd->nhqk/dot_general | solution.py:364
  205.0 9.6 %all-gather.2.cloned.1.call-done = bf16[8,256,1280]{2,1,0:T(8,128)(2,1)} async-done(((bf16[8,32,1280]{2,1,0:T(8,128)(2,1)}), bf16[8,256,1280]{2,1,0:T(8,128)(2,1)}) %all-gather.2.cloned.1.call-update) | async-done | bytes 5242896 | tf_op jit(solution)/shard_map/all_gather | solution.py:403
  214.5 7.8 %copy.68 = bf16[8,256,1280]{1,2,0:T(8,128)(2,1)} copy(bf16[8,256,1280]{2,1,0:T(8,128)(2,1)} %all-gather.2.cloned.1.call-done) | data formatting | bytes 10485760 | tf_op jit(solution)/shard_map/all_gather | solution.py:403
  222.3 14.4 %multiply_convert_fusion = bf16[8,8,256,256]{2,3,0,1:T(8,128)(2,1)} fusion(f32[8,8,256,256]{3,2,1,0:T(8,128)} %get-tuple-element.61, f32[8,8,256]{2,0,1:T(8,128)S(1)} %copy.72, f32[8,8,256]{2,0,1:T(8,128)S(1)} %copy.67, pred[8,256]{1,0:T(8,128)(4,1)S(1)} %get-tuple-element.48, bf16[8,256,8,160]{1,3,2,0:T(8,128)(2,1)} %bitcast.111, ...), kind=kOutput, calls=%fused_computation.3 | convolution fusion | flops 1375731712 | bytes 35784704 | tf_op jit(solution)/shard_map/nqhd,nkhd->nhqk/dot_general | solution.py:408
  236.7 4.9 fusion.42
  242.4 4.5 convolution_convert_fusion
  248.2 2.7 convolution_convert_fusion.1
  252.0 2.7 convolution_convert_fusion.2
  254.8 8.8 %reduce-scatter.10.cloned.1.call-start = ((), (), s32[]{:S(2)}) async-start(), calls=%async_computation.8 | async-start | bytes 737280 | tf_op jit(solution)/shard_map/reduce_scatter | solution.py:472
  264.4 6.0 %fusion.28 = bf16[8,256,8,32]{1,3,0,2:T(8,128)(2,1)S(1)} fusion(bf16[256,8,32,1]{0,2,3,1:T(8,128)(2,1)S(1)} %bitcast.123, bf16[8,8,256,256]{2,3,0,1:T(8,128)(2,1)} %multiply_convert_fusion), kind=kOutput, calls=%fused_computation.43 | convolution fusion | flops 269484032 | bytes 9568256 | tf_op jit(solution)/shard_map/nhqk,qhd->nkhd/dot_general | solution.py:413
  272.3 10.2 %convert_bitcast_fusion = bf16[8,256,8,160]{1,3,2,0:T(8,128)(2,1)} fusion(bf16[8,256,8,160]{1,3,2,0:T(8,128)(2,1)} %bitcast.105, bf16[8,8,256,256]{2,3,0,1:T(8,128)(2,1)} %get-tuple-element.60), kind=kOutput, calls=%fused_computation.27 | convolution fusion | flops 1344798720 | bytes 18874368 | tf_op jit(solution)/shard_map/nhqk,nqhd->nkhd/dot_general | solution.py:417
  282.5 5.7 copy.77
  288.2 2.3 copy.91
  290.6 4.8 fusion.60
  296.5 2.4 fusion.15
  299.2 3.2 fusion.13
  303.2 16.9 %psum.78 = bf16[32,256]{0,1:T(8,128)(2,1)S(1)} all-reduce(bf16[32,256]{0,1:T(8,128)(2,1)S(1)} %copy.89), channel_id=1, replica_groups=mesh['doc'=4,'blk'=8] {'doc'}, use_global_device_ids=true, to_apply=%region_12.13 | all-reduce | flops 8192 | bytes 32768 | tf_op jit(solution)/shard_map/psum | solution.py:447
  321.5 7.8 %fusion.14 = (bf16[8,256,768]{2,1,0:T(8,128)(2,1)S(1)}, f32[8,256,768]{2,1,0:T(8,128)}) fusion(bf16[8,256,768]{2,1,0:T(8,128)(2,1)S(1)} %copy-done.3, f32[8,256]{1,0:T(8,128)S(1)} %get-tuple-element.52, f32[8,256]{1,0:T(8,128)S(1)} %broadcast_multiply_fusion, f32[768]{0:T(1024)S(1)} %copy-done.34, f32[8,256]{1,0:T(8,128)S(1)} %negate_multiply_fusion, ...), kind=kLoop, calls=%fused_computation.22 | loop fusion | flops 17301504 | bytes 18910208 | tf_op jit(solution)/shard_map/convert_element_type | solution.py:359
  329.3 1.7 copy-done.20
  331.0 8.2 %convolution_convert_fusion.3 = bf16[768,1280]{1,0:T(8,128)(2,1)} fusion(bf16[2048,768]{1,0:T(8,128)(2,1)S(1)} %bitcast.117, bf16[2048,1280]{0,1:T(8,128)(2,1)} %bitcast.110), kind=kOutput, calls=%fused_computation.29 | convolution fusion | flops 4027514880 | bytes 10354688 | tf_op jit(solution)/shard_map/dot_general | solution.py:436
  339.3 3.8 convolution_convert_fusion.4
  344.2 12.2 %reduce-scatter.18.cloned.1.call-done = bf16[160,1280]{1,0:T(8,128)(2,1)} async-done(((bf16[1280,1280]{1,0:T(8,128)(2,1)}), bf16[160,1280]{1,0:T(8,128)(2,1)}) %reduce-scatter.18.cloned.1.call-update) | async-done | bytes 409616 | tf_op jit(solution)/shard_map/reduce_scatter | solution.py:484
  356.4 42.4 %reduce-scatter.16.cloned.1.call-done = bf16[160,1280]{1,0:T(8,128)(2,1)} async-done(((bf16[1280,1280]{1,0:T(8,128)(2,1)}), bf16[160,1280]{1,0:T(8,128)(2,1)}) %reduce-scatter.16.cloned.1.call-update) | async-done | bytes 409616 | tf_op jit(solution)/shard_map/reduce_scatter | solution.py:481
  398.8 32.9 %reduce-scatter.10.cloned.1.call-done = bf16[160,256]{1,0:T(8,128)(2,1)} async-done(((bf16[1280,256]{1,0:T(8,128)(2,1)}), bf16[160,256]{1,0:T(8,128)(2,1)}) %reduce-scatter.10.cloned.1.call-update) | async-done | bytes 81936 | tf_op jit(solution)/shard_map/reduce_scatter | solution.py:472
  431.7 36.1 %reduce-scatter.14.cloned.1.call-done = bf16[96,1280]{1,0:T(8,128)(2,1)} async-done(((bf16[768,1280]{1,0:T(8,128)(2,1)}), bf16[96,1280]{1,0:T(8,128)(2,1)}) %reduce-scatter.14.cloned.1.call-update) | async-done | bytes 245776 | tf_op jit(solution)/shard_map/reduce_scatter | solution.py:478
  469.7 5.2 convolution_add_fusion.1
  476.0 26.5 %all-reduce.3 = (bf16[1280]{0:T(1024)(128)(2,1)S(1)}, bf16[768]{0:T(1024)(128)(2,1)S(1)}, bf16[1280]{0:T(1024)(128)(2,1)S(1)}) all-reduce(bf16[1280]{0:T(1024)(128)(2,1)S(1)} %multiply_convert_fusion.6, bf16[768]{0:T(1024)(128)(2,1)S(1)} %get-tuple-element.22, ...), channel_id=3, replica_groups=mesh['doc'=4,'blk'=8] {'blk'}, use_global_device_ids=true, to_apply=%region_19.20.clone | all-reduce | flops 3328 | bytes 13312
  502.8 1.8 fusion.55
  504.6 18.7 %all-reduce.4 = (bf16[160]{0:T(256)(128)(2,1)S(1)}, bf16[96]{0:T(256)(128)(2,1)S(1)}, bf16[160]{0:T(256)(128)(2,1)S(1)}, bf16[96,256]{1,0:T(8,128)(2,1)S(1)}) all-reduce(bf16[160]{0:T(256)(128)(2,1)S(1)} %dynamic-slice.1, bf16[96]{0:T(256)(128)(2,1)S(1)} %dynamic-slice.3, ...), channel_id=1, replica_groups=mesh['doc'=4,'blk'=8] {'doc'}, use_global_device_ids=true, to_apply=%region_18.19 | all-reduce | flops 24992 | bytes 99968 | tf_op jit(solution)/shard_map/psum | solution.py:466
  525.6 40.6 %all-reduce.8.cloned.1.call-done = (bf16[32,1280]{1,0:T(8,128)(2,1)}, bf16[160,256]{1,0:T(8,128)(2,1)}, bf16[96,1280]{1,0:T(8,128)(2,1)}, bf16[160,1280]{1,0:T(8...) async-done(((bf16[32,1280]{1,0:T(8,128)(2,1)}, bf16[160,256]{1,0:T(8,128)(2,1)}, bf16[96,1280]{1,0:T(8,128)(2,1)}, bf16[160,1280]{1,0:T(8,128)(2,1)}, ...) | async-done | bytes 1638416 | tf_op jit(solution)/shard_map/psum | solution.py:446
  566.2 1.6 convert_element_type.177
  567.9 1.8 convert_element_type.182
  569.6 1.9 convert_element_type.185
  571.6 1.9 convert_element_type.187
  (143 shorter events, 25.7 us)
Async XLA Ops:
  7.2 136.8 %copy-start = (bf16[1280,1280]{1,0:T(8,128)(2,1)S(1)}, bf16[1280,1280]{1,0:T(8,128)(2,1)}, u32[]{:S(2)}) copy-start(bf16[1280,1280]{1,0:T(8,128)(2,1)} %param.25) | copy-start | bytes 9830404
  7.2 207.3 %all-gather.2.cloned.1.call-start = ((), (), s32[]{:S(2)}) async-start(), calls=%async_computation.7 | async-start | bytes 5898240 | tf_op jit(solution)/shard_map/all_gather | solution.py:403
  13.6 123.0 %copy-start.7 = (f32[32,1280]{1,0:T(8,128)S(1)}, f32[32,1280]{1,0:T(8,128)}, u32[]{:S(2)}) copy-start(f32[32,1280]{1,0:T(8,128)} %lat_ref.1) | copy-start | bytes 491524
  13.6 123.0 %copy-start.18 = (bf16[1280,1280]{1,0:T(8,128)(2,1)S(1)}, bf16[1280,1280]{1,0:T(8,128)(2,1)}, u32[]{:S(2)}) copy-start(bf16[1280,1280]{1,0:T(8,128)(2,1)} %param.24) | copy-start | bytes 9830404
  136.6 2.1 copy-start.12
  138.8 5.0 copy-start.35
  140.4 3.3 copy-start.6
  144.0 2.7 copy-start.14
  146.7 1.2 copy-start.27
  147.9 1.3 copy-start.9
  147.9 2.3 copy-start.19
  150.2 100.8 %copy-start.4 = (f32[256,1280]{1,0:T(8,128)}, f32[256,1280]{1,0:T(8,128)S(1)}, u32[]{:S(2)}) copy-start(f32[256,1280]{1,0:T(8,128)S(1)} %bitcast_add_fusion) | copy-start | bytes 3932164
  150.3 2.7 copy-start.10
  152.6 2.9 copy-start.31
  152.6 3.0 copy-start.33
  152.6 149.8 %reduce-scatter.22.cloned.1.call-start = ((), (), s32[]{:S(2)}) async-start(), calls=%async_computation.14 | async-start | bytes 147456
  155.5 2.5 copy-start.11
  185.4 7.9 %copy-start.24 = (bf16[8,256,256]{1,2,0:T(8,128)(2,1)S(1)}, bf16[8,256,256]{1,2,0:T(8,128)(2,1)}, u32[]{:S(2)}) copy-start(bf16[8,256,256]{1,2,0:T(8,128)(2,1)} %copy.65) | copy-start | bytes 3145732
  236.7 5.8 copy-start.26
  242.4 101.8 %reduce-scatter.20.cloned.1.call-start = ((), (), s32[]{:S(2)}) async-start(), calls=%async_computation.13 | async-start | bytes 3686400 | tf_op jit(solution)/shard_map/reduce_scatter | solution.py:487
  246.9 1.1 copy-start.15
  246.9 1.3 copy-start.28
  246.9 109.5 %reduce-scatter.18.cloned.1.call-start = ((), (), s32[]{:S(2)}) async-start(), calls=%async_computation.12 | async-start | bytes 3686400 | tf_op jit(solution)/shard_map/reduce_scatter | solution.py:484
  250.9 1.1 copy-start.13
  251.0 147.9 %reduce-scatter.16.cloned.1.call-start = ((), (), s32[]{:S(2)}) async-start(), calls=%async_computation.11 | async-start | bytes 3686400 | tf_op jit(solution)/shard_map/reduce_scatter | solution.py:481
  254.8 9.2 %copy-start.3 = (bf16[8,256,768]{2,1,0:T(8,128)(2,1)S(1)}, bf16[8,256,768]{2,1,0:T(8,128)(2,1)}, u32[]{:S(2)}) copy-start(bf16[8,256,768]{2,1,0:T(8,128)(2,1)} %x_ref.1) | copy-start | bytes 9437188
  254.8 176.9 %reduce-scatter.10.cloned.1.call-start = ((), (), s32[]{:S(2)}) async-start(), calls=%async_computation.8 | async-start | bytes 737280 | tf_op jit(solution)/shard_map/reduce_scatter | solution.py:472
  288.2 2.3 copy-start.22
  290.5 4.8 copy-start.8
  290.6 4.8 copy-start.16
  290.6 4.8 copy-start.23
  295.4 1.1 copy-start.34
  296.5 2.7 copy-start.2
  299.2 21.0 %copy-start.30 = (f32[1280]{0:T(1024)S(1)}, f32[1280]{0:T(1024)}, u32[]{:S(2)}) copy-start(f32[1280]{0:T(1024)} %param.18) | copy-start | bytes 15364
  321.5 146.3 %reduce-scatter.14.cloned.1.call-start = ((), (), s32[]{:S(2)}) async-start(), calls=%async_computation.10 | async-start | bytes 2211840 | tf_op jit(solution)/shard_map/reduce_scatter | solution.py:478
  329.3 1.7 copy-start.20
  331.0 8.3 %copy-start.17 = (bf16[32,8,8,256]{3,1,2,0:T(8,128)(2,1)S(1)}, bf16[32,8,8,256]{3,1,2,0:T(8,128)(2,1)}, u32[]{:S(2)}) copy-start(bf16[32,8,8,256]{3,1,2,0:T(8,128)(2,1)} %copy.90) | copy-start | bytes 3145732
  339.2 4.2 copy-start.5
  339.2 128.5 %copy-start.36 = (u32[32]{0:T(128)S(1)}, u32[32]{0:T(128)}, u32[]{:S(2)}) copy-start(u32[32]{0:T(128)} %constant.65) | copy-start | bytes 388
  339.3 165.3 %reduce-scatter.12.cloned.1.call-start = ((), (), s32[]{:S(2)}) async-start(), calls=%async_computation.9 | async-start | bytes 442368 | tf_op jit(solution)/shard_map/reduce_scatter | solution.py:475
  343.1 223.1 %all-reduce.8.cloned.1.call-start = ((), (), s32[]{:S(2)}) async-start(), calls=%async_computation.15 | async-start | bytes 3276800 | tf_op jit(solution)/shard_map/psum | solution.py:446
  469.7 5.2 copy-start.21
  469.7 105.5 %copy-start.1 = (bf16[1280,1280]{1,0:T(8,128)(2,1)S(1)}, bf16[1280,1280]{1,0:T(8,128)(2,1)}, u32[]{:S(2)}) copy-start(bf16[1280,1280]{1,0:T(8,128)(2,1)} %param.25) | copy-start | bytes 9830404
  504.5 69.9 %copy-start.25 = (f32[32,1280]{1,0:T(8,128)S(1)}, f32[32,1280]{1,0:T(8,128)}, u32[]{:S(2)}) copy-start(f32[32,1280]{1,0:T(8,128)} %get-tuple-element.44) | copy-start | bytes 491524
  566.2 7.3 %copy-start.29 = (bf16[160,1280]{1,0:T(8,128)(2,1)S(1)}, bf16[160,1280]{1,0:T(8,128)(2,1)}, u32[]{:S(2)}) copy-start(bf16[160,1280]{1,0:T(8,128)(2,1)} %get-tuple-element.42) | copy-start | bytes 1228804
  566.2 8.2 %copy-start.32 = (bf16[32,1280]{1,0:T(8,128)(2,1)S(1)}, bf16[32,1280]{1,0:T(8,128)(2,1)}, u32[]{:S(2)}) copy-start(bf16[32,1280]{1,0:T(8,128)(2,1)} %get-tuple-element.37) | copy-start | bytes 245764
Sparse Core Ops, SparseCore 0:
  152.8 61.7 all-gather.1
  242.5 29.5 reduce-scatter.21
  274.5 39.5 reduce-scatter.19
  316.2 40.0 reduce-scatter.17
  358.7 40.1 reduce-scatter.15
  401.5 30.0 reduce-scatter.9
  434.0 33.7 reduce-scatter.13
  470.7 28.9 reduce-scatter.11
  503.9 62.3 all-reduce.7

commit v2 on v1

v2 whole, which is shorter than its diff:
```python
import functools
import math

import jax
import jax.numpy as jnp
from jax import lax
from jax.experimental import pallas as pl
from jax.experimental.pallas import tpu as pltpu
from jax.sharding import PartitionSpec as P

LAT = 256
HEADS = 8
QK_HEAD = 32
V_HEAD = 160
DQK = HEADS * QK_HEAD
DV = HEADS * V_HEAD
MESH = pl.DeviceIdType.MESH
F32 = jnp.float32
BF16 = jnp.bfloat16

epsilon = 1e-05
masked_score = -1e30
LOG2E = math.log2(math.e)
SCORE2 = QK_HEAD ** (-0.5) * LOG2E
SCORE_SCALE = QK_HEAD ** (-0.5)


def dot_nn(a, b):
    return jnp.dot(a, b, preferred_element_type=F32)


def dot_nt(a, b):
    return lax.dot_general(a, b, (((1,), (1,)), ((), ())), preferred_element_type=F32)


def norm_parts(v):
    centered = v - jnp.mean(v, axis=-1, keepdims=True)
    spread = jnp.mean(centered * centered, axis=-1, keepdims=True)
    inv = lax.rsqrt(spread + epsilon)
    return centered * inv, inv


def window(h):
    return V_HEAD * h // 128 * 128


def value_mask(h, rows):
    lane = lax.broadcasted_iota(jnp.int32, (rows, 256), 1) + window(h)
    keep = (lane >= V_HEAD * h) & (lane < V_HEAD * (h + 1))
    return jnp.where(keep, 1.0, 0.0).astype(BF16)


def query_mask(h, rows):
    lane = lax.broadcasted_iota(jnp.int32, (rows, DQK), 1)
    keep = (lane >= QK_HEAD * h) & (lane < QK_HEAD * (h + 1))
    return jnp.where(keep, 1.0, 0.0).astype(BF16)


def row_to_lanes(row):
    return jnp.transpose(jnp.broadcast_to(row, (128, row.shape[1])))


def wide(col, n):
    return jnp.concatenate([col] * (n // 128), axis=1) if n > 128 else col


def remote(src, dst, send, recv, doc, blk):
    return pltpu.make_async_remote_copy(
        src_ref=src, dst_ref=dst, send_sem=send, recv_sem=recv,
        device_id=(doc, blk), device_id_type=MESH,
    )


def forward_kernel(
    nb,
    x_ref, bias_ref, lat_ref, gq_ref, gb_ref, wq_ref, wk_ref, wv_ref,
    att_ref, lse_ref, k_ref, v_ref, nlw_ref, qall_ref,
    nl_cols, normed, qm, lloc, lmate, lz, acc, part, mate_in, rin, lin,
    q_s, q_r, n_s, n_r, l_s, l_r, mate_s, mate_r, rs_s, rs_r, ls_s, ls_r,
):
    D, kc, din = x_ref.shape
    rq = lat_ref.shape[0]
    pos = nb // 2
    doc, blk = lax.axis_index("doc"), lax.axis_index("blk")
    p, c = blk // 2, blk % 2
    mate = 2 * p + 1 - c
    barrier = pltpu.get_barrier_semaphore()
    for i in range(1, nb):
        pl.semaphore_signal(
            barrier, inc=1, device_id=(doc, lax.rem(blk + i, nb)), device_id_type=MESH
        )

    xhat, _ = norm_parts(lat_ref[...])
    nl = (xhat * gq_ref[...]).astype(BF16)
    step = nl.shape[1] // nb
    for j in range(nb):
        at = min(j * step // 128 * 128, nl.shape[1] - 256)
        nl_cols[j] = nl[:, at : at + 256]
    own = pl.ds(pl.multiple_of(blk * rq, rq), rq)
    qall_ref[own, :] = dot_nn(nl, wq_ref[...]).astype(BF16)
    pl.semaphore_wait(barrier, nb - 1)

    def q_copy(i, slot):
        return remote(
            qall_ref.at[own, :], qall_ref.at[slot, :], q_s.at[i - 1], q_r.at[i - 1],
            doc, lax.rem(blk + i, nb),
        )

    def n_copy(i, slot):
        peer = lax.rem(blk + i, nb)
        return remote(
            nl_cols.at[peer], nlw_ref.at[slot, :], n_s.at[i - 1], n_r.at[i - 1], doc, peer
        )

    for i in range(1, nb):
        q_copy(i, own).start()
    for i in range(1, nb):
        n_copy(i, own).start()
    nlw_ref[own, :] = nl_cols[blk]

    @pl.loop(0, D)
    def _(n):
        xh, _ = norm_parts(x_ref[n].astype(F32))
        normed[n] = (xh * gb_ref[...]).astype(BF16)
        k_ref[n] = dot_nn(normed[n], wk_ref[...]).astype(BF16)

    for i in range(1, nb):
        src = lax.rem(blk + nb - i, nb)
        q_copy(i, pl.ds(pl.multiple_of(src * rq, rq), rq)).wait_recv()
    for h in range(HEADS):
        qm[h] = qall_ref[...] * query_mask(h, LAT)

    @pl.loop(0, D)
    def _(n):
        bias = wide(row_to_lanes(bias_ref[pl.ds(n, 1), :]), LAT)
        kn = k_ref[n]
        rows = []
        for h in range(HEADS):
            s = dot_nt(kn, qm[h]) * SCORE2 + bias
            top = jnp.max(s, axis=0, keepdims=True)
            tot = jnp.sum(jnp.exp2(s - top), axis=0, keepdims=True)
            rows.append(top + jnp.log(tot) * LOG2E)
        lloc[n] = jnp.concatenate(rows, axis=0)

    half = D // 2
    mine, other = pl.ds(c * half, half), pl.ds((1 - c) * half, half)

    def merge(a, b):
        top = jnp.maximum(a, b)
        return top + jnp.log(jnp.exp2(a - top) + jnp.exp2(b - top)) * LOG2E

    first = remote(lloc.at[other], lmate, l_s.at[0], l_r.at[0], doc, mate)
    first.start()

    def values(lo, hi):
        @pl.loop(lo, hi)
        def _(n):
            v_ref[n] = dot_nn(normed[n], wv_ref[...]).astype(BF16)

    values(0, D // 4)
    first.wait_recv()
    lz[p] = merge(lloc[mine], lmate[...])

    def z_copy(i, slot):
        return remote(
            lz.at[p], lz.at[slot], l_s.at[i], l_r.at[i],
            doc, 2 * lax.rem(p + i, pos) + c,
        )

    for i in range(1, pos):
        z_copy(i, p).start()
    values(D // 4, 3 * D // 4)
    for i in range(1, pos):
        z_copy(i, lax.rem(p + pos - i, pos)).wait_recv()
    total = lz[0]
    for i in range(1, pos):
        total = merge(total, lz[i])
    lse_ref[mine] = total
    last = remote(lse_ref.at[mine], lse_ref.at[mine], l_s.at[pos], l_r.at[pos], doc, mate)
    last.start()
    values(3 * D // 4, D)
    remote(
        lse_ref.at[other], lse_ref.at[other], l_s.at[pos], l_r.at[pos], doc, mate
    ).wait_recv()

    def mate_copy(n):
        return remote(
            part.at[n, 1 - c], mate_in.at[n], mate_s.at[n], mate_r.at[n], doc, mate
        )

    def right_copy(n, j, src):
        return remote(
            src, rin.at[n, j], rs_s.at[n, j], rs_r.at[n, j],
            doc, 2 * jnp.minimum(p + 1, pos - 1) + c,
        )

    def left_copy(n, j, src):
        return remote(
            src, lin.at[n, j], ls_s.at[n, j], ls_r.at[n, j],
            doc, 2 * jnp.maximum(p - 1, 0) + c,
        )

    def chip_sum(n):
        mate_copy(n).wait_recv()
        for j in range(pos):
            both = part[n, c, j].astype(F32) + mate_in[n, j].astype(F32)
            part[n, c, j] = both.astype(BF16)

            @pl.when((p == 0) & (j > 0))
            def _():
                right_copy(n, j, part.at[n, c, j]).start()

            @pl.when((p == pos - 1) & (j < pos - 1))
            def _():
                left_copy(n, j, part.at[n, c, j]).start()

    @pl.loop(0, D)
    def _(n):
        logs = lse_ref[n]
        logs_t = jnp.transpose(jnp.concatenate([logs] * (128 // HEADS), axis=0))
        bias = bias_ref[pl.ds(n, 1), :]
        kn = k_ref[n]
        acc[...] = jnp.zeros_like(acc)
        for h in range(HEADS):
            s = dot_nt(qm[h], kn) * SCORE2 + bias
            prob = jnp.exp2(s - logs_t[:, h : h + 1]).astype(BF16)
            cols = slice(window(h), window(h) + 256)
            acc[:, cols] += dot_nn(prob, v_ref[n, :, cols] * value_mask(h, kc))
        for j in range(nb):
            part[n, j % 2, j // 2] = acc[rq * j : rq * (j + 1), :].astype(BF16)
        mate_copy(n).start()

        @pl.when(n > 0)
        def _():
            chip_sum(n - 1)

    chip_sum(D - 1)

    def from_left(n):
        for j in range(1, pos):
            @pl.when(j >= p)
            def _():
                right_copy(n, j, part.at[n, c, j]).wait_recv()

            @pl.when(j > p)
            def _():
                both = rin[n, j].astype(F32) + part[n, c, j].astype(F32)
                part[n, c, j] = both.astype(BF16)
                right_copy(n, j, part.at[n, c, j]).start()

    def from_right(n):
        for j in range(pos - 2, -1, -1):
            @pl.when(j <= p)
            def _():
                left_copy(n, j, part.at[n, c, j]).wait_recv()

            @pl.when(j < p)
            def _():
                both = lin[n, j].astype(F32) + part[n, c, j].astype(F32)
                part[n, c, j] = both.astype(BF16)
                left_copy(n, j, part.at[n, c, j]).start()

    def finish(n):
        att_ref[n] = part[n, c, p].astype(F32)

        @pl.when(p > 0)
        def _():
            att_ref[n] += rin[n, p].astype(F32)

        @pl.when(p < pos - 1)
        def _():
            att_ref[n] += lin[n, p].astype(F32)

    @pl.loop(0, D + pos - 1)
    def _(t):
        right_n, left_n, done_n = t - p, t - (pos - 1 - p), t - (pos - 1)

        @pl.when((p > 0) & (right_n >= 0) & (right_n < D))
        def _():
            from_left(right_n)

        @pl.when((p < pos - 1) & (left_n >= 0) & (left_n < D))
        def _():
            from_right(left_n)

        @pl.when(done_n >= 0)
        def _():
            finish(done_n)

    for i in range(1, nb):
        src = lax.rem(blk + nb - i, nb)
        n_copy(i, pl.ds(pl.multiple_of(src * rq, rq), rq)).wait_recv()

    for i in range(1, nb):
        q_copy(i, own).wait_send()
        n_copy(i, own).wait_send()
    first.wait_send()
    for i in range(1, pos):
        z_copy(i, p).wait_send()
    last.wait_send()

    @pl.loop(0, D)
    def _(n):
        mate_copy(n).wait_send()
        for j in range(pos):
            @pl.when((j > p) & (p < pos - 1))
            def _():
                right_copy(n, j, part.at[n, c, j]).wait_send()

            @pl.when((j < p) & (p > 0))
            def _():
                left_copy(n, j, part.at[n, c, j]).wait_send()


def forward(nb, byte_embed, bias, latents, gain_query, gain_bytes, w_query, w_key, w_value):
    D, kc, din = byte_embed.shape
    rq, dl = latents.shape
    pos = nb // 2
    vmem = pl.BlockSpec(memory_space=pltpu.VMEM)
    dma = pltpu.SemaphoreType.DMA
    return pl.pallas_call(
        functools.partial(forward_kernel, nb),
        out_shape=(
            jax.ShapeDtypeStruct((D, rq, DV), F32),
            jax.ShapeDtypeStruct((D, HEADS, LAT), F32),
            jax.ShapeDtypeStruct((D, kc, DQK), BF16),
            jax.ShapeDtypeStruct((D, kc, DV), BF16),
            jax.ShapeDtypeStruct((LAT, 256), BF16),
            jax.ShapeDtypeStruct((LAT, DQK), BF16),
        ),
        in_specs=[vmem] * 8,
        out_specs=(vmem,) * 6,
        scratch_shapes=[
            pltpu.VMEM((nb, rq, 256), BF16),
            pltpu.VMEM((D, kc, din), BF16),
            pltpu.VMEM((HEADS, LAT, DQK), BF16),
            pltpu.VMEM((D, HEADS, LAT), F32),
            pltpu.VMEM((D // 2, HEADS, LAT), F32),
            pltpu.VMEM((pos, D // 2, HEADS, LAT), F32),
            pltpu.VMEM((LAT, DV), F32),
            pltpu.VMEM((D, 2, pos, rq, DV), BF16),
            pltpu.VMEM((D, pos, rq, DV), BF16),
            pltpu.VMEM((D, pos, rq, DV), BF16),
            pltpu.VMEM((D, pos, rq, DV), BF16),
            dma((nb - 1,)), dma((nb - 1,)), dma((nb - 1,)), dma((nb - 1,)),
            dma((pos + 1,)), dma((pos + 1,)),
            dma((D,)), dma((D,)),
            dma((D, pos)), dma((D, pos)), dma((D, pos)), dma((D, pos)),
        ],
        compiler_params=pltpu.CompilerParams(
            collective_id=0, has_side_effects=True, vmem_limit_bytes=56 * 2**20
        ),
        name="forward",
    )(
        byte_embed, bias, latents, gain_query.reshape(1, -1), gain_bytes.reshape(1, -1),
        w_query, w_key, w_value,
    )


def gelu_parts(u):
    k = math.sqrt(2.0 / math.pi)
    sq = u * u
    t = jnp.tanh(k * u * (1.0 + 0.044715 * sq))
    value = 0.5 * u * (1.0 + t)
    slope = 0.5 * (1.0 + t) + 0.5 * k * u * (1.0 - t * t) * (1.0 + 3 * 0.044715 * sq)
    return value, slope


def mlp_kernel(
    nb, half,
    att_ref, lat_ref, gm_ref, wo_ref, wu_ref, wd_ref, cot_ref,
    out_ref, ga_ref, delta_ref, wg_ref, direct_ref, gain_ref,
    mid, xhat, slope, low_t, gmid,
):
    D, rq, dv = att_ref.shape
    rows = D * rq
    dl = lat_ref.shape[1]
    step = dl // nb
    blocks = dl // 256

    def weight_grad(m, left, right_ref_cols):
        low_t[...] = jnp.transpose(left)
        for b in range(blocks):
            r = dot_nn(low_t[...], right_ref_cols(b)).astype(BF16)
            for i in range(2):
                col = 256 * b + 128 * i
                at, lane = col // half, col % half
                for k in range(nb):
                    wg_ref[m, k, at * step : (at + 1) * step, lane : lane + 128] = r[
                        k * step : (k + 1) * step, 128 * i : 128 * (i + 1)
                    ]

    att = att_ref[...].reshape(rows, dv)
    att_low = att.astype(BF16)
    lat = lat_ref[...]
    mid[...] = dot_nn(att_low, wo_ref[...]) + jnp.concatenate([lat] * D, axis=0)
    xh, inv = norm_parts(mid[...])
    xhat[...] = xh
    nm = (xh * gm_ref[...]).astype(BF16)
    up = dot_nn(nm, wu_ref[...])
    act, sl = gelu_parts(up)
    slope[...] = sl
    act_low = act.astype(BF16)
    out_ref[...] = (mid[...] + dot_nn(act_low, wd_ref[...])).reshape(D, rq, dl)
    cot = cot_ref[...].reshape(rows, dl)
    gm = cot.astype(BF16)
    weight_grad(0, act_low, lambda b: gm[:, 256 * b : 256 * (b + 1)])
    g_up = (dot_nt(gm, wd_ref[...]) * slope[...]).astype(BF16)
    weight_grad(1, nm, lambda b: g_up[:, 256 * b : 256 * (b + 1)])
    g_nm = dot_nt(g_up, wu_ref[...])
    xh = xhat[...]
    gain_ref[...] = jnp.sum(g_nm * xh, axis=0, keepdims=True)
    dxh = g_nm * gm_ref[...]
    dmid = inv * (
        dxh
        - jnp.mean(dxh, axis=-1, keepdims=True)
        - xh * jnp.mean(dxh * xh, axis=-1, keepdims=True)
    )
    gmid[...] = cot + dmid
    direct = gmid[0:rq, :]
    for n in range(1, D):
        direct = direct + gmid[n * rq : (n + 1) * rq, :]
    direct_ref[...] = direct.astype(BF16)
    gb = gmid[...].astype(BF16)
    weight_grad(2, att_low, lambda b: gb[:, 256 * b : 256 * (b + 1)])
    ga = dot_nt(gb, wo_ref[...])
    ga_ref[...] = ga.astype(BF16).reshape(D, rq, dv)
    prod = ga * att
    lane = lax.broadcasted_iota(jnp.int32, (rq, 128), 1)
    delta = jnp.zeros((rq, 128), F32)
    for h in range(HEADS):
        cols = lax.broadcasted_iota(jnp.int32, (rows, 256), 1) + window(h)
        keep = (cols >= V_HEAD * h) & (cols < V_HEAD * (h + 1))
        one = jnp.sum(
            jnp.where(keep, prod[:, window(h) : window(h) + 256], 0.0), axis=1, keepdims=True
        )
        for n in range(D):
            delta = delta + jnp.where(lane == n * HEADS + h, one[n * rq : (n + 1) * rq], 0.0)
    delta_ref[...] = delta


def owner_rows(total, docs):
    return -(-total // (16 * docs)) * 16


def mlp(nb, nd, att, latents, gain_mlp, w_out, w_up, w_down, cotangent):
    D, rq, dv = att.shape
    dl = latents.shape[1]
    half = dl // 2
    rows = owner_rows(2 * dl // nb, nd) * nd
    vmem = pl.BlockSpec(memory_space=pltpu.VMEM)
    return pl.pallas_call(
        functools.partial(mlp_kernel, nb, half),
        out_shape=(
            jax.ShapeDtypeStruct((D, rq, dl), F32),
            jax.ShapeDtypeStruct((D, rq, dv), BF16),
            jax.ShapeDtypeStruct((rq, 128), F32),
            jax.ShapeDtypeStruct((3, nb, rows, half), BF16),
            jax.ShapeDtypeStruct((rq, dl), BF16),
            jax.ShapeDtypeStruct((1, dl), F32),
        ),
        in_specs=[vmem] * 7,
        out_specs=(vmem,) * 6,
        scratch_shapes=[
            pltpu.VMEM((D * rq, dl), F32),
            pltpu.VMEM((D * rq, dl), F32),
            pltpu.VMEM((D * rq, dl), F32),
            pltpu.VMEM((dl, D * rq), BF16),
            pltpu.VMEM((D * rq, dl), F32),
        ],
        compiler_params=pltpu.CompilerParams(vmem_limit_bytes=60 * 2**20),
        name="feed_forward",
    )(att, latents, gain_mlp.reshape(1, -1), w_out, w_up, w_down, cotangent)


class ShardSums:
    def __init__(self, doc, blk, nd, nb, count, unit, own, mate_in, inbox, rin, lin, out, sems):
        self.doc, self.p, self.c = doc, blk // 2, blk % 2
        self.nd, self.pos, self.count, self.unit = nd, nb // 2, count, unit
        self.bits = nd.bit_length() - 1
        self.own, self.mate_in, self.inbox = own, mate_in, inbox
        self.rin, self.lin, self.out = rin, lin, out
        (
            self.mate_s, self.mate_r, self.own_s, self.in_s, self.in_r,
            self.right_s, self.right_r, self.left_s, self.left_r, self.out_s, self.out_r,
        ) = sems
        self.lag = self.bits + self.pos - 1

    def weight(self, s, k):
        b = (s + k) % self.bits
        return 1 + b * (b + 1) // 2

    def my_bit(self, w):
        return (self.doc // w) % 2

    def quarter(self, s, k, i, sent):
        q = 0
        for r in range(k):
            w = self.weight(s, r)
            q = q + self.my_bit(w) * w
        w = self.weight(s, k)
        mine = self.my_bit(w)
        q = q + ((1 - mine) if sent else mine) * w
        for r in range(k + 1, self.bits):
            q = q + ((i >> (r - k - 1)) & 1) * self.weight(s, r)
        return q

    def width(self, k):
        return 2 ** (self.bits - 1 - k)

    def slot(self, k, i):
        return sum(self.width(r) for r in range(k)) + i

    def rows(self, q):
        return pl.ds(pl.multiple_of(q * self.unit, self.unit), self.unit)

    def halving(self, s, k, i):
        w = self.weight(s, k)
        peer = self.doc + w * (1 - 2 * self.my_bit(w))
        slot = self.slot(k, i)
        return remote(
            self.own.at[s, self.rows(self.quarter(s, k, i, True)), :], self.inbox.at[s, slot],
            self.in_s.at[s, slot], self.in_r.at[s, slot], peer, 2 * self.p + self.c,
        )

    def right(self, s):
        return remote(
            self.own.at[s, self.rows(self.doc), :], self.rin.at[s],
            self.right_s.at[s], self.right_r.at[s],
            self.doc, 2 * jnp.minimum(self.p + 1, self.pos - 1) + self.c,
        )

    def left(self, s):
        return remote(
            self.own.at[s, self.rows(self.doc), :], self.lin.at[s],
            self.left_s.at[s], self.left_r.at[s],
            self.doc, 2 * jnp.maximum(self.p - 1, 0) + self.c,
        )

    def share(self, m, i):
        return remote(
            self.out.at[m, self.rows(self.doc), :], self.out.at[m, self.rows(self.doc), :],
            self.out_s.at[m, i - 1], self.out_r.at[m, i - 1],
            lax.rem(self.doc + i, self.nd), 2 * self.p + self.c,
        )

    def shared(self, m, i):
        src = lax.rem(self.doc + self.nd - i, self.nd)
        return remote(
            self.out.at[m, self.rows(src), :], self.out.at[m, self.rows(src), :],
            self.out_s.at[m, i - 1], self.out_r.at[m, i - 1], src, 2 * self.p + self.c,
        )

    def add(self, s, q, other):
        rows = self.rows(q)
        self.own[s, rows, :] = (
            self.own[s, rows, :].astype(F32) + other.astype(F32)
        ).astype(BF16)

    def begin(self, s, mate_copy, own_copy):
        own_copy(s).wait()
        mate_copy(s).wait_recv()
        for q in range(self.nd):
            self.add(s, q, self.mate_in[s, self.unit * q : self.unit * (q + 1), :])
        for i in range(self.width(0)):
            self.halving(s, 0, i).start()

    def halve(self, s, k):
        for i in range(self.width(k - 1)):
            self.halving(s, k - 1, i).wait_recv()
            self.add(s, self.quarter(s, k - 1, i, False), self.inbox[s, self.slot(k - 1, i)])
        if k < self.bits:
            for i in range(self.width(k)):
                self.halving(s, k, i).start()
            return
        j = s % self.pos

        @pl.when((self.p == 0) & (j > 0))
        def _():
            self.right(s).start()

        @pl.when((self.p == self.pos - 1) & (j < self.pos - 1))
        def _():
            self.left(s).start()

    def from_left(self, s):
        j = s % self.pos

        @pl.when(j >= self.p)
        def _():
            self.right(s).wait_recv()

        @pl.when(j > self.p)
        def _():
            self.add(s, self.doc, self.rin[s])
            self.right(s).start()

    def from_right(self, s):
        j = s % self.pos

        @pl.when(j <= self.p)
        def _():
            self.left(s).wait_recv()

        @pl.when(j < self.p)
        def _():
            self.add(s, self.doc, self.lin[s])
            self.left(s).start()

    def finish(self, s):
        @pl.when(s % self.pos == self.p)
        def _():
            m = s // self.pos

            @pl.when(self.p > 0)
            def _():
                self.add(s, self.doc, self.rin[s])

            @pl.when(self.p < self.pos - 1)
            def _():
                self.add(s, self.doc, self.lin[s])

            self.out[m, self.rows(self.doc), :] = self.own[s, self.rows(self.doc), :]
            for i in range(1, self.nd):
                self.share(m, i).start()

    def step(self, t, mate_copy, own_copy):
        def at(s, when, run):
            @pl.when((s >= 0) & (s < self.count) & when)
            def _():
                run(s)

        at(t, True, lambda s: self.begin(s, mate_copy, own_copy))
        for k in range(1, self.bits + 1):
            at(t - k, True, functools.partial(self.halve, k=k))
        base = t - self.bits
        at(base - self.p, self.p > 0, self.from_left)
        at(base - (self.pos - 1 - self.p), self.p < self.pos - 1, self.from_right)
        at(base - (self.pos - 1), True, self.finish)

    def drain(self, mate_copy):
        for m in range(self.count // self.pos):
            for i in range(1, self.nd):
                self.shared(m, i).wait_recv()
                self.share(m, i).wait_send()

        @pl.loop(0, self.count)
        def _(s):
            mate_copy(s).wait_send()
            for k in range(self.bits):
                for i in range(self.width(k)):
                    self.halving(s, k, i).wait_send()
            j = s % self.pos

            @pl.when((j > self.p) & (self.p < self.pos - 1))
            def _():
                self.right(s).wait_send()

            @pl.when((j < self.p) & (self.p > 0))
            def _():
                self.left(s).wait_send()


def shard_sum_scratch(nd, nb, count, unit, width):
    dma = pltpu.SemaphoreType.DMA
    arrays = count // (nb // 2)
    return [
        pltpu.VMEM((count, unit * nd, width), BF16),
        pltpu.VMEM((count, unit * nd, width), BF16),
        pltpu.VMEM((count, nd - 1, unit, width), BF16),
        pltpu.VMEM((count, unit, width), BF16),
        pltpu.VMEM((count, unit, width), BF16),
        dma((count,)), dma((count,)), dma((count,)),
        dma((count, nd - 1)), dma((count, nd - 1)),
        dma((count,)), dma((count,)), dma((count,)), dma((count,)),
        dma((arrays, nd - 1)), dma((arrays, nd - 1)),
    ]


def backward_kernel(nb, nd, wunit, vunit, *refs):
    (
        x_hbm, k_hbm, v_hbm, wg_hbm, bias_ref, gb_ref, wk_ref, wv_ref, qall_ref, lse_ref,
        ga_ref, delta_ref, direct_ref, gain_ref,
    ) = refs[:14]
    bg_hbm, wsum_ref, vsum_ref, dsum_ref, gq_ref, gains_ref = refs[14:20]
    wscr, vscr = refs[20:36], refs[36:52]
    (
        x_ref, k_ref, v_ref, ga_all, delta_all, delta_t, qm, ds_all, gv_acc, gq_acc,
        kv_acc, kv_part, gain_acc, bg_buf, dir_in, misc_out, misc_in, misc2_out, misc2_in, gq_own,
        load_s, bg_s, ar_s, ar_r, al_s, al_r, am_s, am_r, d_s, d_r, dir_s, dir_r,
        m1_s, m1_r, m2_s, m2_r, m3_s, m3_r,
    ) = refs[52:]
    D, kc, din = x_ref.shape
    rq = ga_ref.shape[1]
    pos = nb // 2
    doc, blk = lax.axis_index("doc"), lax.axis_index("blk")
    p, c = blk // 2, blk % 2
    mate = 2 * p + 1 - c

    barrier = pltpu.get_barrier_semaphore()
    for i in range(1, nb):
        pl.semaphore_signal(
            barrier, inc=1, device_id=(doc, lax.rem(blk + i, nb)), device_id_type=MESH
        )
    for i in range(1, nd):
        pl.semaphore_signal(
            barrier, inc=1, device_id=(lax.rem(doc + i, nd), blk), device_id_type=MESH
        )

    loads = [
        pltpu.make_async_copy(src, dst, load_s.at[i])
        for i, (src, dst) in enumerate(((k_hbm, k_ref), (v_hbm, v_ref), (x_hbm, x_ref)))
    ]
    for load in loads:
        load.start()

    weights = ShardSums(
        doc, blk, nd, nb, 3 * pos, wunit, *wscr[:5], wsum_ref, wscr[5:]
    )
    values = ShardSums(doc, blk, nd, nb, pos, vunit, *vscr[:5], vsum_ref, vscr[5:])

    def w_mate(s):
        return remote(
            wg_hbm.at[s // pos, 2 * (s % pos) + 1 - c], weights.mate_in.at[s],
            weights.mate_s.at[s], weights.mate_r.at[s], doc, mate,
        )

    def w_own(s):
        return pltpu.make_async_copy(
            wg_hbm.at[s // pos, 2 * (s % pos) + c], weights.own.at[s], weights.own_s.at[s]
        )

    def v_mate(s):
        return remote(
            kv_part.at[2 * s + 1 - c], values.mate_in.at[s],
            values.mate_s.at[s], values.mate_r.at[s], doc, mate,
        )

    def v_own(s):
        return pltpu.make_async_copy(
            kv_part.at[2 * s + c], values.own.at[s], values.own_s.at[s]
        )

    def chunk(j, core):
        return pl.ds(pl.multiple_of((2 * j + core) * rq, rq), rq)

    def right_copy(n, hop, j):
        rows = ga_all.at[n, chunk(j, c), :]
        return remote(
            rows, rows, ar_s.at[n, hop], ar_r.at[n, hop],
            doc, 2 * jnp.minimum(p + 1, pos - 1) + c,
        )

    def left_copy(n, hop, j):
        rows = ga_all.at[n, chunk(j, c), :]
        return remote(
            rows, rows, al_s.at[n, hop], al_r.at[n, hop],
            doc, 2 * jnp.maximum(p - 1, 0) + c,
        )

    def mate_copy(n, j, core):
        rows = ga_all.at[n, chunk(j, core), :]
        return remote(rows, rows, am_s.at[n, j], am_r.at[n, j], doc, mate)

    own_rows = pl.ds(pl.multiple_of(blk * rq, rq), rq)

    def delta_copy(i, rows):
        return remote(
            delta_all.at[rows, :], delta_all.at[rows, :], d_s.at[i - 1], d_r.at[i - 1],
            doc, lax.rem(blk + i, nb),
        )

    def direct_copy(i):
        return remote(
            direct_ref, dir_in.at[i - 1], dir_s.at[i - 1], dir_r.at[i - 1],
            lax.rem(doc + i, nd), blk,
        )

    for h in range(HEADS):
        qm[h * LAT : (h + 1) * LAT, :] = qall_ref[...] * query_mask(h, LAT)
    gq_acc[...] = jnp.zeros_like(gq_acc)
    kv_acc[...] = jnp.zeros_like(kv_acc)
    gain_acc[...] = jnp.zeros_like(gain_acc)
    delta_all[own_rows, :] = delta_ref[...]
    for n in range(D):
        ga_all[n, own_rows, :] = ga_ref[n]

    pl.semaphore_wait(barrier, nb - 1 + nd - 1)
    for i in range(1, nb):
        delta_copy(i, own_rows).start()

    @pl.loop(0, D)
    def _(n):
        @pl.when(p < pos - 1)
        def _():
            right_copy(n, 0, p).start()

        @pl.when(p > 0)
        def _():
            left_copy(n, 0, p).start()

        mate_copy(n, p, c).start()

    @pl.loop(0, weights.count)
    def _(s):
        w_own(s).start()
        w_mate(s).start()

    for i in range(1, nd):
        direct_copy(i).start()

    def forward_chunks(n, hop):
        j = p - 1 - hop

        @pl.when(j >= 0)
        def _():
            right_copy(n, hop, j).wait_recv()
            if hop + 1 < pos - 1:
                @pl.when(p < pos - 1)
                def _():
                    right_copy(n, hop + 1, j).start()

            mate_copy(n, j, c).start()

        i = p + 1 + hop

        @pl.when(i < pos)
        def _():
            left_copy(n, hop, i).wait_recv()
            if hop + 1 < pos - 1:
                @pl.when(p > 0)
                def _():
                    left_copy(n, hop + 1, i).start()

            mate_copy(n, i, c).start()

    def bytes_back(n):
        for j in range(pos):
            mate_copy(n, j, 1 - c).wait_recv()
        bias = wide(row_to_lanes(bias_ref[pl.ds(n, 1), :]), LAT)
        logs, deltas = lse_ref[n], delta_t[n]
        kn = k_ref[n]
        kt = jnp.transpose(kn)
        gv_acc[...] = jnp.zeros_like(gv_acc)
        for h in range(HEADS):
            cols = slice(window(h), window(h) + 256)
            gah = ga_all[n, :, cols] * value_mask(h, LAT)
            s = dot_nt(kn, qm[h * LAT : (h + 1) * LAT, :]) * SCORE2 + bias
            prob = jnp.exp2(s - logs[h : h + 1, :])
            dprob = dot_nt(v_ref[n, :, cols], gah)
            ds = (prob * (dprob - deltas[h : h + 1, :])).astype(BF16)
            ds_all[:, h * LAT : (h + 1) * LAT] = ds
            gv_acc[:, cols] += dot_nn(prob.astype(BF16), gah)
            head = slice(QK_HEAD * h, QK_HEAD * (h + 1))
            gq_acc[head, :] += dot_nn(kt[head, :], ds)
        gk = (dot_nn(ds_all[...], qm[...]) * SCORE_SCALE).astype(BF16)
        gv = gv_acc[...].astype(BF16)
        gx = dot_nt(gv, wv_ref[...]) + dot_nt(gk, wk_ref[...])
        xh, inv = norm_parts(x_ref[n].astype(F32))
        gain_acc[...] += jnp.sum(gx * xh, axis=0, keepdims=True)
        dxh = gx * gb_ref[...]
        slot = lax.rem(n, 2)

        @pl.when(n >= 2)
        def _():
            pltpu.make_async_copy(bg_buf.at[slot], bg_hbm.at[n - 2], bg_s.at[slot]).wait()

        bg_buf[slot] = inv * (
            dxh
            - jnp.mean(dxh, axis=-1, keepdims=True)
            - xh * jnp.mean(dxh * xh, axis=-1, keepdims=True)
        )
        pltpu.make_async_copy(bg_buf.at[slot], bg_hbm.at[n], bg_s.at[slot]).start()
        normed_t = jnp.transpose((xh * gb_ref[...]).astype(BF16))
        kv_acc[:, 0:DV] += dot_nn(normed_t, gv)
        kv_acc[:, DV : DV + DQK] += dot_nn(normed_t, gk)

    @pl.loop(0, D + pos)
    def _(t):
        for hop in range(pos - 1):
            @pl.when((t >= hop) & (t - hop < D))
            def _():
                forward_chunks(t - hop, hop)

        weights.step(t, w_mate, w_own)

        @pl.when(t == pos)
        def _():
            for i in range(1, nb):
                src = lax.rem(blk + nb - i, nb)
                delta_copy(i, pl.ds(pl.multiple_of(src * rq, rq), rq)).wait_recv()
            turned = jnp.transpose(delta_all[...])
            for n in range(D):
                delta_t[n] = turned[n * HEADS : (n + 1) * HEADS, :]
            for load in loads:
                load.wait()

        @pl.when(t >= pos)
        def _():
            bytes_back(t - pos)

    gq_rows = (jnp.transpose(gq_acc[...]) * SCORE_SCALE).astype(BF16)
    gains = jnp.concatenate([gain_ref[...], gain_acc[...]], axis=1)
    rows8 = [gains[:, 256 * i : 256 * (i + 1)] for i in range(8)]
    gains8 = jnp.concatenate(rows8 + [jnp.zeros((8, 256), F32)], axis=0).astype(BF16)
    for j in range(nb):
        misc_out[j, 0:rq] = gq_rows[j * rq : (j + 1) * rq, :]
        misc_out[j, rq : rq + 16] = gains8

    def misc1(i, slot):
        peer = lax.rem(blk + i, nb)
        return remote(
            misc_out.at[peer], misc_in.at[slot], m1_s.at[i - 1], m1_r.at[i - 1], doc, peer
        )

    for i in range(1, nb):
        misc1(i, blk).start()

    step = din // nb
    for k in range(nb):
        rows = slice(k * step, (k + 1) * step)
        kv_part[k, 0:step, :] = kv_acc[rows, 0:din].astype(BF16)
        kv_part[k, step : 2 * step, :] = kv_acc[rows, din : 2 * din].astype(BF16)

    @pl.loop(0, values.count)
    def _(s):
        v_own(s).start()
        v_mate(s).start()

    misc_in[blk] = misc_out[blk]
    for i in range(1, nb):
        misc1(i, lax.rem(blk + nb - i, nb)).wait_recv()
    total = misc_in[0].astype(F32)
    for i in range(1, nb):
        total = total + misc_in[i].astype(F32)
    misc2_out[...] = total.astype(BF16)

    def misc2(i, slot):
        return remote(
            misc2_out, misc2_in.at[slot], m2_s.at[i - 1], m2_r.at[i - 1],
            lax.rem(doc + i, nd), blk,
        )

    for i in range(1, nd):
        misc2(i, doc).start()
    misc2_in[doc] = misc2_out[...]

    first, last = D + pos, weights.count + weights.lag
    last = max(last, first + values.count + values.lag)

    def misc3(i, rows):
        return remote(
            gq_ref.at[rows, :], gq_ref.at[rows, :], m3_s.at[i - 1], m3_r.at[i - 1],
            doc, lax.rem(blk + i, nb),
        )

    @pl.loop(first, last)
    def _(t):
        weights.step(t, w_mate, w_own)
        values.step(t - first, v_mate, v_own)

        @pl.when(t == first + 2)
        def _():
            for i in range(1, nd):
                misc2(i, lax.rem(doc + nd - i, nd)).wait_recv()
            total = misc2_in[0].astype(F32)
            for i in range(1, nd):
                total = total + misc2_in[i].astype(F32)
            gains_ref[...] = total[rq : rq + 8, :]
            gq_ref[own_rows, :] = total[0:rq].astype(BF16)
            for i in range(1, nb):
                misc3(i, own_rows).start()

    for i in range(1, nb):
        src = lax.rem(blk + nb - i, nb)
        misc3(i, pl.ds(pl.multiple_of(src * rq, rq), rq)).wait_recv()

    total = direct_ref[...].astype(F32)
    for i in range(1, nd):
        direct_copy(i).wait_recv()
        total = total + dir_in[i - 1].astype(F32)
    dsum_ref[...] = total

    for n in range(D - 2, D):
        pltpu.make_async_copy(bg_buf.at[n % 2], bg_hbm.at[n], bg_s.at[n % 2]).wait()
    weights.drain(w_mate)
    values.drain(v_mate)
    for i in range(1, nb):
        delta_copy(i, own_rows).wait_send()
        misc1(i, blk).wait_send()
        misc3(i, own_rows).wait_send()
    for i in range(1, nd):
        direct_copy(i).wait_send()
        misc2(i, doc).wait_send()

    @pl.loop(0, D)
    def _(n):
        mate_copy(n, p, c).wait_send()

        @pl.when(p < pos - 1)
        def _():
            right_copy(n, 0, p).wait_send()

        @pl.when(p > 0)
        def _():
            left_copy(n, 0, p).wait_send()

        for hop in range(pos - 1):
            j = p - 1 - hop

            @pl.when(j >= 0)
            def _():
                mate_copy(n, j, c).wait_send()
                if hop + 1 < pos - 1:
                    @pl.when(p < pos - 1)
                    def _():
                        right_copy(n, hop + 1, j).wait_send()

            i = p + 1 + hop

            @pl.when(i < pos)
            def _():
                mate_copy(n, i, c).wait_send()
                if hop + 1 < pos - 1:
                    @pl.when(p > 0)
                    def _():
                        left_copy(n, hop + 1, i).wait_send()


def backward(
    nb, nd, byte_embed, keys, values, wgrads, bias, gain_bytes, w_key, w_value, queries, lse,
    ga, delta, direct, gain_part,
):
    D, kc, din = byte_embed.shape
    rq, dl = direct.shape
    pos = nb // 2
    wunit, vunit = owner_rows(2 * dl // nb, nd), owner_rows(2 * din // nb, nd)
    whalf = dl // 2
    vmem = pl.BlockSpec(memory_space=pltpu.VMEM)
    anywhere = pl.BlockSpec(memory_space=pl.ANY)
    dma = pltpu.SemaphoreType.DMA
    scratch = (
        shard_sum_scratch(nd, nb, 3 * pos, wunit, whalf)
        + shard_sum_scratch(nd, nb, pos, vunit, din)
        + [
            pltpu.VMEM((D, kc, din), BF16),
            pltpu.VMEM((D, kc, DQK), BF16),
            pltpu.VMEM((D, kc, DV), BF16),
            pltpu.VMEM((D, LAT, DV), BF16),
            pltpu.VMEM((LAT, 128), F32),
            pltpu.VMEM((D, HEADS, LAT), F32),
            pltpu.VMEM((HEADS * LAT, DQK), BF16),
            pltpu.VMEM((kc, HEADS * LAT), BF16),
            pltpu.VMEM((kc, DV), F32),
            pltpu.VMEM((DQK, LAT), F32),
            pltpu.VMEM((din, DV + DQK), F32),
            pltpu.VMEM((nb, vunit * nd, din), BF16),
            pltpu.VMEM((1, din), F32),
            pltpu.VMEM((2, kc, din), F32),
            pltpu.VMEM((nd - 1, rq, dl), BF16),
            pltpu.VMEM((nb, rq + 16, 256), BF16),
            pltpu.VMEM((nb, rq + 16, 256), BF16),
            pltpu.VMEM((rq + 16, 256), BF16),
            pltpu.VMEM((nd, rq + 16, 256), BF16),
            pltpu.VMEM((rq, 256), BF16),
            dma((3,)), dma((2,)),
            dma((D, pos - 1)), dma((D, pos - 1)), dma((D, pos - 1)), dma((D, pos - 1)),
            dma((D, pos)), dma((D, pos)),
            dma((nb - 1,)), dma((nb - 1,)), dma((nd - 1,)), dma((nd - 1,)),
            dma((nb - 1,)), dma((nb - 1,)), dma((nd - 1,)), dma((nd - 1,)),
            dma((nb - 1,)), dma((nb - 1,)),
        ]
    )
    return pl.pallas_call(
        functools.partial(backward_kernel, nb, nd, wunit, vunit),
        out_shape=(
            jax.ShapeDtypeStruct((D, kc, din), F32),
            jax.ShapeDtypeStruct((3, wunit * nd, whalf), BF16),
            jax.ShapeDtypeStruct((1, vunit * nd, din), BF16),
            jax.ShapeDtypeStruct((rq, dl), F32),
            jax.ShapeDtypeStruct((LAT, DQK), BF16),
            jax.ShapeDtypeStruct((8, 256), F32),
        ),
        in_specs=[anywhere] * 4 + [vmem] * 10,
        out_specs=(anywhere,) + (vmem,) * 5,
        scratch_shapes=scratch,
        compiler_params=pltpu.CompilerParams(
            collective_id=1, has_side_effects=True, vmem_limit_bytes=62 * 2**20
        ),
        name="backward",
    )(
        byte_embed, keys, values, wgrads, bias, gain_bytes.reshape(1, -1), w_key, w_value,
        queries, lse, ga, delta, direct, gain_part,
    )


def body(
    byte_embed,
    doc_lengths,
    key_mask,
    latents,
    gain_query,
    gain_bytes,
    gain_mlp,
    w_query,
    w_key,
    w_value,
    w_out,
    w_up,
    w_down,
    cotangent,
):
    nb, nd = lax.axis_size("blk"), lax.axis_size("doc")
    blk = lax.axis_index("blk")
    key_count, din = byte_embed.shape[1:]
    dl = latents.shape[1]
    positions = blk * key_count + jnp.arange(key_count, dtype=jnp.int32)
    usable = (positions[None, :] < doc_lengths[:, None]) & (key_mask == 1)
    bias = jnp.where(usable, 0.0, masked_score).astype(F32)
    attended, lse, keys, values, norm_cols, queries = forward(
        nb, byte_embed, bias, latents, gain_query, gain_bytes, w_query, w_key, w_value
    )
    latents_out, ga, delta, wgrads, direct, gain_part = mlp(
        nb, nd, attended, latents, gain_mlp, w_out, w_up, w_down, cotangent
    )
    byte_grad, wsum, vsum, direct_sum, gq, gains = backward(
        nb, nd, byte_embed, keys, values, wgrads, bias, gain_bytes, w_key, w_value, queries, lse,
        ga, delta, direct, gain_part,
    )

    def unfold(shard, rows):
        return jnp.concatenate([shard[:rows], shard[rows : 2 * rows]], axis=1).astype(F32)

    step = dl // nb
    grad_w_down, grad_w_up, grad_w_out = (unfold(wsum[m], step) for m in range(3))
    grad_kv = unfold(vsum[0], din // nb)
    grad_w_value, grad_w_key = grad_kv[:, :DV], grad_kv[:, DV:]
    gains = gains.reshape(-1)
    gain_mlp_grad = lax.dynamic_slice(gains[:dl], (blk * step,), (step,))
    gain_bytes_grad = lax.dynamic_slice(gains[dl:], (blk * (din // nb),), (din // nb,))
    skip = blk * step - jnp.minimum(blk * step // 128 * 128, dl - 256)
    cols = lax.dynamic_slice(norm_cols, (0, skip), (LAT, step))
    grad_w_query = lax.dot_general(
        cols, gq, (((0,), (0,)), ((), ())), preferred_element_type=F32
    )
    wq_rows = lax.dynamic_slice(w_query, (blk * step, 0), (step, DQK))
    dy_cols = dot_nt(gq, wq_rows)
    gain_rows = lax.dynamic_slice(gain_query, (blk * step,), (step,))
    gain_query_grad = jnp.sum(dy_cols * cols.astype(F32), axis=0) / gain_rows
    own = lax.dynamic_slice(gq, (blk * latents.shape[0], 0), (latents.shape[0], DQK))
    dxh = dot_nt(own, w_query) * gain_query
    xh, inv = norm_parts(latents)
    latents_grad = direct_sum + inv * (
        dxh
        - jnp.mean(dxh, axis=-1, keepdims=True)
        - xh * jnp.mean(dxh * xh, axis=-1, keepdims=True)
    )
    return (
        latents_out,
        byte_grad,
        latents_grad,
        gain_query_grad,
        gain_bytes_grad,
        gain_mlp_grad,
        grad_w_query,
        grad_w_key,
        grad_w_value,
        grad_w_out,
        grad_w_up,
        grad_w_down,
    )


def solution(mesh):
    in_specs = (
        P("doc", "blk", None),
        P("doc"),
        P("doc", "blk"),
        P("blk", None),
        P(),
        P(),
        P(),
        P(),
        P(),
        P(),
        P(),
        P(),
        P(),
        P("doc", "blk", None),
    )
    out_specs = (
        P("doc", "blk", None),
        P("doc", "blk", None),
        P("blk", None),
        P("blk"),
        P("blk"),
        P("blk"),
        P("blk", None),
        P("blk", None),
        P("blk", None),
        P("blk", None),
        P("blk", None),
        P("blk", None),
    )
    return jax.shard_map(body, mesh=mesh, in_specs=in_specs, out_specs=out_specs, check_vma=False)
```

time: 591 us -> 264 us (0.45)
  waiting for transfers between devices: 174 us -> 0 us
  Pallas kernels: 122 us -> 237 us
  matrix products: 94 us -> 4.15 us
  blocking collectives: 84 us -> 0 us
  local copies, waits for them, and re-layouts: 44.8 us -> 10.3 us
  other arithmetic: 38 us -> 7.73 us
  between operations: 16.2 us -> 0.77 us
  starting transfers between devices: 9.63 us -> 0 us
    pallas_call x0 -> x2, Pallas kernels: none -> 149 us  [the longest x1 132 us: backward(): pl.pallas_call(functools.partial(backward_kernel, nb, nd, wunit, vunit),...]
    reduce_scatter x6 -> x0, waiting for transfers between devices: 124 us -> none  [the longest x1 42.4 us: body(): lax.psum_scatter(sum_out.astype(jnp.bfloat16), 'blk', scatter_dimension=0...]
    dot_general x20 -> x3, matrix products: 94 us -> 4.15 us  [the longest x2 2.3 us: dot_nt(): lax.dot_general(a, b, (((1,), (1,)), ((), ())), preferred_element_type=F32)]
    psum x1 -> x0, waiting for transfers between devices: 40.6 us -> none  [body(): lax.psum(direct.astype(jnp.bfloat16), 'doc').astype(jnp.float32)]
    psum x2 -> x0, blocking collectives: 35.6 us -> none  [the longest x1 18.7 us: body(): lax.psum(grad_gain_query.astype(jnp.bfloat16), 'doc').astype(jnp.float32)]
    pallas_call x1, Pallas kernels: 122 us -> 87.9 us  [forward(): pl.pallas_call(functools.partial(forward_kernel, nb), out_shape=(jax.Shap...]
    unnamed x1 -> x0, blocking collectives: 26.5 us -> none
    all_gather x1 -> x0, blocking collectives: 21.8 us -> none  [body(): lax.all_gather(grad_totals, 'blk', axis=1, tiled=True).transpose(0, 2, 1)]
  transfers between devices with their start and end apart: 9 -> 0, of which waited for: 6 -> 0; matrix products, arithmetic and copies ran while one was open for 19% -> 0% of each run, Pallas kernels for 0% -> 0%
where the time goes in v2:
time: 264 us; the launch traced here: 260 us
  Pallas kernels  237 us (90%)
  local copies, waits for them, and re-layouts  10.3 us (4%)
  other arithmetic  7.73 us (3%)
  matrix products  4.15 us (2%)
    pallas_call x1, Pallas kernels, backward(): pl.pallas_call(functools.partial(backward_kernel, nb, nd, wunit, vunit),...  132 us
    pallas_call x1, Pallas kernels, forward(): pl.pallas_call(functools.partial(forward_kernel, nb), out_shape=(jax.Shap...  87.9 us
    pallas_call x1, Pallas kernels, mlp(): pl.pallas_call(functools.partial(mlp_kernel, nb, half), out_shape=(jax.Sh...  17.2 us

profile of v2, /device:TPU:0, one launch (start us, length us, event | category | flops | bytes accessed | tf_op | source)
XLA Modules:
  0.0 260.4 jit_solution(16979349815952888976)
XLA Ops:
  0.6 0.0 copy-start.6
  0.7 1.4 and_select_fusion.bias_ref.refs_4_
  2.0 1.3 reshape.71.gq_ref
  3.3 1.3 reshape.72.gb_ref.refs_5_
  4.6 87.9 %forward.1 = (f32[8,32,1280]{2,1,0:T(8,128)}, f32[8,8,256]{2,1,0:T(8,128)}, bf16[8,256,256]{2,1,0:T(8,128)(2,1)}, bf16[8,256,1280]{2,1,0:T(8,128)(2,1)}, bf16[25...) custom-call(bf16[8,256,768]{2,1,0:T(8,128)(2,1)} %refs_0_.1, f32[8,256]{1,0:T(8,128)} %and_select_fusion.bias_ref.refs_4_, ...), custom_call_target="tpu_custom_call" | custom-call | tf_op jit(solution)/shard_map/forward/pallas_call | solution.py:321
  92.5 0.0 copy-done.6
  92.5 0.6 reshape.73.gm_ref
  93.1 17.2 %feed_forward.1 = (f32[8,32,1280]{2,1,0:T(8,128)}, bf16[8,32,1280]{2,1,0:T(8,128)(2,1)}, f32[32,128]{1,0:T(8,128)}, bf16[3,8,320,640]{3,2,1,0:T(8,128)(2,1)}, bf...) custom-call(f32[8,32,1280]{2,1,0:T(8,128)} %get-tuple-element.30.att_ref, f32[32,1280]{1,0:T(8,128)} %lat_ref.3, ...), custom_call_target="tpu_custom_call" | custom-call | tf_op jit(solution)/shard_map/feed_forward/pallas_call | solution.py:452
  110.3 0.0 copy-start.1
  110.3 0.0 copy-start.2
  110.4 0.0 copy-start.5
  110.4 0.0 copy-start.4
  110.4 132.2 %backward.1 = (f32[8,256,768]{2,1,0:T(8,128)}, bf16[3,320,640]{2,1,0:T(8,128)(2,1)}, bf16[1,192,768]{2,1,0:T(8,128)(2,1)}, f32[32,1280]{1,0:T(8,128)}, bf16[256,256]{1,0:T(8,128)(2,1)}, /*index=5*/f32[8,256]{1,0:T(8,128)}) custom-call(bf16[8,256,768]{2,1,0:T(8,128)(2,1)} %refs_0_.1, bf16[8,256,256]{2,1,0:T(8,128)(2,1)} %get-tuple-element.32.refs_1_, ...), custom_call_target="tpu_custom_call" | custom-call | tf_op jit(solution)/shard_map/backward/pallas_call | solution.py:1074
  242.6 0.0 copy-start.3
  242.6 0.0 copy-done.1
  242.6 0.1 reduce_sum.45
  242.8 0.2 multiply_reduce_fusion.1
  243.0 0.0 copy-done.2
  243.0 0.0 copy-done.5
  243.0 1.2 fusion.9
  244.2 1.7 multiply_add_fusion
  245.9 0.0 copy-done.4
  245.9 1.1 fusion
  247.0 0.7 dynamic-slice_divide_fusion
  247.7 0.7 slice.75
  248.4 0.6 dynamic_slice.22
  249.0 0.7 slice.78
  249.7 0.6 dynamic_slice.23
  250.3 1.9 fusion.2
  252.2 1.0 slice_bitcast_fusion.7
  253.2 0.6 maximum_convert_fusion.3
  253.8 0.0 copy-start
  253.8 0.8 fusion.1
  254.6 0.0 copy-done.3
  254.6 0.1 slice_bitcast_fusion.1
  254.7 1.3 maximum_convert_fusion
  256.0 0.9 maximum_convert_fusion.2
  256.9 0.7 copy-done
  257.7 2.7 %copy.29 = f32[8,256,768]{2,1,0:T(8,128)} copy(f32[8,256,768]{2,1,0:T(8,128)S(1)} %copy-done) | data formatting | bytes 12582912
  (5 shorter events, 0.0 us)
Async XLA Ops:
  0.6 91.8 %copy-start.6 = (f32[1280]{0:T(1024)S(1)}, f32[1280]{0:T(1024)}, u32[]{:S(2)}) copy-start(f32[1280]{0:T(1024)} %param.20) | copy-start | bytes 15364
  110.3 132.3 %copy-start.1 = (f32[32,1280]{1,0:T(8,128)S(1)}, f32[32,1280]{1,0:T(8,128)}, u32[]{:S(2)}) copy-start(f32[32,1280]{1,0:T(8,128)} %lat_ref.3) | copy-start | bytes 491524
  110.3 132.6 %copy-start.2 = (bf16[1280,256]{1,0:T(8,128)(2,1)S(1)}, bf16[1280,256]{1,0:T(8,128)(2,1)}, u32[]{:S(2)}) copy-start(bf16[1280,256]{1,0:T(8,128)(2,1)} %wq_ref.1) | copy-start | bytes 1966084
  110.4 132.6 %copy-start.5 = (f32[1280]{0:T(1024)S(1)}, f32[1280]{0:T(1024)}, u32[]{:S(2)}) copy-start(f32[1280]{0:T(1024)} %param.18) | copy-start | bytes 15364
  110.4 135.5 %copy-start.4 = (bf16[256,256]{1,0:T(8,128)(2,1)S(1)}, bf16[256,256]{1,0:T(8,128)(2,1)}, u32[]{:S(2)}) copy-start(bf16[256,256]{1,0:T(8,128)(2,1)} %get-tuple-element.44) | copy-start | bytes 393220
  242.6 12.0 %copy-start.3 = (bf16[3,320,640]{2,1,0:T(8,128)(2,1)S(1)}, bf16[3,320,640]{2,1,0:T(8,128)(2,1)}, u32[]{:S(2)}) copy-start(bf16[3,320,640]{2,1,0:T(8,128)(2,1)} %get-tuple-element.47) | copy-start | bytes 3686404
  253.8 3.9 %copy-start = (f32[8,256,768]{2,1,0:T(8,128)S(1)}, f32[8,256,768]{2,1,0:T(8,128)}, u32[]{:S(2)}) copy-start(f32[8,256,768]{2,1,0:T(8,128)} %get-tuple-element.76) | copy-start | bytes 18874372

commit v3 on v2

--- a/solution.py
+++ b/solution.py
@@ -261,15 +261,17 @@
                 left_copy(n, j, part.at[n, c, j]).start()
 
     def finish(n):
-        att_ref[n] = part[n, c, p].astype(F32)
+        acc[0:rq, :] = part[n, c, p].astype(F32)
 
         @pl.when(p > 0)
         def _():
-            att_ref[n] += rin[n, p].astype(F32)
+            acc[0:rq, :] += rin[n, p].astype(F32)
 
         @pl.when(p < pos - 1)
         def _():
-            att_ref[n] += lin[n, p].astype(F32)
+            acc[0:rq, :] += lin[n, p].astype(F32)
+
+        att_ref[n] = acc[0:rq, :].astype(BF16)
 
     @pl.loop(0, D + pos - 1)
     def _(t):
@@ -321,7 +323,7 @@
     return pl.pallas_call(
         functools.partial(forward_kernel, nb),
         out_shape=(
-            jax.ShapeDtypeStruct((D, rq, DV), F32),
+            jax.ShapeDtypeStruct((D, rq, DV), BF16),
             jax.ShapeDtypeStruct((D, HEADS, LAT), F32),
             jax.ShapeDtypeStruct((D, kc, DQK), BF16),
             jax.ShapeDtypeStruct((D, kc, DV), BF16),
@@ -366,125 +368,26 @@
     return value, slope
 
 
-def mlp_kernel(
-    nb, half,
-    att_ref, lat_ref, gm_ref, wo_ref, wu_ref, wd_ref, cot_ref,
-    out_ref, ga_ref, delta_ref, wg_ref, direct_ref, gain_ref,
-    mid, xhat, slope, low_t, gmid,
-):
-    D, rq, dv = att_ref.shape
-    rows = D * rq
-    dl = lat_ref.shape[1]
-    step = dl // nb
-    blocks = dl // 256
-
-    def weight_grad(m, left, right_ref_cols):
-        low_t[...] = jnp.transpose(left)
-        for b in range(blocks):
-            r = dot_nn(low_t[...], right_ref_cols(b)).astype(BF16)
-            for i in range(2):
-                col = 256 * b + 128 * i
-                at, lane = col // half, col % half
-                for k in range(nb):
-                    wg_ref[m, k, at * step : (at + 1) * step, lane : lane + 128] = r[
-                        k * step : (k + 1) * step, 128 * i : 128 * (i + 1)
-                    ]
-
-    att = att_ref[...].reshape(rows, dv)
-    att_low = att.astype(BF16)
-    lat = lat_ref[...]
-    mid[...] = dot_nn(att_low, wo_ref[...]) + jnp.concatenate([lat] * D, axis=0)
-    xh, inv = norm_parts(mid[...])
-    xhat[...] = xh
-    nm = (xh * gm_ref[...]).astype(BF16)
-    up = dot_nn(nm, wu_ref[...])
-    act, sl = gelu_parts(up)
-    slope[...] = sl
-    act_low = act.astype(BF16)
-    out_ref[...] = (mid[...] + dot_nn(act_low, wd_ref[...])).reshape(D, rq, dl)
-    cot = cot_ref[...].reshape(rows, dl)
-    gm = cot.astype(BF16)
-    weight_grad(0, act_low, lambda b: gm[:, 256 * b : 256 * (b + 1)])
-    g_up = (dot_nt(gm, wd_ref[...]) * slope[...]).astype(BF16)
-    weight_grad(1, nm, lambda b: g_up[:, 256 * b : 256 * (b + 1)])
-    g_nm = dot_nt(g_up, wu_ref[...])
-    xh = xhat[...]
-    gain_ref[...] = jnp.sum(g_nm * xh, axis=0, keepdims=True)
-    dxh = g_nm * gm_ref[...]
-    dmid = inv * (
-        dxh
-        - jnp.mean(dxh, axis=-1, keepdims=True)
-        - xh * jnp.mean(dxh * xh, axis=-1, keepdims=True)
-    )
-    gmid[...] = cot + dmid
-    direct = gmid[0:rq, :]
-    for n in range(1, D):
-        direct = direct + gmid[n * rq : (n + 1) * rq, :]
-    direct_ref[...] = direct.astype(BF16)
-    gb = gmid[...].astype(BF16)
-    weight_grad(2, att_low, lambda b: gb[:, 256 * b : 256 * (b + 1)])
-    ga = dot_nt(gb, wo_ref[...])
-    ga_ref[...] = ga.astype(BF16).reshape(D, rq, dv)
-    prod = ga * att
-    lane = lax.broadcasted_iota(jnp.int32, (rq, 128), 1)
-    delta = jnp.zeros((rq, 128), F32)
-    for h in range(HEADS):
-        cols = lax.broadcasted_iota(jnp.int32, (rows, 256), 1) + window(h)
-        keep = (cols >= V_HEAD * h) & (cols < V_HEAD * (h + 1))
-        one = jnp.sum(
-            jnp.where(keep, prod[:, window(h) : window(h) + 256], 0.0), axis=1, keepdims=True
-        )
-        for n in range(D):
-            delta = delta + jnp.where(lane == n * HEADS + h, one[n * rq : (n + 1) * rq], 0.0)
-    delta_ref[...] = delta
-
-
 def owner_rows(total, docs):
     return -(-total // (16 * docs)) * 16
 
 
-def mlp(nb, nd, att, latents, gain_mlp, w_out, w_up, w_down, cotangent):
-    D, rq, dv = att.shape
-    dl = latents.shape[1]
-    half = dl // 2
-    rows = owner_rows(2 * dl // nb, nd) * nd
-    vmem = pl.BlockSpec(memory_space=pltpu.VMEM)
-    return pl.pallas_call(
-        functools.partial(mlp_kernel, nb, half),
-        out_shape=(
-            jax.ShapeDtypeStruct((D, rq, dl), F32),
-            jax.ShapeDtypeStruct((D, rq, dv), BF16),
-            jax.ShapeDtypeStruct((rq, 128), F32),
-            jax.ShapeDtypeStruct((3, nb, rows, half), BF16),
-            jax.ShapeDtypeStruct((rq, dl), BF16),
-            jax.ShapeDtypeStruct((1, dl), F32),
-        ),
-        in_specs=[vmem] * 7,
-        out_specs=(vmem,) * 6,
-        scratch_shapes=[
-            pltpu.VMEM((D * rq, dl), F32),
-            pltpu.VMEM((D * rq, dl), F32),
-            pltpu.VMEM((D * rq, dl), F32),
-            pltpu.VMEM((dl, D * rq), BF16),
-            pltpu.VMEM((D * rq, dl), F32),
-        ],
-        compiler_params=pltpu.CompilerParams(vmem_limit_bytes=60 * 2**20),
-        name="feed_forward",
-    )(att, latents, gain_mlp.reshape(1, -1), w_out, w_up, w_down, cotangent)
-
-
 class ShardSums:
-    def __init__(self, doc, blk, nd, nb, count, unit, own, mate_in, inbox, rin, lin, out, sems):
+    def __init__(
+        self, doc, blk, nd, nb, count, unit, group, lags,
+        own, mate_in, inbox, rin, lin, out, sems,
+    ):
         self.doc, self.p, self.c = doc, blk // 2, blk % 2
         self.nd, self.pos, self.count, self.unit = nd, nb // 2, count, unit
         self.bits = nd.bit_length() - 1
         self.own, self.mate_in, self.inbox = own, mate_in, inbox
         self.rin, self.lin, self.out = rin, lin, out
         (
-            self.mate_s, self.mate_r, self.own_s, self.in_s, self.in_r,
+            self.mate_s, self.mate_r, self.in_s, self.in_r,
             self.right_s, self.right_r, self.left_s, self.left_r, self.out_s, self.out_r,
         ) = sems
-        self.lag = self.bits + self.pos - 1
+        self.group, self.lags = group, lags
+        self.steps = count // group + lags[-1] + self.pos - 1
 
     def weight(self, s, k):
         b = (s + k) % self.bits
@@ -557,11 +460,12 @@
             self.own[s, rows, :].astype(F32) + other.astype(F32)
         ).astype(BF16)
 
-    def begin(self, s, mate_copy, own_copy):
-        own_copy(s).wait()
+    def begin(self, s, mate_copy):
         mate_copy(s).wait_recv()
-        for q in range(self.nd):
-            self.add(s, q, self.mate_in[s, self.unit * q : self.unit * (q + 1), :])
+        rows = self.mate_in.shape[1]
+        self.own[s, 0:rows, :] = (
+            self.own[s, 0:rows, :].astype(F32) + self.mate_in[s].astype(F32)
+        ).astype(BF16)
         for i in range(self.width(0)):
             self.halving(s, 0, i).start()
 
@@ -624,21 +528,22 @@
             for i in range(1, self.nd):
                 self.share(m, i).start()
 
-    def step(self, t, mate_copy, own_copy):
-        def at(s, when, run):
-            @pl.when((s >= 0) & (s < self.count) & when)
-            def _():
-                run(s)
-
-        at(t, True, lambda s: self.begin(s, mate_copy, own_copy))
+    def step(self, t, mate_copy, entered=0):
+        def at(t, when, run, turned=False):
+            @pl.when((t >= 0) & (t < self.count // self.group) & when)
+            def _():
+                for i in range(self.group):
+                    run(t * self.group + (self.group - 1 - i if turned else i))
+
+        at(t, t >= entered, lambda s: self.begin(s, mate_copy))
         for k in range(1, self.bits + 1):
-            at(t - k, True, functools.partial(self.halve, k=k))
-        base = t - self.bits
-        at(base - self.p, self.p > 0, self.from_left)
+            at(t - self.lags[k - 1], True, functools.partial(self.halve, k=k))
+        base = t - self.lags[-1]
+        at(base - self.p, self.p > 0, self.from_left, True)
         at(base - (self.pos - 1 - self.p), self.p < self.pos - 1, self.from_right)
         at(base - (self.pos - 1), True, self.finish)
 
-    def drain(self, mate_copy):
+    def drain(self):
         for m in range(self.count // self.pos):
             for i in range(1, self.nd):
                 self.shared(m, i).wait_recv()
@@ -646,7 +551,6 @@
 
         @pl.loop(0, self.count)
         def _(s):
-            mate_copy(s).wait_send()
             for k in range(self.bits):
                 for i in range(self.width(k)):
                     self.halving(s, k, i).wait_send()
@@ -661,16 +565,16 @@
                 self.left(s).wait_send()
 
 
-def shard_sum_scratch(nd, nb, count, unit, width):
+def shard_sum_scratch(nd, nb, count, unit, rows, width):
     dma = pltpu.SemaphoreType.DMA
     arrays = count // (nb // 2)
     return [
         pltpu.VMEM((count, unit * nd, width), BF16),
-        pltpu.VMEM((count, unit * nd, width), BF16),
+        pltpu.VMEM((count, rows, width), BF16),
         pltpu.VMEM((count, nd - 1, unit, width), BF16),
         pltpu.VMEM((count, unit, width), BF16),
         pltpu.VMEM((count, unit, width), BF16),
-        dma((count,)), dma((count,)), dma((count,)),
+        dma((count,)), dma((count,)),
         dma((count, nd - 1)), dma((count, nd - 1)),
         dma((count,)), dma((count,)), dma((count,)), dma((count,)),
         dma((arrays, nd - 1)), dma((arrays, nd - 1)),
@@ -679,20 +583,24 @@
 
 def backward_kernel(nb, nd, wunit, vunit, *refs):
     (
-        x_hbm, k_hbm, v_hbm, wg_hbm, bias_ref, gb_ref, wk_ref, wv_ref, qall_ref, lse_ref,
-        ga_ref, delta_ref, direct_ref, gain_ref,
-    ) = refs[:14]
-    bg_hbm, wsum_ref, vsum_ref, dsum_ref, gq_ref, gains_ref = refs[14:20]
-    wscr, vscr = refs[20:36], refs[36:52]
+        x_hbm, k_hbm, v_hbm, wo_hbm, wu_hbm, wd_hbm, wk_hbm, wv_hbm, cot_hbm,
+        att_ref, lat_ref, gm_ref, bias_ref, gb_ref, qall_ref, lse_ref,
+    ) = refs[:16]
+    out_hbm, bg_hbm, wsum_ref, vsum0_ref, vsum1_ref, dsum_ref, gq_ref, gains_ref = refs[16:24]
+    wscr, vscr = refs[24:39], (refs[39:54], refs[54:69])
     (
-        x_ref, k_ref, v_ref, ga_all, delta_all, delta_t, qm, ds_all, gv_acc, gq_acc,
-        kv_acc, kv_part, gain_acc, bg_buf, dir_in, misc_out, misc_in, misc2_out, misc2_in, gq_own,
-        load_s, bg_s, ar_s, ar_r, al_s, al_r, am_s, am_r, d_s, d_r, dir_s, dir_r,
+        wpool, x_ref, k_ref, ga_all, delta_all, delta_t, qm, wkv, ds_all, gv_acc, gq_acc,
+        fpool, frames, low_t, right, stage, vstage, gain_acc, gmlp_acc, direct_out, dir_in,
+        misc_out, misc_in, misc2_out, misc2_in,
+        load_s, out_s, bg_s, ar_s, ar_r, al_s, al_r, am_s, am_r, d_s, d_r, dir_s, dir_r,
         m1_s, m1_r, m2_s, m2_r, m3_s, m3_r,
-    ) = refs[52:]
+    ) = refs[69:]
     D, kc, din = x_ref.shape
-    rq = ga_ref.shape[1]
+    rq, dl = lat_ref.shape
+    rows_all = D * rq
     pos = nb // 2
+    hh, vh, qh = HEADS // 2, DV // 2, DQK // 2
+    bits = nd.bit_length() - 1
     doc, blk = lax.axis_index("doc"), lax.axis_index("blk")
     p, c = blk // 2, blk % 2
     mate = 2 * p + 1 - c
@@ -707,60 +615,78 @@
             barrier, inc=1, device_id=(lax.rem(doc + i, nd), blk), device_id_type=MESH
         )
 
-    loads = [
-        pltpu.make_async_copy(src, dst, load_s.at[i])
-        for i, (src, dst) in enumerate(((k_hbm, k_ref), (v_hbm, v_ref), (x_hbm, x_ref)))
+    def load(src, dst, i):
+        return pltpu.make_async_copy(src, dst, load_s.at[i])
+
+    slot0, slot1 = wpool.at[0:dl, :], wpool.at[dl : 2 * dl, :]
+    load_out, load_up = load(wo_hbm, slot0, 0), load(wu_hbm, slot1, 1)
+    load_down, load_out2 = load(wd_hbm, slot0, 2), load(wo_hbm, slot0, 3)
+    load_v = load(v_hbm, wpool.at[0 : D * kc, :], 4)
+    load_cot = load(cot_hbm, frames.at[1], 5)
+    later = [load(k_hbm, k_ref, 6), load(x_hbm, x_ref, 7)]
+    for g in range(2):
+        later.append(load(wv_hbm.at[:, g * vh : (g + 1) * vh], wkv.at[g, :, 0:vh], 8 + g))
+        later.append(
+            load(wk_hbm.at[:, g * qh : (g + 1) * qh], wkv.at[g, :, vh : vh + qh], 10 + g)
+        )
+    load_out.start()
+    load_up.start()
+    load_cot.start()
+
+    weights = ShardSums(
+        doc, blk, nd, nb, 3 * pos, wunit, 2, [3 + k for k in range(bits)],
+        *wscr[:5], wsum_ref, wscr[5:],
+    )
+    values = [
+        ShardSums(
+            doc, blk, nd, nb, pos, vunit, pos, lags, *vscr[g][:5], out, vscr[g][5:],
+        )
+        for g, (lags, out) in enumerate(
+            (
+                ([2 + k for k in range(bits)], vsum0_ref),
+                ([1 + k for k in range(bits)], vsum1_ref),
+            )
+        )
     ]
-    for load in loads:
-        load.start()
-
-    weights = ShardSums(
-        doc, blk, nd, nb, 3 * pos, wunit, *wscr[:5], wsum_ref, wscr[5:]
-    )
-    values = ShardSums(doc, blk, nd, nb, pos, vunit, *vscr[:5], vsum_ref, vscr[5:])
+
+    wrows, whalf = 2 * dl // nb, dl // 2
+    vhalf = (vh + qh) // 2
 
     def w_mate(s):
-        return remote(
-            wg_hbm.at[s // pos, 2 * (s % pos) + 1 - c], weights.mate_in.at[s],
+        rows = pl.ds(pl.multiple_of(s % (2 * pos) * wrows, wrows), wrows)
+        return remote(
+            stage.at[rows, 0:whalf], weights.mate_in.at[s],
             weights.mate_s.at[s], weights.mate_r.at[s], doc, mate,
         )
 
-    def w_own(s):
-        return pltpu.make_async_copy(
-            wg_hbm.at[s // pos, 2 * (s % pos) + c], weights.own.at[s], weights.own_s.at[s]
-        )
-
-    def v_mate(s):
-        return remote(
-            kv_part.at[2 * s + 1 - c], values.mate_in.at[s],
-            values.mate_s.at[s], values.mate_r.at[s], doc, mate,
-        )
-
-    def v_own(s):
-        return pltpu.make_async_copy(
-            kv_part.at[2 * s + c], values.own.at[s], values.own_s.at[s]
-        )
+    def v_mate(g):
+        return lambda s: remote(
+            vstage.at[g, s], values[g].mate_in.at[s],
+            values[g].mate_s.at[s], values[g].mate_r.at[s], doc, mate,
+        )
+
+    parts, ahead = 2 * D, 4
 
     def chunk(j, core):
         return pl.ds(pl.multiple_of((2 * j + core) * rq, rq), rq)
 
-    def right_copy(n, hop, j):
-        rows = ga_all.at[n, chunk(j, c), :]
-        return remote(
-            rows, rows, ar_s.at[n, hop], ar_r.at[n, hop],
+    def right_copy(e, hop, j):
+        rows = ga_all.at[e, chunk(j, c), :]
+        return remote(
+            rows, rows, ar_s.at[e, hop], ar_r.at[e, hop],
             doc, 2 * jnp.minimum(p + 1, pos - 1) + c,
         )
 
-    def left_copy(n, hop, j):
-        rows = ga_all.at[n, chunk(j, c), :]
-        return remote(
-            rows, rows, al_s.at[n, hop], al_r.at[n, hop],
+    def left_copy(e, hop, j):
+        rows = ga_all.at[e, chunk(j, c), :]
+        return remote(
+            rows, rows, al_s.at[e, hop], al_r.at[e, hop],
             doc, 2 * jnp.maximum(p - 1, 0) + c,
         )
 
-    def mate_copy(n, j, core):
-        rows = ga_all.at[n, chunk(j, core), :]
-        return remote(rows, rows, am_s.at[n, j], am_r.at[n, j], doc, mate)
+    def mate_copy(e, j, core):
+        rows = ga_all.at[e, chunk(j, core), :]
+        return remote(rows, rows, am_s.at[e, j], am_r.at[e, j], doc, mate)
 
     own_rows = pl.ds(pl.multiple_of(blk * rq, rq), rq)
 
@@ -772,117 +698,233 @@
 
     def direct_copy(i):
         return remote(
-            direct_ref, dir_in.at[i - 1], dir_s.at[i - 1], dir_r.at[i - 1],
+            direct_out, dir_in.at[i - 1], dir_s.at[i - 1], dir_r.at[i - 1],
             lax.rem(doc + i, nd), blk,
         )
 
+    def send_own(e):
+        @pl.when(p < pos - 1)
+        def _():
+            right_copy(e, 0, p).start()
+
+        @pl.when(p > 0)
+        def _():
+            left_copy(e, 0, p).start()
+
+        mate_copy(e, p, c).start()
+
+    mid = fpool.at[0:rows_all, :]
+    xhat = fpool.at[rows_all : 2 * rows_all, :]
+    slope = fpool.at[2 * rows_all : 3 * rows_all, :]
+    kv_acc = fpool.at[0:din, 0 : vh + qh]
+    step_w = dl // nb
+
+    def weight_grad(m, left):
+        low_t[...] = jnp.transpose(left)
+
+        @pl.loop(0, pos)
+        def _(j):
+            s = m * pos + j
+            for core in (1 - c, c):
+                rows = pl.ds(pl.multiple_of((2 * j + core) * step_w, step_w), step_w)
+                shard = dot_nn(low_t[rows, :], right[...]).astype(BF16)
+                for i in range(2):
+                    part = shard[:, i * whalf : (i + 1) * whalf]
+                    if core is c:
+                        weights.own[s, i * step_w : (i + 1) * step_w, :] = part
+                    else:
+                        at = pl.multiple_of(s % (2 * pos) * wrows, wrows) + i * step_w
+                        stage[pl.ds(pl.multiple_of(at, 16), step_w), 0:whalf] = part
+                if core is not c:
+                    w_mate(s).start()
+
+    att_low = att_ref[...].reshape(rows_all, DV)
+    load_out.wait()
+    mid[...] = dot_nn(att_low, slot0[...]) + jnp.concatenate([lat_ref[...]] * D, axis=0)
+    load_down.start()
+    xh, inv = norm_parts(mid[...])
+    xhat[...] = xh
+    nm = (xh * gm_ref[...]).astype(BF16)
+    load_up.wait()
+    act, sl = gelu_parts(dot_nn(nm, slot1[...]))
+    slope[...] = sl
+    act_low = act.astype(BF16)
+    load_cot.wait()
+    gm = frames[1].astype(BF16)
+    right[...] = gm
+    pl.semaphore_wait(barrier, nb - 1 + nd - 1)
+    weight_grad(0, act_low)
+    load_down.wait()
+    frames[0] = mid[...] + dot_nn(act_low, slot0[...])
+    store_out = pltpu.make_async_copy(frames.at[0], out_hbm, out_s)
+    store_out.start()
+    g_up = (dot_nt(gm, slot0[...]) * slope[...]).astype(BF16)
+    load_out2.start()
+    for item in later:
+        item.start()
+    for s in range(pos):
+        weights.begin(s, w_mate)
+    right[...] = g_up
+    weight_grad(1, nm)
+    g_nm = dot_nt(g_up, slot1[...])
+    gmlp_acc[...] = jnp.sum(g_nm * xhat[...], axis=0, keepdims=True)
+    dxh = g_nm * gm_ref[...]
+    mid[...] = frames[1] + inv * (
+        dxh
+        - jnp.mean(dxh, axis=-1, keepdims=True)
+        - xhat[...] * jnp.mean(dxh * xhat[...], axis=-1, keepdims=True)
+    )
+    gb = mid[...].astype(BF16)
+    right[...] = gb
+    load_out2.wait()
+    ga = dot_nt(gb, slot0[...])
+    load_v.start()
+    for g in range(2):
+        for n in range(D):
+            ga_all[g * D + n, own_rows, :] = ga[
+                n * rq : (n + 1) * rq, g * vh : (g + 1) * vh
+            ].astype(BF16)
+    for e in range(ahead):
+        send_own(e)
+    lane = lax.broadcasted_iota(jnp.int32, (rq, 128), 1)
+    delta = jnp.zeros((rq, 128), F32)
     for h in range(HEADS):
-        qm[h * LAT : (h + 1) * LAT, :] = qall_ref[...] * query_mask(h, LAT)
-    gq_acc[...] = jnp.zeros_like(gq_acc)
-    kv_acc[...] = jnp.zeros_like(kv_acc)
-    gain_acc[...] = jnp.zeros_like(gain_acc)
-    delta_all[own_rows, :] = delta_ref[...]
-    for n in range(D):
-        ga_all[n, own_rows, :] = ga_ref[n]
-
-    pl.semaphore_wait(barrier, nb - 1 + nd - 1)
+        cols = slice(window(h), window(h) + 256)
+        prod = ga[:, cols] * (att_low[:, cols] * value_mask(h, rows_all)).astype(F32)
+        one = jnp.sum(prod, axis=1, keepdims=True)
+        for n in range(D):
+            delta = delta + jnp.where(lane == n * HEADS + h, one[n * rq : (n + 1) * rq], 0.0)
+    delta_all[own_rows, :] = delta
     for i in range(1, nb):
         delta_copy(i, own_rows).start()
-
-    @pl.loop(0, D)
-    def _(n):
-        @pl.when(p < pos - 1)
-        def _():
-            right_copy(n, 0, p).start()
-
-        @pl.when(p > 0)
-        def _():
-            left_copy(n, 0, p).start()
-
-        mate_copy(n, p, c).start()
-
-    @pl.loop(0, weights.count)
-    def _(s):
-        w_own(s).start()
-        w_mate(s).start()
-
+    direct = mid[0:rq, :]
+    for n in range(1, D):
+        direct = direct + mid[n * rq : (n + 1) * rq, :]
+    direct_out[...] = direct.astype(BF16)
     for i in range(1, nd):
         direct_copy(i).start()
-
-    def forward_chunks(n, hop):
+    for s in range(pos):
+        w_mate(s).wait_send()
+    weight_grad(2, att_low)
+
+    for h in range(HEADS):
+        half = slice(h // hh * qh, h // hh * qh + qh)
+        qm[h] = (qall_ref[...] * query_mask(h, LAT))[:, half]
+    gq_acc[...] = jnp.zeros_like(gq_acc)
+    kv_acc[...] = jnp.zeros((din, vh + qh), F32)
+    gain_acc[...] = jnp.zeros_like(gain_acc)
+
+    def forward_chunks(e, hop):
         j = p - 1 - hop
 
         @pl.when(j >= 0)
         def _():
-            right_copy(n, hop, j).wait_recv()
+            right_copy(e, hop, j).wait_recv()
             if hop + 1 < pos - 1:
                 @pl.when(p < pos - 1)
                 def _():
-                    right_copy(n, hop + 1, j).start()
-
-            mate_copy(n, j, c).start()
+                    right_copy(e, hop + 1, j).start()
+
+            mate_copy(e, j, c).start()
 
         i = p + 1 + hop
 
         @pl.when(i < pos)
         def _():
-            left_copy(n, hop, i).wait_recv()
+            left_copy(e, hop, i).wait_recv()
             if hop + 1 < pos - 1:
                 @pl.when(p > 0)
                 def _():
-                    left_copy(n, hop + 1, i).start()
-
-            mate_copy(n, i, c).start()
-
-    def bytes_back(n):
+                    left_copy(e, hop + 1, i).start()
+
+            mate_copy(e, i, c).start()
+
+    def doc_rows(n):
+        return pl.ds(pl.multiple_of(n * kc, kc), kc)
+
+    def bytes_back(g, n):
+        e = g * D + n
         for j in range(pos):
-            mate_copy(n, j, 1 - c).wait_recv()
+            mate_copy(e, j, 1 - c).wait_recv()
         bias = wide(row_to_lanes(bias_ref[pl.ds(n, 1), :]), LAT)
         logs, deltas = lse_ref[n], delta_t[n]
-        kn = k_ref[n]
+        kn = k_ref[n, :, g * qh : (g + 1) * qh]
         kt = jnp.transpose(kn)
         gv_acc[...] = jnp.zeros_like(gv_acc)
-        for h in range(HEADS):
-            cols = slice(window(h), window(h) + 256)
-            gah = ga_all[n, :, cols] * value_mask(h, LAT)
-            s = dot_nt(kn, qm[h * LAT : (h + 1) * LAT, :]) * SCORE2 + bias
+        for i in range(hh):
+            h = g * hh + i
+            cols = slice(window(i), window(i) + 256)
+            vcols = slice(g * vh + window(i), g * vh + window(i) + 256)
+            gah = ga_all[e, :, cols] * value_mask(i, LAT)
+            s = dot_nt(kn, qm[h]) * SCORE2 + bias
             prob = jnp.exp2(s - logs[h : h + 1, :])
-            dprob = dot_nt(v_ref[n, :, cols], gah)
+            dprob = dot_nt(wpool[doc_rows(n), vcols], gah)
             ds = (prob * (dprob - deltas[h : h + 1, :])).astype(BF16)
-            ds_all[:, h * LAT : (h + 1) * LAT] = ds
+            ds_all[:, i * LAT : (i + 1) * LAT] = ds
             gv_acc[:, cols] += dot_nn(prob.astype(BF16), gah)
-            head = slice(QK_HEAD * h, QK_HEAD * (h + 1))
-            gq_acc[head, :] += dot_nn(kt[head, :], ds)
-        gk = (dot_nn(ds_all[...], qm[...]) * SCORE_SCALE).astype(BF16)
-        gv = gv_acc[...].astype(BF16)
-        gx = dot_nt(gv, wv_ref[...]) + dot_nt(gk, wk_ref[...])
+            head = slice(QK_HEAD * i, QK_HEAD * (i + 1))
+            rows = slice(QK_HEAD * h, QK_HEAD * (h + 1))
+            gq_acc[rows, :] += dot_nn(kt[head, :], ds)
+        gk = dot_nn(ds_all[:, 0:LAT], qm[g * hh])
+        for i in range(1, hh):
+            gk = gk + dot_nn(ds_all[:, i * LAT : (i + 1) * LAT], qm[g * hh + i])
+        grads_now = jnp.concatenate(
+            [gv_acc[...].astype(BF16), (gk * SCORE_SCALE).astype(BF16)], axis=1
+        )
         xh, inv = norm_parts(x_ref[n].astype(F32))
-        gain_acc[...] += jnp.sum(gx * xh, axis=0, keepdims=True)
-        dxh = gx * gb_ref[...]
-        slot = lax.rem(n, 2)
-
-        @pl.when(n >= 2)
-        def _():
-            pltpu.make_async_copy(bg_buf.at[slot], bg_hbm.at[n - 2], bg_s.at[slot]).wait()
-
-        bg_buf[slot] = inv * (
-            dxh
-            - jnp.mean(dxh, axis=-1, keepdims=True)
-            - xh * jnp.mean(dxh * xh, axis=-1, keepdims=True)
-        )
-        pltpu.make_async_copy(bg_buf.at[slot], bg_hbm.at[n], bg_s.at[slot]).start()
+        kept = stage.at[doc_rows(n), 0 : vh + qh]
+        if g == 0:
+            kept[...] = grads_now
+        else:
+            gx = dot_nt(kept[...], wkv[0]) + dot_nt(grads_now, wkv[1])
+            gain_acc[...] += jnp.sum(gx * xh, axis=0, keepdims=True)
+            dxh = gx * gb_ref[...]
+            slot = lax.rem(n, 2)
+
+            @pl.when(n >= 2)
+            def _():
+                pltpu.make_async_copy(frames.at[slot, 0:kc, 0:din], bg_hbm.at[n - 2], bg_s.at[slot]).wait()
+
+            frames[slot, 0:kc, 0:din] = inv * (
+                dxh
+                - jnp.mean(dxh, axis=-1, keepdims=True)
+                - xh * jnp.mean(dxh * xh, axis=-1, keepdims=True)
+            )
+            pltpu.make_async_copy(frames.at[slot, 0:kc, 0:din], bg_hbm.at[n], bg_s.at[slot]).start()
         normed_t = jnp.transpose((xh * gb_ref[...]).astype(BF16))
-        kv_acc[:, 0:DV] += dot_nn(normed_t, gv)
-        kv_acc[:, DV : DV + DQK] += dot_nn(normed_t, gk)
-
-    @pl.loop(0, D + pos)
+        kv_acc[...] += dot_nn(normed_t, grads_now)
+
+    def cut_values(g):
+        step = din // nb
+        for s in range(pos):
+            for core in (1 - c, c):
+                rows = pl.ds(pl.multiple_of((2 * s + core) * step, step), step)
+                to = values[g].own if core is c else vstage.at[g]
+                for i in range(2):
+                    to[s, i * step : (i + 1) * step, :] = fpool[
+                        rows, i * vhalf : (i + 1) * vhalf
+                    ].astype(BF16)
+            v_mate(g)(s).start()
+        if g == 0:
+            kv_acc[...] = jnp.zeros((din, vh + qh), F32)
+
+    start0 = (pos + D + 2) // 2
+
+    @pl.loop(0, parts + pos)
     def _(t):
+        @pl.when(t < parts - ahead)
+        def _():
+            send_own(t + ahead)
+
         for hop in range(pos - 1):
-            @pl.when((t >= hop) & (t - hop < D))
+            @pl.when((t >= hop) & (t - hop < parts))
             def _():
                 forward_chunks(t - hop, hop)
 
-        weights.step(t, w_mate, w_own)
+        @pl.when(t % 2 == 0)
+        def _():
+            weights.step(t // 2 + 2, w_mate, pos // 2)
+            values[0].step(t // 2 - start0, v_mate(0))
 
         @pl.when(t == pos)
         def _():
@@ -892,15 +934,29 @@
             turned = jnp.transpose(delta_all[...])
             for n in range(D):
                 delta_t[n] = turned[n * HEADS : (n + 1) * HEADS, :]
-            for load in loads:
-                load.wait()
-
-        @pl.when(t >= pos)
-        def _():
-            bytes_back(t - pos)
+            for item in later:
+                item.wait()
+            load_v.wait()
+            store_out.wait()
+            for s in range(pos, 3 * pos):
+                w_mate(s).wait_send()
+
+        @pl.when((t >= pos) & (t < pos + D))
+        def _():
+            bytes_back(0, t - pos)
+
+        @pl.when(t == pos + D)
+        def _():
+            cut_values(0)
+
+        @pl.when(t >= pos + D)
+        def _():
+            bytes_back(1, t - pos - D)
+
+    cut_values(1)
 
     gq_rows = (jnp.transpose(gq_acc[...]) * SCORE_SCALE).astype(BF16)
-    gains = jnp.concatenate([gain_ref[...], gain_acc[...]], axis=1)
+    gains = jnp.concatenate([gmlp_acc[...], gain_acc[...]], axis=1)
     rows8 = [gains[:, 256 * i : 256 * (i + 1)] for i in range(8)]
     gains8 = jnp.concatenate(rows8 + [jnp.zeros((8, 256), F32)], axis=0).astype(BF16)
     for j in range(nb):
@@ -913,53 +969,44 @@
             misc_out.at[peer], misc_in.at[slot], m1_s.at[i - 1], m1_r.at[i - 1], doc, peer
         )
 
+    def misc2(i, slot):
+        return remote(
+            misc2_out, misc2_in.at[slot], m2_s.at[i - 1], m2_r.at[i - 1],
+            lax.rem(doc + i, nd), blk,
+        )
+
+    def misc3(i, rows):
+        return remote(
+            gq_ref.at[rows, :], gq_ref.at[rows, :], m3_s.at[i - 1], m3_r.at[i - 1],
+            doc, lax.rem(blk + i, nb),
+        )
+
     for i in range(1, nb):
         misc1(i, blk).start()
-
-    step = din // nb
-    for k in range(nb):
-        rows = slice(k * step, (k + 1) * step)
-        kv_part[k, 0:step, :] = kv_acc[rows, 0:din].astype(BF16)
-        kv_part[k, step : 2 * step, :] = kv_acc[rows, din : 2 * din].astype(BF16)
-
-    @pl.loop(0, values.count)
-    def _(s):
-        v_own(s).start()
-        v_mate(s).start()
-
     misc_in[blk] = misc_out[blk]
-    for i in range(1, nb):
-        misc1(i, lax.rem(blk + nb - i, nb)).wait_recv()
-    total = misc_in[0].astype(F32)
-    for i in range(1, nb):
-        total = total + misc_in[i].astype(F32)
-    misc2_out[...] = total.astype(BF16)
-
-    def misc2(i, slot):
-        return remote(
-            misc2_out, misc2_in.at[slot], m2_s.at[i - 1], m2_r.at[i - 1],
-            lax.rem(doc + i, nd), blk,
-        )
-
-    for i in range(1, nd):
-        misc2(i, doc).start()
-    misc2_in[doc] = misc2_out[...]
-
-    first, last = D + pos, weights.count + weights.lag
-    last = max(last, first + values.count + values.lag)
-
-    def misc3(i, rows):
-        return remote(
-            gq_ref.at[rows, :], gq_ref.at[rows, :], m3_s.at[i - 1], m3_r.at[i - 1],
-            doc, lax.rem(blk + i, nb),
-        )
+
+    first = (parts + pos + 1) // 2
+    last = max(weights.steps - 2, start0 + values[0].steps, first + values[1].steps)
 
     @pl.loop(first, last)
     def _(t):
-        weights.step(t, w_mate, w_own)
-        values.step(t - first, v_mate, v_own)
-
-        @pl.when(t == first + 2)
+        values[1].step(t - first, v_mate(1))
+        values[0].step(t - start0, v_mate(0))
+        weights.step(t + 2, w_mate, pos // 2)
+
+        @pl.when(t == first + 1)
+        def _():
+            for i in range(1, nb):
+                misc1(i, lax.rem(blk + nb - i, nb)).wait_recv()
+            total = misc_in[0].astype(F32)
+            for i in range(1, nb):
+                total = total + misc_in[i].astype(F32)
+            misc2_out[...] = total.astype(BF16)
+            for i in range(1, nd):
+                misc2(i, doc).start()
+            misc2_in[doc] = misc2_out[...]
+
+        @pl.when(t == first + 3)
         def _():
             for i in range(1, nd):
                 misc2(i, lax.rem(doc + nd - i, nd)).wait_recv()
@@ -975,16 +1022,19 @@
         src = lax.rem(blk + nb - i, nb)
         misc3(i, pl.ds(pl.multiple_of(src * rq, rq), rq)).wait_recv()
 
-    total = direct_ref[...].astype(F32)
+    total = direct_out[...].astype(F32)
     for i in range(1, nd):
         direct_copy(i).wait_recv()
         total = total + dir_in[i - 1].astype(F32)
     dsum_ref[...] = total
 
     for n in range(D - 2, D):
-        pltpu.make_async_copy(bg_buf.at[n % 2], bg_hbm.at[n], bg_s.at[n % 2]).wait()
-    weights.drain(w_mate)
-    values.drain(v_mate)
+        pltpu.make_async_copy(frames.at[n % 2, 0:kc, 0:din], bg_hbm.at[n], bg_s.at[n % 2]).wait()
+    weights.drain()
+    for g in range(2):
+        values[g].drain()
+        for s in range(pos):
+            v_mate(g)(s).wait_send()
     for i in range(1, nb):
         delta_copy(i, own_rows).wait_send()
         misc1(i, blk).wait_send()
@@ -993,79 +1043,87 @@
         direct_copy(i).wait_send()
         misc2(i, doc).wait_send()
 
-    @pl.loop(0, D)
-    def _(n):
-        mate_copy(n, p, c).wait_send()
+    @pl.loop(0, parts)
+    def _(e):
+        mate_copy(e, p, c).wait_send()
 
         @pl.when(p < pos - 1)
         def _():
-            right_copy(n, 0, p).wait_send()
+            right_copy(e, 0, p).wait_send()
 
         @pl.when(p > 0)
         def _():
-            left_copy(n, 0, p).wait_send()
+            left_copy(e, 0, p).wait_send()
 
         for hop in range(pos - 1):
             j = p - 1 - hop
 
             @pl.when(j >= 0)
             def _():
-                mate_copy(n, j, c).wait_send()
+                mate_copy(e, j, c).wait_send()
                 if hop + 1 < pos - 1:
                     @pl.when(p < pos - 1)
                     def _():
-                        right_copy(n, hop + 1, j).wait_send()
+                        right_copy(e, hop + 1, j).wait_send()
 
             i = p + 1 + hop
 
             @pl.when(i < pos)
             def _():
-                mate_copy(n, i, c).wait_send()
+                mate_copy(e, i, c).wait_send()
                 if hop + 1 < pos - 1:
                     @pl.when(p > 0)
                     def _():
-                        left_copy(n, hop + 1, i).wait_send()
+                        left_copy(e, hop + 1, i).wait_send()
 
 
 def backward(
-    nb, nd, byte_embed, keys, values, wgrads, bias, gain_bytes, w_key, w_value, queries, lse,
-    ga, delta, direct, gain_part,
+    nb, nd, byte_embed, keys, values, w_out, w_up, w_down, w_key, w_value, cotangent,
+    attended, latents, gain_mlp, bias, gain_bytes, queries, lse,
 ):
     D, kc, din = byte_embed.shape
-    rq, dl = direct.shape
+    rq, dl = latents.shape
     pos = nb // 2
+    rows = D * rq
     wunit, vunit = owner_rows(2 * dl // nb, nd), owner_rows(2 * din // nb, nd)
-    whalf = dl // 2
+    whalf, vhalf = dl // 2, (DV + DQK) // 4
     vmem = pl.BlockSpec(memory_space=pltpu.VMEM)
     anywhere = pl.BlockSpec(memory_space=pl.ANY)
     dma = pltpu.SemaphoreType.DMA
     scratch = (
-        shard_sum_scratch(nd, nb, 3 * pos, wunit, whalf)
-        + shard_sum_scratch(nd, nb, pos, vunit, din)
+        shard_sum_scratch(nd, nb, 3 * pos, wunit, 2 * dl // nb, whalf)
+        + shard_sum_scratch(nd, nb, pos, vunit, 2 * din // nb, vhalf)
+        + shard_sum_scratch(nd, nb, pos, vunit, 2 * din // nb, vhalf)
         + [
+            pltpu.VMEM((max(2 * dl, D * kc), dl), BF16),
             pltpu.VMEM((D, kc, din), BF16),
             pltpu.VMEM((D, kc, DQK), BF16),
-            pltpu.VMEM((D, kc, DV), BF16),
-            pltpu.VMEM((D, LAT, DV), BF16),
+            pltpu.VMEM((2 * D, LAT, DV // 2), BF16),
             pltpu.VMEM((LAT, 128), F32),
             pltpu.VMEM((D, HEADS, LAT), F32),
-            pltpu.VMEM((HEADS * LAT, DQK), BF16),
-            pltpu.VMEM((kc, HEADS * LAT), BF16),
-            pltpu.VMEM((kc, DV), F32),
+            pltpu.VMEM((HEADS, LAT, DQK // 2), BF16),
+            pltpu.VMEM((2, din, (DV + DQK) // 2), BF16),
+            pltpu.VMEM((kc, HEADS // 2 * LAT), BF16),
+            pltpu.VMEM((kc, DV // 2), F32),
             pltpu.VMEM((DQK, LAT), F32),
-            pltpu.VMEM((din, DV + DQK), F32),
-            pltpu.VMEM((nb, vunit * nd, din), BF16),
+            pltpu.VMEM((max(3 * rows, din), dl), F32),
+            pltpu.VMEM((2, rows, dl), F32),
+            pltpu.VMEM((dl, rows), BF16),
+            pltpu.VMEM((rows, dl), BF16),
+            pltpu.VMEM((max(2 * dl, D * kc), (DV + DQK) // 2), BF16),
+            pltpu.VMEM((2, pos, 2 * din // nb, vhalf), BF16),
             pltpu.VMEM((1, din), F32),
-            pltpu.VMEM((2, kc, din), F32),
+            pltpu.VMEM((1, dl), F32),
+            pltpu.VMEM((rq, dl), BF16),
             pltpu.VMEM((nd - 1, rq, dl), BF16),
             pltpu.VMEM((nb, rq + 16, 256), BF16),
             pltpu.VMEM((nb, rq + 16, 256), BF16),
             pltpu.VMEM((rq + 16, 256), BF16),
             pltpu.VMEM((nd, rq + 16, 256), BF16),
-            pltpu.VMEM((rq, 256), BF16),
-            dma((3,)), dma((2,)),
-            dma((D, pos - 1)), dma((D, pos - 1)), dma((D, pos - 1)), dma((D, pos - 1)),
-            dma((D, pos)), dma((D, pos)),
+            dma((12,)), dma, dma((2,)),
+            dma((2 * D, pos - 1)), dma((2 * D, pos - 1)),
+            dma((2 * D, pos - 1)), dma((2 * D, pos - 1)),
+            dma((2 * D, pos)), dma((2 * D, pos)),
             dma((nb - 1,)), dma((nb - 1,)), dma((nd - 1,)), dma((nd - 1,)),
             dma((nb - 1,)), dma((nb - 1,)), dma((nd - 1,)), dma((nd - 1,)),
             dma((nb - 1,)), dma((nb - 1,)),
@@ -1074,23 +1132,26 @@
     return pl.pallas_call(
         functools.partial(backward_kernel, nb, nd, wunit, vunit),
         out_shape=(
+            jax.ShapeDtypeStruct((rows, dl), F32),
             jax.ShapeDtypeStruct((D, kc, din), F32),
             jax.ShapeDtypeStruct((3, wunit * nd, whalf), BF16),
-            jax.ShapeDtypeStruct((1, vunit * nd, din), BF16),
+            jax.ShapeDtypeStruct((1, vunit * nd, vhalf), BF16),
+            jax.ShapeDtypeStruct((1, vunit * nd, vhalf), BF16),
             jax.ShapeDtypeStruct((rq, dl), F32),
             jax.ShapeDtypeStruct((LAT, DQK), BF16),
             jax.ShapeDtypeStruct((8, 256), F32),
         ),
-        in_specs=[anywhere] * 4 + [vmem] * 10,
-        out_specs=(anywhere,) + (vmem,) * 5,
+        in_specs=[anywhere] * 9 + [vmem] * 7,
+        out_specs=(anywhere,) * 2 + (vmem,) * 6,
         scratch_shapes=scratch,
         compiler_params=pltpu.CompilerParams(
-            collective_id=1, has_side_effects=True, vmem_limit_bytes=62 * 2**20
+            collective_id=1, has_side_effects=True, vmem_limit_bytes=63 * 2**20
         ),
         name="backward",
     )(
-        byte_embed, keys, values, wgrads, bias, gain_bytes.reshape(1, -1), w_key, w_value,
-        queries, lse, ga, delta, direct, gain_part,
+        byte_embed, keys, values.reshape(D * kc, DV), w_out, w_up, w_down, w_key, w_value,
+        cotangent.reshape(rows, dl), attended, latents, gain_mlp.reshape(1, -1), bias,
+        gain_bytes.reshape(1, -1), queries, lse,
     )
 
 
@@ -1120,21 +1181,20 @@
     attended, lse, keys, values, norm_cols, queries = forward(
         nb, byte_embed, bias, latents, gain_query, gain_bytes, w_query, w_key, w_value
     )
-    latents_out, ga, delta, wgrads, direct, gain_part = mlp(
-        nb, nd, attended, latents, gain_mlp, w_out, w_up, w_down, cotangent
+    latents_out, byte_grad, wsum, vsum0, vsum1, direct_sum, gq, gains = backward(
+        nb, nd, byte_embed, keys, values, w_out, w_up, w_down, w_key, w_value, cotangent,
+        attended, latents, gain_mlp, bias, gain_bytes, queries, lse,
     )
-    byte_grad, wsum, vsum, direct_sum, gq, gains = backward(
-        nb, nd, byte_embed, keys, values, wgrads, bias, gain_bytes, w_key, w_value, queries, lse,
-        ga, delta, direct, gain_part,
-    )
+    latents_out = latents_out.reshape(cotangent.shape)
 
     def unfold(shard, rows):
         return jnp.concatenate([shard[:rows], shard[rows : 2 * rows]], axis=1).astype(F32)
 
     step = dl // nb
     grad_w_down, grad_w_up, grad_w_out = (unfold(wsum[m], step) for m in range(3))
-    grad_kv = unfold(vsum[0], din // nb)
-    grad_w_value, grad_w_key = grad_kv[:, :DV], grad_kv[:, DV:]
+    halves = [unfold(v[0], din // nb) for v in (vsum0, vsum1)]
+    grad_w_value = jnp.concatenate([v[:, : DV // 2] for v in halves], axis=1)
+    grad_w_key = jnp.concatenate([v[:, DV // 2 :] for v in halves], axis=1)
     gains = gains.reshape(-1)
     gain_mlp_grad = lax.dynamic_slice(gains[:dl], (blk * step,), (step,))
     gain_bytes_grad = lax.dynamic_slice(gains[dl:], (blk * (din // nb),), (din // nb,))

time: 264 us -> 235 us (0.89); the launches traced: 260 us -> 235 us
  Pallas kernels: 237 us -> 211 us
    pallas_call x1 -> x0, Pallas kernels: 17.2 us -> none  [mlp(): pl.pallas_call(functools.partial(mlp_kernel, nb, half), out_shape=(jax.Sh...]
    pallas_call x1, Pallas kernels: 132 us -> 123 us  [backward(): pl.pallas_call(functools.partial(backward_kernel, nb, nd, wunit, vunit),...]
where the time goes in v3:
time: 235 us
  Pallas kernels  211 us (90%)
  local copies, waits for them, and re-layouts  11.3 us (5%)
  other arithmetic  7.93 us (3%)
  matrix products  4.15 us (2%)
    pallas_call x1, Pallas kernels, backward(): pl.pallas_call(functools.partial(backward_kernel, nb, nd, wunit, vunit),...  123 us
    pallas_call x1, Pallas kernels, forward(): pl.pallas_call(functools.partial(forward_kernel, nb), out_shape=(jax.Shap...  87.5 us

profile of v3, /device:TPU:0, one launch (start us, length us, event | category | flops | bytes accessed | tf_op | source)
XLA Modules:
  0.0 234.8 jit_solution(16484355108610393114)
XLA Ops:
  0.7 1.4 and_select_fusion.bias_ref.refs_12_
  2.0 1.3 reshape.82.gq_ref
  3.3 1.3 reshape.83.gb_ref.refs_13_
  4.6 0.0 copy-start.6
  4.6 87.5 %forward.1 = (bf16[8,32,1280]{2,1,0:T(8,128)(2,1)}, f32[8,8,256]{2,1,0:T(8,128)}, bf16[8,256,256]{2,1,0:T(8,128)(2,1)}, bf16[8,256,1280]{2,1,0:T(8,128)(2,1)}, b...) custom-call(bf16[8,256,768]{2,1,0:T(8,128)(2,1)} %refs_0_.1, f32[8,256]{1,0:T(8,128)} %and_select_fusion.bias_ref.refs_12_, ...), custom_call_target="tpu_custom_call" | custom-call | tf_op jit(solution)/shard_map/forward/pallas_call | solution.py:323
  92.1 0.0 copy-done.6
  92.1 0.6 reshape.86.refs_11_
  92.7 0.0 copy-start
  92.7 0.0 copy-start.1
  92.7 0.0 copy-start.5
  92.7 0.0 copy-start.4
  92.7 123.2 %backward.1 = (f32[256,1280]{1,0:T(8,128)}, f32[8,256,768]{2,1,0:T(8,128)}, bf16[3,320,640]{2,1,0:T(8,128)(2,1)}, bf16[1,192,384]{2,1,0:T(8,128)(2,1)}, bf16[1,1...) custom-call(bf16[8,256,768]{2,1,0:T(8,128)(2,1)} %refs_0_.1, ...), custom_call_target="tpu_custom_call" | custom-call | tf_op jit(solution)/shard_map/backward/pallas_call | solution.py:1132
  215.9 0.0 copy-done
  215.9 0.1 reduce_sum.45
  216.0 0.2 multiply_reduce_fusion.1
  216.2 0.0 copy-done.1
  216.3 0.0 copy-done.5
  216.3 1.2 fusion.10
  217.4 0.0 slice-start
  217.5 1.8 multiply_add_fusion
  219.3 0.0 copy-done.4
  219.3 1.1 fusion
  220.4 0.0 copy-start.3
  220.4 0.6 dynamic-slice_divide_fusion
  221.1 0.7 slice.93
  221.8 0.6 dynamic_slice.22
  222.4 0.7 slice.96
  223.1 0.6 dynamic_slice.23
  223.7 1.9 fusion.3
  225.6 1.0 slice_bitcast_fusion.7
  226.6 0.6 pad_maximum_fusion.3
  227.3 0.8 pad_maximum_fusion
  228.1 0.0 copy-start.2
  228.1 0.0 copy-done.3
  228.1 0.0 slice-start.1
  228.1 0.1 slice_bitcast_fusion.1
  228.3 1.3 maximum_convert_fusion
  229.5 0.9 maximum_convert_fusion.2
  230.5 0.0 copy-done.2
  230.5 1.1 copy.30
  231.5 0.0 slice-done
  231.5 0.6 slice-done.1
  232.1 2.7 %copy.31 = f32[8,256,768]{2,1,0:T(8,128)} copy(f32[8,256,768]{2,1,0:T(8,128)S(1)} %bitcast.28) | data formatting | bytes 12582912
  (10 shorter events, 0.1 us)
Async XLA Ops:
  4.6 87.5 %copy-start.6 = (f32[1280]{0:T(1024)S(1)}, f32[1280]{0:T(1024)}, u32[]{:S(2)}) copy-start(f32[1280]{0:T(1024)} %param.20) | copy-start | bytes 15364
  92.7 123.2 %copy-start = (f32[32,1280]{1,0:T(8,128)S(1)}, f32[32,1280]{1,0:T(8,128)}, u32[]{:S(2)}) copy-start(f32[32,1280]{1,0:T(8,128)} %refs_10_.1) | copy-start | bytes 491524
  92.7 123.5 %copy-start.1 = (bf16[1280,256]{1,0:T(8,128)(2,1)S(1)}, bf16[1280,256]{1,0:T(8,128)(2,1)}, u32[]{:S(2)}) copy-start(bf16[1280,256]{1,0:T(8,128)(2,1)} %wq_ref.1) | copy-start | bytes 1966084
  92.7 123.5 %copy-start.5 = (f32[1280]{0:T(1024)S(1)}, f32[1280]{0:T(1024)}, u32[]{:S(2)}) copy-start(f32[1280]{0:T(1024)} %param.18) | copy-start | bytes 15364
  92.7 126.6 %copy-start.4 = (bf16[256,256]{1,0:T(8,128)(2,1)S(1)}, bf16[256,256]{1,0:T(8,128)(2,1)}, u32[]{:S(2)}) copy-start(bf16[256,256]{1,0:T(8,128)(2,1)} %get-tuple-element.35) | copy-start | bytes 393220
  217.4 14.1 %slice-start = ((s8[6291456]{0:T(1024)(128)(4,1)}), s8[2097152]{0:T(1024)(128)(4,1)S(1)}, s32[]{:S(2)}) async-start(s8[6291456]{0:T(1024)(128)(4,1)} %bitcast.27), calls=%async_computation | async-start | bytes 4194304
  220.4 7.7 %copy-start.3 = (bf16[3,320,640]{2,1,0:T(8,128)(2,1)S(1)}, bf16[3,320,640]{2,1,0:T(8,128)(2,1)}, u32[]{:S(2)}) copy-start(bf16[3,320,640]{2,1,0:T(8,128)(2,1)} %get-tuple-element.39) | copy-start | bytes 3686404
  228.1 2.3 copy-start.2
  228.1 3.9 %slice-start.1 = ((s8[6291456]{0:T(1024)(128)(4,1)}), s8[4194304]{0:T(1024)(128)(4,1)S(1)}, s32[]{:S(2)}) async-start(s8[6291456]{0:T(1024)(128)(4,1)} %bitcast.27), calls=%async_computation.1 | async-start | bytes 8388608

commit v4 on v3

--- a/solution.py
+++ b/solution.py
@@ -73,8 +73,8 @@
 
 def forward_kernel(
     nb,
-    x_ref, bias_ref, lat_ref, gq_ref, gb_ref, wq_ref, wk_ref, wv_ref,
-    att_ref, lse_ref, k_ref, v_ref, nlw_ref, qall_ref,
+    x_ref, len_ref, mask_ref, lat_ref, gq_ref, gb_ref, wq_ref, wk_ref, wv_ref,
+    att_ref, lse_ref, k_ref, v_ref, nlw_ref, qall_ref, bias_ref,
     nl_cols, normed, qm, lloc, lmate, lz, acc, part, mate_in, rin, lin,
     q_s, q_r, n_s, n_r, l_s, l_r, mate_s, mate_r, rs_s, rs_r, ls_s, ls_r,
 ):
@@ -90,8 +90,13 @@
             barrier, inc=1, device_id=(doc, lax.rem(blk + i, nb)), device_id_type=MESH
         )
 
+    slots = blk * kc + lax.broadcasted_iota(jnp.int32, (1, kc), 1)
+    for n in range(D):
+        usable = (slots < len_ref[n]) & (mask_ref[n : n + 1, :] == 1)
+        bias_ref[n : n + 1, :] = jnp.where(usable, 0.0, masked_score)
+
     xhat, _ = norm_parts(lat_ref[...])
-    nl = (xhat * gq_ref[...]).astype(BF16)
+    nl = (xhat * gq_ref[...].reshape(1, -1)).astype(BF16)
     step = nl.shape[1] // nb
     for j in range(nb):
         at = min(j * step // 128 * 128, nl.shape[1] - 256)
@@ -121,7 +126,7 @@
     @pl.loop(0, D)
     def _(n):
         xh, _ = norm_parts(x_ref[n].astype(F32))
-        normed[n] = (xh * gb_ref[...]).astype(BF16)
+        normed[n] = (xh * gb_ref[...].reshape(1, -1)).astype(BF16)
         k_ref[n] = dot_nn(normed[n], wk_ref[...]).astype(BF16)
 
     for i in range(1, nb):
@@ -314,7 +319,9 @@
                 left_copy(n, j, part.at[n, c, j]).wait_send()
 
 
-def forward(nb, byte_embed, bias, latents, gain_query, gain_bytes, w_query, w_key, w_value):
+def forward(
+    nb, byte_embed, doc_lengths, key_mask, latents, gain_query, gain_bytes, w_query, w_key, w_value
+):
     D, kc, din = byte_embed.shape
     rq, dl = latents.shape
     pos = nb // 2
@@ -329,9 +336,10 @@
             jax.ShapeDtypeStruct((D, kc, DV), BF16),
             jax.ShapeDtypeStruct((LAT, 256), BF16),
             jax.ShapeDtypeStruct((LAT, DQK), BF16),
+            jax.ShapeDtypeStruct((D, kc), F32),
         ),
-        in_specs=[vmem] * 8,
-        out_specs=(vmem,) * 6,
+        in_specs=[vmem, pl.BlockSpec(memory_space=pltpu.SMEM)] + [vmem] * 7,
+        out_specs=(vmem,) * 7,
         scratch_shapes=[
             pltpu.VMEM((nb, rq, 256), BF16),
             pltpu.VMEM((D, kc, din), BF16),
@@ -354,8 +362,7 @@
         ),
         name="forward",
     )(
-        byte_embed, bias, latents, gain_query.reshape(1, -1), gain_bytes.reshape(1, -1),
-        w_query, w_key, w_value,
+        byte_embed, doc_lengths, key_mask, latents, gain_query, gain_bytes, w_query, w_key, w_value,
     )
 
 
@@ -374,7 +381,7 @@
 
 class ShardSums:
     def __init__(
-        self, doc, blk, nd, nb, count, unit, group, lags,
+        self, doc, blk, nd, nb, count, unit, group, lags, direct,
         own, mate_in, inbox, rin, lin, out, sems,
     ):
         self.doc, self.p, self.c = doc, blk // 2, blk % 2
@@ -386,8 +393,8 @@
             self.mate_s, self.mate_r, self.in_s, self.in_r,
             self.right_s, self.right_r, self.left_s, self.left_r, self.out_s, self.out_r,
         ) = sems
-        self.group, self.lags = group, lags
-        self.steps = count // group + lags[-1] + self.pos - 1
+        self.group, self.lags, self.direct = group, lags, direct
+        self.steps = count // group + lags[-1] + (1 if direct else self.pos - 1)
 
     def weight(self, s, k):
         b = (s + k) % self.bits
@@ -477,6 +484,8 @@
             for i in range(self.width(k)):
                 self.halving(s, k, i).start()
             return
+        if self.direct:
+            return
         j = s % self.pos
 
         @pl.when((self.p == 0) & (j > 0))
@@ -528,22 +537,50 @@
             for i in range(1, self.nd):
                 self.share(m, i).start()
 
-    def step(self, t, mate_copy, entered=0):
+    def spread(self, i, back):
+        to = lax.rem(self.p + (self.pos - i if back else i), self.pos)
+        return remote(
+            self.own.at[to, self.rows(self.doc), :], self.rin.at[i - 1],
+            self.right_s.at[i - 1], self.right_r.at[i - 1], self.doc, 2 * to + self.c,
+        )
+
+    def scatter(self):
+        for i in range(1, self.pos):
+            self.spread(i, False).start()
+
+    def collect(self):
+        rows = self.rows(self.doc)
+        total = self.own[self.p, rows, :].astype(F32)
+        for i in range(1, self.pos):
+            self.spread(i, True).wait_recv()
+            total = total + self.rin[i - 1].astype(F32)
+        self.out[0, rows, :] = total.astype(BF16)
+        for i in range(1, self.nd):
+            self.share(0, i).start()
+
+    def step(self, t, mate_copy):
         def at(t, when, run, turned=False):
             @pl.when((t >= 0) & (t < self.count // self.group) & when)
             def _():
                 for i in range(self.group):
                     run(t * self.group + (self.group - 1 - i if turned else i))
 
-        at(t, t >= entered, lambda s: self.begin(s, mate_copy))
+        at(t, True, lambda s: self.begin(s, mate_copy))
         for k in range(1, self.bits + 1):
             at(t - self.lags[k - 1], True, functools.partial(self.halve, k=k))
         base = t - self.lags[-1]
+        if self.direct:
+            pl.when(base == 0)(self.scatter)
+            pl.when(base == 1)(self.collect)
+            return
         at(base - self.p, self.p > 0, self.from_left, True)
         at(base - (self.pos - 1 - self.p), self.p < self.pos - 1, self.from_right)
         at(base - (self.pos - 1), True, self.finish)
 
     def drain(self):
+        if self.direct:
+            for i in range(1, self.pos):
+                self.spread(i, False).wait_send()
         for m in range(self.count // self.pos):
             for i in range(1, self.nd):
                 self.shared(m, i).wait_recv()
@@ -554,6 +591,8 @@
             for k in range(self.bits):
                 for i in range(self.width(k)):
                     self.halving(s, k, i).wait_send()
+            if self.direct:
+                return
             j = s % self.pos
 
             @pl.when((j > self.p) & (self.p < self.pos - 1))
@@ -590,7 +629,7 @@
     wscr, vscr = refs[24:39], (refs[39:54], refs[54:69])
     (
         wpool, x_ref, k_ref, ga_all, delta_all, delta_t, qm, wkv, ds_all, gv_acc, gq_acc,
-        fpool, frames, low_t, right, stage, vstage, gain_acc, gmlp_acc, direct_out, dir_in,
+        fpool, frames, low_t, nm, act_low, gm, g_up, gb, stage, vstage, gain_acc, gmlp_acc, direct_out, dir_in,
         misc_out, misc_in, misc2_out, misc2_in,
         load_s, out_s, bg_s, ar_s, ar_r, al_s, al_r, am_s, am_r, d_s, d_r, dir_s, dir_r,
         m1_s, m1_r, m2_s, m2_r, m3_s, m3_r,
@@ -634,12 +673,12 @@
     load_cot.start()
 
     weights = ShardSums(
-        doc, blk, nd, nb, 3 * pos, wunit, 2, [3 + k for k in range(bits)],
+        doc, blk, nd, nb, 3 * pos, wunit, 2, [4 + k for k in range(bits)], False,
         *wscr[:5], wsum_ref, wscr[5:],
     )
     values = [
         ShardSums(
-            doc, blk, nd, nb, pos, vunit, pos, lags, *vscr[g][:5], out, vscr[g][5:],
+            doc, blk, nd, nb, pos, vunit, pos, lags, True, *vscr[g][:5], out, vscr[g][5:],
         )
         for g, (lags, out) in enumerate(
             (
@@ -719,8 +758,8 @@
     kv_acc = fpool.at[0:din, 0 : vh + qh]
     step_w = dl // nb
 
-    def weight_grad(m, left):
-        low_t[...] = jnp.transpose(left)
+    def weight_grad(m, left, right):
+        low_t[...] = jnp.transpose(left[...])
 
         @pl.loop(0, pos)
         def _(j):
@@ -744,48 +783,42 @@
     load_down.start()
     xh, inv = norm_parts(mid[...])
     xhat[...] = xh
-    nm = (xh * gm_ref[...]).astype(BF16)
+    nm[...] = (xh * gm_ref[...].reshape(1, -1)).astype(BF16)
     load_up.wait()
-    act, sl = gelu_parts(dot_nn(nm, slot1[...]))
+    act, sl = gelu_parts(dot_nn(nm[...], slot1[...]))
     slope[...] = sl
-    act_low = act.astype(BF16)
+    act_low[...] = act.astype(BF16)
     load_cot.wait()
-    gm = frames[1].astype(BF16)
-    right[...] = gm
-    pl.semaphore_wait(barrier, nb - 1 + nd - 1)
-    weight_grad(0, act_low)
+    gm[...] = frames[1].astype(BF16)
     load_down.wait()
-    frames[0] = mid[...] + dot_nn(act_low, slot0[...])
+    frames[0] = mid[...] + dot_nn(act_low[...], slot0[...])
     store_out = pltpu.make_async_copy(frames.at[0], out_hbm, out_s)
     store_out.start()
-    g_up = (dot_nt(gm, slot0[...]) * slope[...]).astype(BF16)
+    g_up[...] = (dot_nt(gm[...], slot0[...]) * slope[...]).astype(BF16)
     load_out2.start()
     for item in later:
         item.start()
-    for s in range(pos):
-        weights.begin(s, w_mate)
-    right[...] = g_up
-    weight_grad(1, nm)
-    g_nm = dot_nt(g_up, slot1[...])
+    g_nm = dot_nt(g_up[...], slot1[...])
     gmlp_acc[...] = jnp.sum(g_nm * xhat[...], axis=0, keepdims=True)
-    dxh = g_nm * gm_ref[...]
+    dxh = g_nm * gm_ref[...].reshape(1, -1)
     mid[...] = frames[1] + inv * (
         dxh
         - jnp.mean(dxh, axis=-1, keepdims=True)
         - xhat[...] * jnp.mean(dxh * xhat[...], axis=-1, keepdims=True)
     )
-    gb = mid[...].astype(BF16)
-    right[...] = gb
+    gb[...] = mid[...].astype(BF16)
     load_out2.wait()
-    ga = dot_nt(gb, slot0[...])
+    ga = dot_nt(gb[...], slot0[...])
     load_v.start()
     for g in range(2):
         for n in range(D):
             ga_all[g * D + n, own_rows, :] = ga[
                 n * rq : (n + 1) * rq, g * vh : (g + 1) * vh
             ].astype(BF16)
+    pl.semaphore_wait(barrier, nb - 1 + nd - 1)
     for e in range(ahead):
         send_own(e)
+    weight_grad(0, act_low, gm)
     lane = lax.broadcasted_iota(jnp.int32, (rq, 128), 1)
     delta = jnp.zeros((rq, 128), F32)
     for h in range(HEADS):
@@ -803,9 +836,10 @@
     direct_out[...] = direct.astype(BF16)
     for i in range(1, nd):
         direct_copy(i).start()
+    weight_grad(1, nm, g_up)
     for s in range(pos):
         w_mate(s).wait_send()
-    weight_grad(2, att_low)
+    weight_grad(2, att_low, gb)
 
     for h in range(HEADS):
         half = slice(h // hh * qh, h // hh * qh + qh)
@@ -872,13 +906,13 @@
             [gv_acc[...].astype(BF16), (gk * SCORE_SCALE).astype(BF16)], axis=1
         )
         xh, inv = norm_parts(x_ref[n].astype(F32))
-        kept = stage.at[doc_rows(n), 0 : vh + qh]
+        kept = stage.at[doc_rows(n), 0:din]
         if g == 0:
-            kept[...] = grads_now
+            kept[...] = dot_nt(grads_now, wkv[0]).astype(BF16)
         else:
-            gx = dot_nt(kept[...], wkv[0]) + dot_nt(grads_now, wkv[1])
+            gx = kept[...].astype(F32) + dot_nt(grads_now, wkv[1])
             gain_acc[...] += jnp.sum(gx * xh, axis=0, keepdims=True)
-            dxh = gx * gb_ref[...]
+            dxh = gx * gb_ref[...].reshape(1, -1)
             slot = lax.rem(n, 2)
 
             @pl.when(n >= 2)
@@ -891,7 +925,7 @@
                 - xh * jnp.mean(dxh * xh, axis=-1, keepdims=True)
             )
             pltpu.make_async_copy(frames.at[slot, 0:kc, 0:din], bg_hbm.at[n], bg_s.at[slot]).start()
-        normed_t = jnp.transpose((xh * gb_ref[...]).astype(BF16))
+        normed_t = jnp.transpose((xh * gb_ref[...].reshape(1, -1)).astype(BF16))
         kv_acc[...] += dot_nn(normed_t, grads_now)
 
     def cut_values(g):
@@ -923,7 +957,7 @@
 
         @pl.when(t % 2 == 0)
         def _():
-            weights.step(t // 2 + 2, w_mate, pos // 2)
+            weights.step(t // 2, w_mate)
             values[0].step(t // 2 - start0, v_mate(0))
 
         @pl.when(t == pos)
@@ -986,13 +1020,13 @@
     misc_in[blk] = misc_out[blk]
 
     first = (parts + pos + 1) // 2
-    last = max(weights.steps - 2, start0 + values[0].steps, first + values[1].steps)
+    last = max(weights.steps, start0 + values[0].steps, first + values[1].steps)
 
     @pl.loop(first, last)
     def _(t):
         values[1].step(t - first, v_mate(1))
         values[0].step(t - start0, v_mate(0))
-        weights.step(t + 2, w_mate, pos // 2)
+        weights.step(t, w_mate)
 
         @pl.when(t == first + 1)
         def _():
@@ -1110,6 +1144,10 @@
             pltpu.VMEM((2, rows, dl), F32),
             pltpu.VMEM((dl, rows), BF16),
             pltpu.VMEM((rows, dl), BF16),
+            pltpu.VMEM((rows, dl), BF16),
+            pltpu.VMEM((rows, dl), BF16),
+            pltpu.VMEM((rows, dl), BF16),
+            pltpu.VMEM((rows, dl), BF16),
             pltpu.VMEM((max(2 * dl, D * kc), (DV + DQK) // 2), BF16),
             pltpu.VMEM((2, pos, 2 * din // nb, vhalf), BF16),
             pltpu.VMEM((1, din), F32),
@@ -1150,8 +1188,111 @@
         name="backward",
     )(
         byte_embed, keys, values.reshape(D * kc, DV), w_out, w_up, w_down, w_key, w_value,
-        cotangent.reshape(rows, dl), attended, latents, gain_mlp.reshape(1, -1), bias,
-        gain_bytes.reshape(1, -1), queries, lse,
+        cotangent.reshape(rows, dl), attended, latents, gain_mlp, bias,
+        gain_bytes, queries, lse,
+    )
+
+
+def finish_kernel(
+    nb, rows_hbm, bytes_hbm, wsum_hbm, vsum0_ref, vsum1_ref, dsum_ref, gq_ref, gains_ref, cols_ref,
+    lat_ref, gain_ref, wq_ref, rows_out, bytes_out, lgrad_ref, gq_gain_ref, gb_gain_ref,
+    gm_gain_ref, wq_out, wk_out, wv_out, wo_out, wu_out, wd_out, turned,
+    wsum_ref, bytes_buf, rows_buf, take_s, move_s,
+):
+    D = bytes_hbm.shape[0]
+    pairs = [(bytes_hbm.at[n], bytes_buf.at[n], bytes_out.at[n]) for n in range(D)]
+    pairs.append((rows_hbm, rows_buf, rows_out))
+    takes = [
+        pltpu.make_async_copy(src, buf, take_s.at[i]) for i, (src, buf, _) in enumerate(pairs)
+    ]
+    takes.append(pltpu.make_async_copy(wsum_hbm, wsum_ref, take_s.at[D + 1]))
+    moves = [
+        pltpu.make_async_copy(buf, out, move_s.at[i]) for i, (_, buf, out) in enumerate(pairs)
+    ]
+    for take in takes:
+        take.start()
+    for take, move in zip(takes, moves):
+        take.wait()
+        move.start()
+    takes[-1].wait()
+    rq, dl = lat_ref.shape
+    din, step, vstep = wk_out.shape[0] * nb, dl // nb, wk_out.shape[0]
+    blk = lax.axis_index("blk")
+    half = dl // 2
+    for m, out in enumerate((wd_out, wu_out, wo_out)):
+        for i in range(2):
+            out[:, i * half : (i + 1) * half] = wsum_ref[
+                m, i * step : (i + 1) * step, :
+            ].astype(F32)
+    width = (DV + DQK) // 4
+    for g, ref in enumerate((vsum0_ref, vsum1_ref)):
+        both = jnp.concatenate(
+            [ref[0, i * vstep : (i + 1) * vstep, :].astype(F32) for i in range(2)], axis=1
+        )
+        at = DV // 2
+        wv_out[:, g * at : (g + 1) * at] = both[:, :at]
+        wk_out[:, g * DQK // 2 : (g + 1) * DQK // 2] = both[:, at : 2 * width]
+
+    gq = gq_ref[...]
+    cols = cols_ref[...]
+    first = pl.multiple_of(jnp.minimum(blk * step // 128 * 128, dl - 256), 128)
+    skip = blk * step - first
+    turned[...] = dot_nn(jnp.transpose(cols), gq)
+    wq_out[...] = turned[pl.ds(pl.multiple_of(skip, 16), step), :]
+    dy = dot_nt(gq, wq_ref[pl.ds(first, 256), :])
+    gain = jnp.sum(dy * cols.astype(F32), axis=0, keepdims=True) / gain_ref[pl.ds(first, 256)].reshape(1, -1)
+
+    def cut(row, at, count):
+        size = row.shape[1]
+        return pltpu.roll(row, lax.rem(size - at, size), 1)[:, :count]
+
+    gq_gain_ref[...] = cut(gain, skip, step)
+    row = jnp.concatenate([gains_ref[i : i + 1, :] for i in range(8)], axis=1)
+    gm_gain_ref[...] = cut(row[:, :dl], blk * step, step)
+    gb_gain_ref[...] = cut(row[:, dl:], blk * vstep, vstep)
+
+    own = gq_ref[pl.ds(pl.multiple_of(blk * rq, rq), rq), :]
+    dxh = dot_nt(own, wq_ref[...]) * gain_ref[...].reshape(1, -1)
+    xh, inv = norm_parts(lat_ref[...])
+    lgrad_ref[...] = dsum_ref[...] + inv * (
+        dxh
+        - jnp.mean(dxh, axis=-1, keepdims=True)
+        - xh * jnp.mean(dxh * xh, axis=-1, keepdims=True)
+    )
+    for move in moves:
+        move.wait()
+
+
+def finish(
+    nb, latents_out, byte_grad, wsum, vsum0, vsum1, direct_sum, gq, gains, norm_cols, latents,
+    gain_query, w_query,
+):
+    rq, dl = latents.shape
+    din = gains.size - dl
+    vmem = pl.BlockSpec(memory_space=pltpu.VMEM)
+    anywhere = pl.BlockSpec(memory_space=pl.ANY)
+    shapes = (
+        latents_out.shape, byte_grad.shape, (rq, dl), (1, dl // nb), (1, din // nb), (1, dl // nb), (dl // nb, DQK),
+        (din // nb, DQK), (din // nb, DV), (dl // nb, dl), (dl // nb, dl), (dl // nb, dl),
+    )
+    return pl.pallas_call(
+        functools.partial(finish_kernel, nb),
+        out_shape=tuple(jax.ShapeDtypeStruct(s, F32) for s in shapes),
+        in_specs=[anywhere] * 3 + [vmem] * 9,
+        out_specs=(anywhere,) * 2 + (vmem,) * 10,
+        scratch_shapes=[
+            pltpu.VMEM((256, DQK), F32),
+            pltpu.VMEM(wsum.shape, BF16),
+            pltpu.VMEM(byte_grad.shape, F32),
+            pltpu.VMEM(latents_out.shape, F32),
+            pltpu.SemaphoreType.DMA((byte_grad.shape[0] + 2,)),
+            pltpu.SemaphoreType.DMA((byte_grad.shape[0] + 1,)),
+        ],
+        compiler_params=pltpu.CompilerParams(vmem_limit_bytes=60 * 2**20),
+        name="finish",
+    )(
+        latents_out, byte_grad, wsum, vsum0, vsum1, direct_sum, gq, gains, norm_cols, latents,
+        gain_query, w_query,
     )
 
 
@@ -1172,56 +1313,29 @@
     cotangent,
 ):
     nb, nd = lax.axis_size("blk"), lax.axis_size("doc")
-    blk = lax.axis_index("blk")
-    key_count, din = byte_embed.shape[1:]
-    dl = latents.shape[1]
-    positions = blk * key_count + jnp.arange(key_count, dtype=jnp.int32)
-    usable = (positions[None, :] < doc_lengths[:, None]) & (key_mask == 1)
-    bias = jnp.where(usable, 0.0, masked_score).astype(F32)
-    attended, lse, keys, values, norm_cols, queries = forward(
-        nb, byte_embed, bias, latents, gain_query, gain_bytes, w_query, w_key, w_value
+    attended, lse, keys, values, norm_cols, queries, bias = forward(
+        nb, byte_embed, doc_lengths, key_mask, latents, gain_query, gain_bytes, w_query, w_key,
+        w_value,
     )
     latents_out, byte_grad, wsum, vsum0, vsum1, direct_sum, gq, gains = backward(
         nb, nd, byte_embed, keys, values, w_out, w_up, w_down, w_key, w_value, cotangent,
         attended, latents, gain_mlp, bias, gain_bytes, queries, lse,
     )
+    (
+        latents_out, byte_grad, latents_grad, gain_query_grad, gain_bytes_grad, gain_mlp_grad,
+        grad_w_query, grad_w_key, grad_w_value, grad_w_out, grad_w_up, grad_w_down,
+    ) = finish(
+        nb, latents_out, byte_grad, wsum, vsum0, vsum1, direct_sum, gq, gains, norm_cols,
+        latents, gain_query, w_query,
+    )
     latents_out = latents_out.reshape(cotangent.shape)
-
-    def unfold(shard, rows):
-        return jnp.concatenate([shard[:rows], shard[rows : 2 * rows]], axis=1).astype(F32)
-
-    step = dl // nb
-    grad_w_down, grad_w_up, grad_w_out = (unfold(wsum[m], step) for m in range(3))
-    halves = [unfold(v[0], din // nb) for v in (vsum0, vsum1)]
-    grad_w_value = jnp.concatenate([v[:, : DV // 2] for v in halves], axis=1)
-    grad_w_key = jnp.concatenate([v[:, DV // 2 :] for v in halves], axis=1)
-    gains = gains.reshape(-1)
-    gain_mlp_grad = lax.dynamic_slice(gains[:dl], (blk * step,), (step,))
-    gain_bytes_grad = lax.dynamic_slice(gains[dl:], (blk * (din // nb),), (din // nb,))
-    skip = blk * step - jnp.minimum(blk * step // 128 * 128, dl - 256)
-    cols = lax.dynamic_slice(norm_cols, (0, skip), (LAT, step))
-    grad_w_query = lax.dot_general(
-        cols, gq, (((0,), (0,)), ((), ())), preferred_element_type=F32
-    )
-    wq_rows = lax.dynamic_slice(w_query, (blk * step, 0), (step, DQK))
-    dy_cols = dot_nt(gq, wq_rows)
-    gain_rows = lax.dynamic_slice(gain_query, (blk * step,), (step,))
-    gain_query_grad = jnp.sum(dy_cols * cols.astype(F32), axis=0) / gain_rows
-    own = lax.dynamic_slice(gq, (blk * latents.shape[0], 0), (latents.shape[0], DQK))
-    dxh = dot_nt(own, w_query) * gain_query
-    xh, inv = norm_parts(latents)
-    latents_grad = direct_sum + inv * (
-        dxh
-        - jnp.mean(dxh, axis=-1, keepdims=True)
-        - xh * jnp.mean(dxh * xh, axis=-1, keepdims=True)
-    )
     return (
         latents_out,
         byte_grad,
         latents_grad,
-        gain_query_grad,
-        gain_bytes_grad,
-        gain_mlp_grad,
+        gain_query_grad.reshape(-1),
+        gain_bytes_grad.reshape(-1),
+        gain_mlp_grad.reshape(-1),
         grad_w_query,
         grad_w_key,
         grad_w_value,

time: 235 us -> 214 us (0.911)
  local copies, waits for them, and re-layouts: 11.3 us -> 0 us
  other arithmetic: 7.93 us -> 0 us
  matrix products: 4.15 us -> 0 us
    pallas_call x0 -> x1, Pallas kernels: none -> 9.78 us  [finish(): pl.pallas_call(functools.partial(finish_kernel, nb), out_shape=tuple((jax...]
    pallas_call x1, Pallas kernels: 123 us -> 116 us  [backward(): pl.pallas_call(functools.partial(backward_kernel, nb, nd, wunit, vunit),...]
    unnamed x20 -> x0, local copies, waits for them, and re-layouts: 4.34 us -> none
    dot_general x3 -> x0, matrix products: 4.15 us -> none  [the longest x2 2.3 us: dot_nt(): lax.dot_general(a, b, (((1,), (1,)), ((), ())), preferred_element_type=F32)]
    reshape x3 -> x0, local copies, waits for them, and re-layouts: 3.16 us -> none  [the longest x1 1.29 us: forward(): gain_query.reshape(1, -1)]
    slice x5 -> x0, local copies, waits for them, and re-layouts: 2.53 us -> none  [the longest x2 1.13 us: unfold(): shard[:rows]]
where the time goes in v4:
time: 214 us
  Pallas kernels  213 us (100%)
    pallas_call x1, Pallas kernels, backward(): pl.pallas_call(functools.partial(backward_kernel, nb, nd, wunit, vunit),...  116 us
    pallas_call x1, Pallas kernels, forward(): pl.pallas_call(functools.partial(forward_kernel, nb), out_shape=(jax.Shap...  87.6 us
    pallas_call x1, Pallas kernels, finish(): pl.pallas_call(functools.partial(finish_kernel, nb), out_shape=tuple((jax...  9.78 us

profile of v4, /device:TPU:0, one launch (start us, length us, event | category | flops | bytes accessed | tf_op | source)
XLA Modules:
  0.0 214.2 jit_solution(10621482160862058147)
XLA Ops:
  0.6 87.6 %forward.1 = (bf16[8,32,1280]{2,1,0:T(8,128)(2,1)}, f32[8,8,256]{2,1,0:T(8,128)}, bf16[8,256,256]{2,1,0:T(8,128)(2,1)}, bf16[8,256,1280]{2,1,0:T(8,128)(2,1)}, b...) custom-call(bf16[8,256,768]{2,1,0:T(8,128)(2,1)} %refs_0_.1, s32[8]{0:T(128)} %len_ref.1, ...), custom_call_target="tpu_custom_call" | custom-call | tf_op jit(solution)/shard_map/forward/pallas_call | solution.py:330
  88.2 116.0 %backward.1 = (f32[256,1280]{1,0:T(8,128)}, f32[8,256,768]{2,1,0:T(8,128)}, bf16[3,320,640]{2,1,0:T(8,128)(2,1)}, bf16[1,192,384]{2,1,0:T(8,128)(2,1)}, bf16[1,1...) custom-call(bf16[8,256,768]{2,1,0:T(8,128)(2,1)} %refs_0_.1, ...), custom_call_target="tpu_custom_call" | custom-call | tf_op jit(solution)/shard_map/backward/pallas_call | solution.py:1170
  204.2 9.8 %finish.1 = (f32[256,1280]{1,0:T(8,128)}, f32[8,256,768]{2,1,0:T(8,128)}, f32[32,1280]{1,0:T(8,128)}, f32[1,160]{1,0:T(1,128)}, f32[1,96]{1,0:T(1,128)}, /*index...) custom-call(f32[256,1280]{1,0:T(8,128)} %get-tuple-element.45.rows_h, ...), custom_call_target="tpu_custom_call" | custom-call | tf_op jit(solution)/shard_map/finish/pallas_call | solution.py:1278

commit v5 on v4

--- a/solution.py
+++ b/solution.py
@@ -73,17 +73,35 @@
 
 def forward_kernel(
     nb,
-    x_ref, len_ref, mask_ref, lat_ref, gq_ref, gb_ref, wq_ref, wk_ref, wv_ref,
-    att_ref, lse_ref, k_ref, v_ref, nlw_ref, qall_ref, bias_ref,
-    nl_cols, normed, qm, lloc, lmate, lz, acc, part, mate_in, rin, lin,
-    q_s, q_r, n_s, n_r, l_s, l_r, mate_s, mate_r, rs_s, rs_r, ls_s, ls_r,
+    x_hbm, wq_hbm, wk_hbm, wv_hbm, len_ref, mask_ref, lat_ref, gq_ref, gb_ref,
+    att_ref, lse_ref, k_hbm, v_hbm, nlw_ref, qall_ref, bias_ref,
+    x_ref, wq_ref, wk_ref, wv_ref, k_ref, v_ref, nl_cols, normed, qm, lloc, lmate, lz, acc, part, mate_in, rin, lin,
+    load_s, x_s, out_s, q_s, q_r, n_s, n_r, l_s, l_r, mate_s, mate_r, rs_s, rs_r, ls_s, ls_r,
 ):
-    D, kc, din = x_ref.shape
+    D, kc, din = x_hbm.shape
     rq = lat_ref.shape[0]
     pos = nb // 2
     doc, blk = lax.axis_index("doc"), lax.axis_index("blk")
     p, c = blk // 2, blk % 2
     mate = 2 * p + 1 - c
+    loads = [
+        pltpu.make_async_copy(src, dst, load_s.at[i])
+        for i, (src, dst) in enumerate(((wq_hbm, wq_ref), (wk_hbm, wk_ref), (wv_hbm, wv_ref)))
+    ]
+
+    def x_load(n):
+        return pltpu.make_async_copy(x_hbm.at[n], x_ref.at[n], x_s.at[n])
+
+    stores = [
+        pltpu.make_async_copy(src, dst, out_s.at[i])
+        for i, (src, dst) in enumerate(((k_ref, k_hbm), (v_ref, v_hbm)))
+    ]
+    loads[0].start()
+    x_load(0).start()
+    loads[1].start()
+    for n in range(1, D):
+        x_load(n).start()
+    loads[2].start()
     barrier = pltpu.get_barrier_semaphore()
     for i in range(1, nb):
         pl.semaphore_signal(
@@ -102,6 +120,7 @@
         at = min(j * step // 128 * 128, nl.shape[1] - 256)
         nl_cols[j] = nl[:, at : at + 256]
     own = pl.ds(pl.multiple_of(blk * rq, rq), rq)
+    loads[0].wait()
     qall_ref[own, :] = dot_nn(nl, wq_ref[...]).astype(BF16)
     pl.semaphore_wait(barrier, nb - 1)
 
@@ -123,8 +142,11 @@
         n_copy(i, own).start()
     nlw_ref[own, :] = nl_cols[blk]
 
+    loads[1].wait()
+
     @pl.loop(0, D)
     def _(n):
+        x_load(n).wait()
         xh, _ = norm_parts(x_ref[n].astype(F32))
         normed[n] = (xh * gb_ref[...].reshape(1, -1)).astype(BF16)
         k_ref[n] = dot_nn(normed[n], wk_ref[...]).astype(BF16)
@@ -135,58 +157,80 @@
     for h in range(HEADS):
         qm[h] = qall_ref[...] * query_mask(h, LAT)
 
-    @pl.loop(0, D)
-    def _(n):
-        bias = wide(row_to_lanes(bias_ref[pl.ds(n, 1), :]), LAT)
-        kn = k_ref[n]
-        rows = []
-        for h in range(HEADS):
-            s = dot_nt(kn, qm[h]) * SCORE2 + bias
-            top = jnp.max(s, axis=0, keepdims=True)
-            tot = jnp.sum(jnp.exp2(s - top), axis=0, keepdims=True)
-            rows.append(top + jnp.log(tot) * LOG2E)
-        lloc[n] = jnp.concatenate(rows, axis=0)
-
-    half = D // 2
-    mine, other = pl.ds(c * half, half), pl.ds((1 - c) * half, half)
+    stores[0].start()
+
+    def own_logs(lo, hi):
+        @pl.loop(lo, hi)
+        def _(n):
+            bias = wide(row_to_lanes(bias_ref[pl.ds(n, 1), :]), LAT)
+            kn = k_ref[n]
+            rows = []
+            for h in range(HEADS):
+                s = dot_nt(kn, qm[h]) * SCORE2 + bias
+                top = jnp.max(s, axis=0, keepdims=True)
+                tot = jnp.sum(jnp.exp2(s - top), axis=0, keepdims=True)
+                rows.append(top + jnp.log(tot) * LOG2E)
+            lloc[n] = jnp.concatenate(rows, axis=0)
+
+    half, quarter = D // 2, D // 4
+
+    def mine(b):
+        return pl.ds(b * half + c * quarter, quarter)
+
+    def other(b):
+        return pl.ds(b * half + (1 - c) * quarter, quarter)
 
     def merge(a, b):
         top = jnp.maximum(a, b)
         return top + jnp.log(jnp.exp2(a - top) + jnp.exp2(b - top)) * LOG2E
 
-    first = remote(lloc.at[other], lmate, l_s.at[0], l_r.at[0], doc, mate)
-    first.start()
+    def first(b):
+        return remote(lloc.at[other(b)], lmate.at[b], l_s.at[b, 0], l_r.at[b, 0], doc, mate)
+
+    def z_copy(b, i, slot):
+        return remote(
+            lz.at[b, p], lz.at[b, slot], l_s.at[b, i], l_r.at[b, i],
+            doc, 2 * lax.rem(p + i, pos) + c,
+        )
+
+    def last(b, part):
+        return remote(
+            lse_ref.at[part], lse_ref.at[part], l_s.at[b, pos], l_r.at[b, pos], doc, mate
+        )
+
+    def along(b):
+        first(b).wait_recv()
+        lz[b, p] = merge(lloc[mine(b)], lmate[b])
+        for i in range(1, pos):
+            z_copy(b, i, p).start()
+
+    def close(b):
+        for i in range(1, pos):
+            z_copy(b, i, lax.rem(p + pos - i, pos)).wait_recv()
+        total = lz[b, 0]
+        for i in range(1, pos):
+            total = merge(total, lz[b, i])
+        lse_ref[mine(b)] = total
+        last(b, mine(b)).start()
 
     def values(lo, hi):
         @pl.loop(lo, hi)
         def _(n):
             v_ref[n] = dot_nn(normed[n], wv_ref[...]).astype(BF16)
 
-    values(0, D // 4)
-    first.wait_recv()
-    lz[p] = merge(lloc[mine], lmate[...])
-
-    def z_copy(i, slot):
-        return remote(
-            lz.at[p], lz.at[slot], l_s.at[i], l_r.at[i],
-            doc, 2 * lax.rem(p + i, pos) + c,
-        )
-
-    for i in range(1, pos):
-        z_copy(i, p).start()
-    values(D // 4, 3 * D // 4)
-    for i in range(1, pos):
-        z_copy(i, lax.rem(p + pos - i, pos)).wait_recv()
-    total = lz[0]
-    for i in range(1, pos):
-        total = merge(total, lz[i])
-    lse_ref[mine] = total
-    last = remote(lse_ref.at[mine], lse_ref.at[mine], l_s.at[pos], l_r.at[pos], doc, mate)
-    last.start()
-    values(3 * D // 4, D)
-    remote(
-        lse_ref.at[other], lse_ref.at[other], l_s.at[pos], l_r.at[pos], doc, mate
-    ).wait_recv()
+    own_logs(0, half)
+    first(0).start()
+    own_logs(half, D)
+    first(1).start()
+    along(0)
+    loads[2].wait()
+    values(0, quarter)
+    along(1)
+    values(quarter, D)
+    stores[1].start()
+    close(0)
+    close(1)
+    last(0, other(0)).wait_recv()
 
     def mate_copy(n):
         return remote(
@@ -207,20 +251,25 @@
 
     def chip_sum(n):
         mate_copy(n).wait_recv()
-        for j in range(pos):
-            both = part[n, c, j].astype(F32) + mate_in[n, j].astype(F32)
-            part[n, c, j] = both.astype(BF16)
-
-            @pl.when((p == 0) & (j > 0))
-            def _():
+        both = part[n, c].astype(F32) + mate_in[n].astype(F32)
+        part[n, c] = both.astype(BF16)
+
+        @pl.when(p == 0)
+        def _():
+            for j in range(pos - 1, 0, -1):
                 right_copy(n, j, part.at[n, c, j]).start()
 
-            @pl.when((p == pos - 1) & (j < pos - 1))
-            def _():
+        @pl.when(p == pos - 1)
+        def _():
+            for j in range(pos - 1):
                 left_copy(n, j, part.at[n, c, j]).start()
 
     @pl.loop(0, D)
     def _(n):
+        @pl.when(n == half)
+        def _():
+            last(1, other(1)).wait_recv()
+
         logs = lse_ref[n]
         logs_t = jnp.transpose(jnp.concatenate([logs] * (128 // HEADS), axis=0))
         bias = bias_ref[pl.ds(n, 1), :]
@@ -242,7 +291,7 @@
     chip_sum(D - 1)
 
     def from_left(n):
-        for j in range(1, pos):
+        for j in range(pos - 1, 0, -1):
             @pl.when(j >= p)
             def _():
                 right_copy(n, j, part.at[n, c, j]).wait_recv()
@@ -254,7 +303,7 @@
                 right_copy(n, j, part.at[n, c, j]).start()
 
     def from_right(n):
-        for j in range(pos - 2, -1, -1):
+        for j in range(pos - 1):
             @pl.when(j <= p)
             def _():
                 left_copy(n, j, part.at[n, c, j]).wait_recv()
@@ -301,10 +350,13 @@
     for i in range(1, nb):
         q_copy(i, own).wait_send()
         n_copy(i, own).wait_send()
-    first.wait_send()
-    for i in range(1, pos):
-        z_copy(i, p).wait_send()
-    last.wait_send()
+    for b in range(2):
+        first(b).wait_send()
+        for i in range(1, pos):
+            z_copy(b, i, p).wait_send()
+        last(b, mine(b)).wait_send()
+    for store in stores:
+        store.wait()
 
     @pl.loop(0, D)
     def _(n):
@@ -326,6 +378,7 @@
     rq, dl = latents.shape
     pos = nb // 2
     vmem = pl.BlockSpec(memory_space=pltpu.VMEM)
+    anywhere = pl.BlockSpec(memory_space=pl.ANY)
     dma = pltpu.SemaphoreType.DMA
     return pl.pallas_call(
         functools.partial(forward_kernel, nb),
@@ -338,22 +391,29 @@
             jax.ShapeDtypeStruct((LAT, DQK), BF16),
             jax.ShapeDtypeStruct((D, kc), F32),
         ),
-        in_specs=[vmem, pl.BlockSpec(memory_space=pltpu.SMEM)] + [vmem] * 7,
-        out_specs=(vmem,) * 7,
+        in_specs=[anywhere] * 4 + [pl.BlockSpec(memory_space=pltpu.SMEM)] + [vmem] * 4,
+        out_specs=(vmem, vmem, anywhere, anywhere, vmem, vmem, vmem),
         scratch_shapes=[
+            pltpu.VMEM((D, kc, din), BF16),
+            pltpu.VMEM(w_query.shape, BF16),
+            pltpu.VMEM(w_key.shape, BF16),
+            pltpu.VMEM(w_value.shape, BF16),
+            pltpu.VMEM((D, kc, DQK), BF16),
+            pltpu.VMEM((D, kc, DV), BF16),
             pltpu.VMEM((nb, rq, 256), BF16),
             pltpu.VMEM((D, kc, din), BF16),
             pltpu.VMEM((HEADS, LAT, DQK), BF16),
             pltpu.VMEM((D, HEADS, LAT), F32),
-            pltpu.VMEM((D // 2, HEADS, LAT), F32),
-            pltpu.VMEM((pos, D // 2, HEADS, LAT), F32),
+            pltpu.VMEM((2, D // 4, HEADS, LAT), F32),
+            pltpu.VMEM((2, pos, D // 4, HEADS, LAT), F32),
             pltpu.VMEM((LAT, DV), F32),
             pltpu.VMEM((D, 2, pos, rq, DV), BF16),
             pltpu.VMEM((D, pos, rq, DV), BF16),
             pltpu.VMEM((D, pos, rq, DV), BF16),
             pltpu.VMEM((D, pos, rq, DV), BF16),
+            dma((3,)), dma((D,)), dma((2,)),
             dma((nb - 1,)), dma((nb - 1,)), dma((nb - 1,)), dma((nb - 1,)),
-            dma((pos + 1,)), dma((pos + 1,)),
+            dma((2, pos + 1)), dma((2, pos + 1)),
             dma((D,)), dma((D,)),
             dma((D, pos)), dma((D, pos)), dma((D, pos)), dma((D, pos)),
         ],
@@ -362,7 +422,8 @@
         ),
         name="forward",
     )(
-        byte_embed, doc_lengths, key_mask, latents, gain_query, gain_bytes, w_query, w_key, w_value,
+        byte_embed, w_query, w_key, w_value, doc_lengths, key_mask, latents, gain_query,
+        gain_bytes,
     )
 
 
@@ -558,14 +619,14 @@
         for i in range(1, self.nd):
             self.share(0, i).start()
 
-    def step(self, t, mate_copy):
+    def step(self, t, mate_copy, entered=0):
         def at(t, when, run, turned=False):
             @pl.when((t >= 0) & (t < self.count // self.group) & when)
             def _():
                 for i in range(self.group):
                     run(t * self.group + (self.group - 1 - i if turned else i))
 
-        at(t, True, lambda s: self.begin(s, mate_copy))
+        at(t, t >= entered, lambda s: self.begin(s, mate_copy))
         for k in range(1, self.bits + 1):
             at(t - self.lags[k - 1], True, functools.partial(self.halve, k=k))
         base = t - self.lags[-1]
@@ -629,7 +690,7 @@
     wscr, vscr = refs[24:39], (refs[39:54], refs[54:69])
     (
         wpool, x_ref, k_ref, ga_all, delta_all, delta_t, qm, wkv, ds_all, gv_acc, gq_acc,
-        fpool, frames, low_t, nm, act_low, gm, g_up, gb, stage, vstage, gain_acc, gmlp_acc, direct_out, dir_in,
+        fpool, frames, low_t, acts, gm, g_up, gb, stage, vstage, gain_acc, gmlp_acc, direct_out, dir_in,
         misc_out, misc_in, misc2_out, misc2_in,
         load_s, out_s, bg_s, ar_s, ar_r, al_s, al_r, am_s, am_r, d_s, d_r, dir_s, dir_r,
         m1_s, m1_r, m2_s, m2_r, m3_s, m3_r,
@@ -673,7 +734,7 @@
     load_cot.start()
 
     weights = ShardSums(
-        doc, blk, nd, nb, 3 * pos, wunit, 2, [4 + k for k in range(bits)], False,
+        doc, blk, nd, nb, 3 * pos, wunit, pos, [3 + 3 * k for k in range(bits)], False,
         *wscr[:5], wsum_ref, wscr[5:],
     )
     values = [
@@ -682,7 +743,7 @@
         )
         for g, (lags, out) in enumerate(
             (
-                ([2 + k for k in range(bits)], vsum0_ref),
+                ([1 + k for k in range(bits)], vsum0_ref),
                 ([1 + k for k in range(bits)], vsum1_ref),
             )
         )
@@ -752,6 +813,7 @@
 
         mate_copy(e, p, c).start()
 
+    nm, act_low = acts.at[0], acts.at[1]
     mid = fpool.at[0:rows_all, :]
     xhat = fpool.at[rows_all : 2 * rows_all, :]
     slope = fpool.at[2 * rows_all : 3 * rows_all, :]
@@ -790,6 +852,8 @@
     act_low[...] = act.astype(BF16)
     load_cot.wait()
     gm[...] = frames[1].astype(BF16)
+    pl.semaphore_wait(barrier, nb - 1 + nd - 1)
+    weight_grad(0, act_low, gm)
     load_down.wait()
     frames[0] = mid[...] + dot_nn(act_low[...], slot0[...])
     store_out = pltpu.make_async_copy(frames.at[0], out_hbm, out_s)
@@ -807,6 +871,8 @@
         - xhat[...] * jnp.mean(dxh * xhat[...], axis=-1, keepdims=True)
     )
     gb[...] = mid[...].astype(BF16)
+    for s in range(pos):
+        weights.begin(s, w_mate)
     load_out2.wait()
     ga = dot_nt(gb[...], slot0[...])
     load_v.start()
@@ -815,10 +881,8 @@
             ga_all[g * D + n, own_rows, :] = ga[
                 n * rq : (n + 1) * rq, g * vh : (g + 1) * vh
             ].astype(BF16)
-    pl.semaphore_wait(barrier, nb - 1 + nd - 1)
     for e in range(ahead):
         send_own(e)
-    weight_grad(0, act_low, gm)
     lane = lax.broadcasted_iota(jnp.int32, (rq, 128), 1)
     delta = jnp.zeros((rq, 128), F32)
     for h in range(HEADS):
@@ -917,14 +981,15 @@
 
             @pl.when(n >= 2)
             def _():
-                pltpu.make_async_copy(frames.at[slot, 0:kc, 0:din], bg_hbm.at[n - 2], bg_s.at[slot]).wait()
-
-            frames[slot, 0:kc, 0:din] = inv * (
+                pltpu.make_async_copy(acts.at[slot, 0:kc, 0:din], bg_hbm.at[n - 2], bg_s.at[slot]).wait()
+
+            dx = inv * (
                 dxh
                 - jnp.mean(dxh, axis=-1, keepdims=True)
                 - xh * jnp.mean(dxh * xh, axis=-1, keepdims=True)
             )
-            pltpu.make_async_copy(frames.at[slot, 0:kc, 0:din], bg_hbm.at[n], bg_s.at[slot]).start()
+            acts[slot, 0:kc, 0:din] = dx.astype(BF16)
+            pltpu.make_async_copy(acts.at[slot, 0:kc, 0:din], bg_hbm.at[n], bg_s.at[slot]).start()
         normed_t = jnp.transpose((xh * gb_ref[...].reshape(1, -1)).astype(BF16))
         kv_acc[...] += dot_nn(normed_t, grads_now)
 
@@ -957,7 +1022,7 @@
 
         @pl.when(t % 2 == 0)
         def _():
-            weights.step(t // 2, w_mate)
+            weights.step(t // 2 + 1, w_mate, 1)
             values[0].step(t // 2 - start0, v_mate(0))
 
         @pl.when(t == pos)
@@ -1020,13 +1085,13 @@
     misc_in[blk] = misc_out[blk]
 
     first = (parts + pos + 1) // 2
-    last = max(weights.steps, start0 + values[0].steps, first + values[1].steps)
+    last = max(weights.steps - 1, start0 + values[0].steps, first + values[1].steps)
 
     @pl.loop(first, last)
     def _(t):
         values[1].step(t - first, v_mate(1))
         values[0].step(t - start0, v_mate(0))
-        weights.step(t, w_mate)
+        weights.step(t + 1, w_mate, 1)
 
         @pl.when(t == first + 1)
         def _():
@@ -1063,7 +1128,7 @@
     dsum_ref[...] = total
 
     for n in range(D - 2, D):
-        pltpu.make_async_copy(frames.at[n % 2, 0:kc, 0:din], bg_hbm.at[n], bg_s.at[n % 2]).wait()
+        pltpu.make_async_copy(acts.at[n % 2, 0:kc, 0:din], bg_hbm.at[n], bg_s.at[n % 2]).wait()
     weights.drain()
     for g in range(2):
         values[g].drain()
@@ -1143,8 +1208,7 @@
             pltpu.VMEM((max(3 * rows, din), dl), F32),
             pltpu.VMEM((2, rows, dl), F32),
             pltpu.VMEM((dl, rows), BF16),
-            pltpu.VMEM((rows, dl), BF16),
-            pltpu.VMEM((rows, dl), BF16),
+            pltpu.VMEM((2, rows, dl), BF16),
             pltpu.VMEM((rows, dl), BF16),
             pltpu.VMEM((rows, dl), BF16),
             pltpu.VMEM((rows, dl), BF16),
@@ -1171,7 +1235,7 @@
         functools.partial(backward_kernel, nb, nd, wunit, vunit),
         out_shape=(
             jax.ShapeDtypeStruct((rows, dl), F32),
-            jax.ShapeDtypeStruct((D, kc, din), F32),
+            jax.ShapeDtypeStruct((D, kc, din), BF16),
             jax.ShapeDtypeStruct((3, wunit * nd, whalf), BF16),
             jax.ShapeDtypeStruct((1, vunit * nd, vhalf), BF16),
             jax.ShapeDtypeStruct((1, vunit * nd, vhalf), BF16),
@@ -1197,23 +1261,25 @@
     nb, rows_hbm, bytes_hbm, wsum_hbm, vsum0_ref, vsum1_ref, dsum_ref, gq_ref, gains_ref, cols_ref,
     lat_ref, gain_ref, wq_ref, rows_out, bytes_out, lgrad_ref, gq_gain_ref, gb_gain_ref,
     gm_gain_ref, wq_out, wk_out, wv_out, wo_out, wu_out, wd_out, turned,
-    wsum_ref, bytes_buf, rows_buf, take_s, move_s,
+    wsum_ref, bytes_in, bytes_buf, rows_buf, take_s, move_s,
 ):
     D = bytes_hbm.shape[0]
-    pairs = [(bytes_hbm.at[n], bytes_buf.at[n], bytes_out.at[n]) for n in range(D)]
-    pairs.append((rows_hbm, rows_buf, rows_out))
+    pairs = [(bytes_hbm.at[n], bytes_in.at[n], bytes_buf.at[n], bytes_out.at[n]) for n in range(D)]
+    pairs.append((rows_hbm, rows_buf, rows_buf, rows_out))
     takes = [
-        pltpu.make_async_copy(src, buf, take_s.at[i]) for i, (src, buf, _) in enumerate(pairs)
+        pltpu.make_async_copy(src, buf, take_s.at[i]) for i, (src, buf, _, _) in enumerate(pairs)
     ]
     takes.append(pltpu.make_async_copy(wsum_hbm, wsum_ref, take_s.at[D + 1]))
     moves = [
-        pltpu.make_async_copy(buf, out, move_s.at[i]) for i, (_, buf, out) in enumerate(pairs)
+        pltpu.make_async_copy(buf, out, move_s.at[i]) for i, (_, _, buf, out) in enumerate(pairs)
     ]
     for take in takes:
         take.start()
-    for take, move in zip(takes, moves):
-        take.wait()
-        move.start()
+    for n in range(D + 1):
+        takes[n].wait()
+        if n < D:
+            bytes_buf[n] = bytes_in[n].astype(F32)
+        moves[n].start()
     takes[-1].wait()
     rq, dl = lat_ref.shape
     din, step, vstep = wk_out.shape[0] * nb, dl // nb, wk_out.shape[0]
@@ -1283,6 +1349,7 @@
         scratch_shapes=[
             pltpu.VMEM((256, DQK), F32),
             pltpu.VMEM(wsum.shape, BF16),
+            pltpu.VMEM(byte_grad.shape, BF16),
             pltpu.VMEM(byte_grad.shape, F32),
             pltpu.VMEM(latents_out.shape, F32),
             pltpu.SemaphoreType.DMA((byte_grad.shape[0] + 2,)),

time: 214 us -> 206 us (0.963)
  Pallas kernels: 213 us -> 205 us
    pallas_call x1, Pallas kernels: 87.6 us -> 78.6 us  [forward(): pl.pallas_call(functools.partial(forward_kernel, nb), out_shape=(jax.Shap...]
    pallas_call x1, Pallas kernels: 116 us -> 118 us  [backward(): pl.pallas_call(functools.partial(backward_kernel, nb, nd, wunit, vunit),...]
where the time goes in v5:
time: 206 us
  Pallas kernels  205 us (100%)
    pallas_call x1, Pallas kernels, backward(): pl.pallas_call(functools.partial(backward_kernel, nb, nd, wunit, vunit),...  118 us
    pallas_call x1, Pallas kernels, forward(): pl.pallas_call(functools.partial(forward_kernel, nb), out_shape=(jax.Shap...  78.6 us
    pallas_call x1, Pallas kernels, finish(): pl.pallas_call(functools.partial(finish_kernel, nb), out_shape=tuple((jax...  8.36 us

profile of v5, /device:TPU:0, one launch (start us, length us, event | category | flops | bytes accessed | tf_op | source)
XLA Modules:
  0.0 206.1 jit_solution(14814063362768675592)
XLA Ops:
  0.6 78.6 %forward.1 = (bf16[8,32,1280]{2,1,0:T(8,128)(2,1)}, f32[8,8,256]{2,1,0:T(8,128)}, bf16[8,256,256]{2,1,0:T(8,128)(2,1)}, bf16[8,256,1280]{2,1,0:T(8,128)(2,1)}, b...) custom-call(bf16[8,256,768]{2,1,0:T(8,128)(2,1)} %refs_0_.1, bf16[1280,256]{1,0:T(8,128)(2,1)} %wq_ref.1, ...), custom_call_target="tpu_custom_call" | custom-call | tf_op jit(solution)/shard_map/forward/pallas_call | solution.py:383
  79.3 118.3 %backward.1 = (f32[256,1280]{1,0:T(8,128)}, bf16[8,256,768]{2,1,0:T(8,128)(2,1)}, bf16[3,320,640]{2,1,0:T(8,128)(2,1)}, bf16[1,192,384]{2,1,0:T(8,128)(2,1)}, bf...) custom-call(bf16[8,256,768]{2,1,0:T(8,128)(2,1)} %refs_0_.1, ...), custom_call_target="tpu_custom_call" | custom-call | tf_op jit(solution)/shard_map/backward/pallas_call | solution.py:1234
  197.5 8.4 %finish.1 = (f32[256,1280]{1,0:T(8,128)}, f32[8,256,768]{2,1,0:T(8,128)}, f32[32,1280]{1,0:T(8,128)}, f32[1,160]{1,0:T(1,128)}, f32[1,96]{1,0:T(1,128)}, /*index...) custom-call(f32[256,1280]{1,0:T(8,128)} %get-tuple-element.45.rows_h, ...), custom_call_target="tpu_custom_call" | custom-call | tf_op jit(solution)/shard_map/finish/pallas_call | solution.py:1344

commit v6 on v5

--- a/solution.py
+++ b/solution.py
@@ -638,6 +638,13 @@
         at(base - (self.pos - 1 - self.p), self.p < self.pos - 1, self.from_right)
         at(base - (self.pos - 1), True, self.finish)
 
+    def halved(self):
+        @pl.loop(0, self.count)
+        def _(s):
+            for k in range(self.bits):
+                for i in range(self.width(k)):
+                    self.halving(s, k, i).wait_send()
+
     def drain(self):
         if self.direct:
             for i in range(1, self.pos):
@@ -647,13 +654,11 @@
                 self.shared(m, i).wait_recv()
                 self.share(m, i).wait_send()
 
+        if self.direct:
+            return
+
         @pl.loop(0, self.count)
         def _(s):
-            for k in range(self.bits):
-                for i in range(self.width(k)):
-                    self.halving(s, k, i).wait_send()
-            if self.direct:
-                return
             j = s % self.pos
 
             @pl.when((j > self.p) & (self.p < self.pos - 1))
@@ -665,7 +670,7 @@
                 self.left(s).wait_send()
 
 
-def shard_sum_scratch(nd, nb, count, unit, rows, width):
+def shard_sum_scratch(nd, nb, count, unit, rows, width, direct):
     dma = pltpu.SemaphoreType.DMA
     arrays = count // (nb // 2)
     return [
@@ -673,7 +678,7 @@
         pltpu.VMEM((count, rows, width), BF16),
         pltpu.VMEM((count, nd - 1, unit, width), BF16),
         pltpu.VMEM((count, unit, width), BF16),
-        pltpu.VMEM((count, unit, width), BF16),
+        pltpu.VMEM((1, 16, 128) if direct else (count, unit, width), BF16),
         dma((count,)), dma((count,)),
         dma((count, nd - 1)), dma((count, nd - 1)),
         dma((count,)), dma((count,)), dma((count,)), dma((count,)),
@@ -689,7 +694,7 @@
     out_hbm, bg_hbm, wsum_ref, vsum0_ref, vsum1_ref, dsum_ref, gq_ref, gains_ref = refs[16:24]
     wscr, vscr = refs[24:39], (refs[39:54], refs[54:69])
     (
-        wpool, x_ref, k_ref, ga_all, delta_all, delta_t, qm, wkv, ds_all, gv_acc, gq_acc,
+        wpool, x_ref, k_ref, ga_all, delta_all, delta_t, qm, wkv, gq_acc,
         fpool, frames, low_t, acts, gm, g_up, gb, stage, vstage, gain_acc, gmlp_acc, direct_out, dir_in,
         misc_out, misc_in, misc2_out, misc2_in,
         load_s, out_s, bg_s, ar_s, ar_r, al_s, al_r, am_s, am_r, d_s, d_r, dir_s, dir_r,
@@ -734,7 +739,7 @@
     load_cot.start()
 
     weights = ShardSums(
-        doc, blk, nd, nb, 3 * pos, wunit, pos, [3 + 3 * k for k in range(bits)], False,
+        doc, blk, nd, nb, 3 * pos, wunit, pos, [5 + 3 * k for k in range(bits)], False,
         *wscr[:5], wsum_ref, wscr[5:],
     )
     values = [
@@ -761,7 +766,7 @@
 
     def v_mate(g):
         return lambda s: remote(
-            vstage.at[g, s], values[g].mate_in.at[s],
+            vstage.at[s], values[g].mate_in.at[s],
             values[g].mate_s.at[s], values[g].mate_r.at[s], doc, mate,
         )
 
@@ -940,65 +945,91 @@
     def doc_rows(n):
         return pl.ds(pl.multiple_of(n * kc, kc), kc)
 
-    def bytes_back(g, n):
+    def scores_back(g, n, i):
         e = g * D + n
-        for j in range(pos):
-            mate_copy(e, j, 1 - c).wait_recv()
         bias = wide(row_to_lanes(bias_ref[pl.ds(n, 1), :]), LAT)
         logs, deltas = lse_ref[n], delta_t[n]
         kn = k_ref[n, :, g * qh : (g + 1) * qh]
         kt = jnp.transpose(kn)
-        gv_acc[...] = jnp.zeros_like(gv_acc)
-        for i in range(hh):
-            h = g * hh + i
-            cols = slice(window(i), window(i) + 256)
-            vcols = slice(g * vh + window(i), g * vh + window(i) + 256)
-            gah = ga_all[e, :, cols] * value_mask(i, LAT)
+        gk = None
+        for k in range(hh):
+            h, at = g * hh + k, window(k)
+            vcols = slice(g * vh + at, g * vh + at + 256)
+            gah = ga_all[e, :, at : at + 256] * value_mask(k, LAT)
             s = dot_nt(kn, qm[h]) * SCORE2 + bias
             prob = jnp.exp2(s - logs[h : h + 1, :])
             dprob = dot_nt(wpool[doc_rows(n), vcols], gah)
             ds = (prob * (dprob - deltas[h : h + 1, :])).astype(BF16)
-            ds_all[:, i * LAT : (i + 1) * LAT] = ds
-            gv_acc[:, cols] += dot_nn(prob.astype(BF16), gah)
-            head = slice(QK_HEAD * i, QK_HEAD * (i + 1))
+            gv = dot_nn(prob.astype(BF16), gah)
+            if k == 0:
+                frames[i, 0:kc, 0:128] = gv[:, 0:128]
+            else:
+                frames[i, 0:kc, at : at + 128] += gv[:, 0:128]
+            frames[i, 0:kc, at + 128 : at + 256] = gv[:, 128:256]
+            part = dot_nn(ds, qm[h])
+            gk = part if k == 0 else gk + part
             rows = slice(QK_HEAD * h, QK_HEAD * (h + 1))
-            gq_acc[rows, :] += dot_nn(kt[head, :], ds)
-        gk = dot_nn(ds_all[:, 0:LAT], qm[g * hh])
-        for i in range(1, hh):
-            gk = gk + dot_nn(ds_all[:, i * LAT : (i + 1) * LAT], qm[g * hh + i])
-        grads_now = jnp.concatenate(
-            [gv_acc[...].astype(BF16), (gk * SCORE_SCALE).astype(BF16)], axis=1
-        )
-        xh, inv = norm_parts(x_ref[n].astype(F32))
-        kept = stage.at[doc_rows(n), 0:din]
+            gq_acc[rows, :] += dot_nn(kt[QK_HEAD * k : QK_HEAD * (k + 1), :], ds)
+        return jnp.concatenate(
+            [frames[i, 0:kc, 0:vh].astype(BF16), (gk * SCORE_SCALE).astype(BF16)], axis=1
+        )
+
+    def wave(w):
+        @pl.when(w < parts - ahead)
+        def _():
+            send_own(w + ahead)
+
+        for hop in range(pos - 1):
+            @pl.when((w >= hop) & (w - hop < parts))
+            def _():
+                forward_chunks(w - hop, hop)
+
+    def bytes_back(g, m, w):
+        n0 = 2 * m
+        both = []
+        for i in range(2):
+            if i == 1:
+                wave(w)
+            for j in range(pos):
+                mate_copy(g * D + n0 + i, j, 1 - c).wait_recv()
+            both.append(scores_back(g, n0 + i, i))
+        grads = jnp.concatenate(both, axis=0)
+        xh, inv = norm_parts(x_ref[pl.ds(n0, 2)].reshape(2 * kc, din).astype(F32))
+        kept = stage.at[pl.ds(pl.multiple_of(n0 * kc, 2 * kc), 2 * kc), 0:din]
         if g == 0:
-            kept[...] = dot_nt(grads_now, wkv[0]).astype(BF16)
+            kept[...] = dot_nt(grads, wkv[0]).astype(BF16)
         else:
-            gx = kept[...].astype(F32) + dot_nt(grads_now, wkv[1])
+            gx = kept[...].astype(F32) + dot_nt(grads, wkv[1])
             gain_acc[...] += jnp.sum(gx * xh, axis=0, keepdims=True)
             dxh = gx * gb_ref[...].reshape(1, -1)
-            slot = lax.rem(n, 2)
-
-            @pl.when(n >= 2)
-            def _():
-                pltpu.make_async_copy(acts.at[slot, 0:kc, 0:din], bg_hbm.at[n - 2], bg_s.at[slot]).wait()
-
             dx = inv * (
                 dxh
                 - jnp.mean(dxh, axis=-1, keepdims=True)
                 - xh * jnp.mean(dxh * xh, axis=-1, keepdims=True)
             )
-            acts[slot, 0:kc, 0:din] = dx.astype(BF16)
-            pltpu.make_async_copy(acts.at[slot, 0:kc, 0:din], bg_hbm.at[n], bg_s.at[slot]).start()
+            for i in range(2):
+                @pl.when(m >= 1)
+                def _():
+                    pltpu.make_async_copy(
+                        acts.at[i, 0:kc, 0:din], bg_hbm.at[n0 + i - 2], bg_s.at[i]
+                    ).wait()
+
+                acts[i, 0:kc, 0:din] = dx[i * kc : (i + 1) * kc, :].astype(BF16)
+                pltpu.make_async_copy(
+                    acts.at[i, 0:kc, 0:din], bg_hbm.at[n0 + i], bg_s.at[i]
+                ).start()
         normed_t = jnp.transpose((xh * gb_ref[...].reshape(1, -1)).astype(BF16))
-        kv_acc[...] += dot_nn(normed_t, grads_now)
+        kv_acc[...] += dot_nn(normed_t, grads)
 
     def cut_values(g):
         step = din // nb
+        if g == 1:
+            for s in range(pos):
+                v_mate(0)(s).wait_send()
         for s in range(pos):
             for core in (1 - c, c):
                 rows = pl.ds(pl.multiple_of((2 * s + core) * step, step), step)
-                to = values[g].own if core is c else vstage.at[g]
+                to = values[g].own if core is c else vstage
                 for i in range(2):
                     to[s, i * step : (i + 1) * step, :] = fpool[
                         rows, i * vhalf : (i + 1) * vhalf
@@ -1007,25 +1038,21 @@
         if g == 0:
             kv_acc[...] = jnp.zeros((din, vh + qh), F32)
 
-    start0 = (pos + D + 2) // 2
-
-    @pl.loop(0, parts + pos)
+    pairs, fill = D // 2, pos // 2
+    start0 = fill + pairs + 1
+
+    @pl.loop(0, 2 * pairs + fill)
     def _(t):
-        @pl.when(t < parts - ahead)
-        def _():
-            send_own(t + ahead)
-
-        for hop in range(pos - 1):
-            @pl.when((t >= hop) & (t - hop < parts))
-            def _():
-                forward_chunks(t - hop, hop)
-
-        @pl.when(t % 2 == 0)
-        def _():
-            weights.step(t // 2 + 1, w_mate, 1)
-            values[0].step(t // 2 - start0, v_mate(0))
-
-        @pl.when(t == pos)
+        wave(2 * t)
+
+        @pl.when(t < fill)
+        def _():
+            wave(2 * t + 1)
+
+        weights.step(t + 1, w_mate, 1)
+        values[0].step(t - start0, v_mate(0))
+
+        @pl.when(t == fill)
         def _():
             for i in range(1, nb):
                 src = lax.rem(blk + nb - i, nb)
@@ -1040,17 +1067,17 @@
             for s in range(pos, 3 * pos):
                 w_mate(s).wait_send()
 
-        @pl.when((t >= pos) & (t < pos + D))
-        def _():
-            bytes_back(0, t - pos)
-
-        @pl.when(t == pos + D)
+        @pl.when((t >= fill) & (t < fill + pairs))
+        def _():
+            bytes_back(0, t - fill, 2 * t + 1)
+
+        @pl.when(t == fill + pairs)
         def _():
             cut_values(0)
 
-        @pl.when(t >= pos + D)
-        def _():
-            bytes_back(1, t - pos - D)
+        @pl.when(t >= fill + pairs)
+        def _():
+            bytes_back(1, t - fill - pairs, 2 * t + 1)
 
     cut_values(1)
 
@@ -1084,7 +1111,48 @@
         misc1(i, blk).start()
     misc_in[blk] = misc_out[blk]
 
-    first = (parts + pos + 1) // 2
+    @pl.loop(0, parts)
+    def _(e):
+        mate_copy(e, p, c).wait_send()
+
+        @pl.when(p < pos - 1)
+        def _():
+            right_copy(e, 0, p).wait_send()
+
+        @pl.when(p > 0)
+        def _():
+            left_copy(e, 0, p).wait_send()
+
+        for hop in range(pos - 1):
+            j = p - 1 - hop
+
+            @pl.when(j >= 0)
+            def _():
+                mate_copy(e, j, c).wait_send()
+                if hop + 1 < pos - 1:
+                    @pl.when(p < pos - 1)
+                    def _():
+                        right_copy(e, hop + 1, j).wait_send()
+
+            i = p + 1 + hop
+
+            @pl.when(i < pos)
+            def _():
+                mate_copy(e, i, c).wait_send()
+                if hop + 1 < pos - 1:
+                    @pl.when(p > 0)
+                    def _():
+                        left_copy(e, hop + 1, i).wait_send()
+
+    total = direct_out[...].astype(F32)
+    for i in range(1, nd):
+        direct_copy(i).wait_recv()
+        total = total + dir_in[i - 1].astype(F32)
+    dsum_ref[...] = total
+
+    for n in range(D - 2, D):
+        pltpu.make_async_copy(acts.at[n % 2, 0:kc, 0:din], bg_hbm.at[n], bg_s.at[n % 2]).wait()
+    first = 2 * pairs + fill
     last = max(weights.steps - 1, start0 + values[0].steps, first + values[1].steps)
 
     @pl.loop(first, last)
@@ -1093,7 +1161,7 @@
         values[0].step(t - start0, v_mate(0))
         weights.step(t + 1, w_mate, 1)
 
-        @pl.when(t == first + 1)
+        @pl.when(t == first)
         def _():
             for i in range(1, nb):
                 misc1(i, lax.rem(blk + nb - i, nb)).wait_recv()
@@ -1105,13 +1173,15 @@
                 misc2(i, doc).start()
             misc2_in[doc] = misc2_out[...]
 
-        @pl.when(t == first + 3)
+        @pl.when(t == first + 1)
         def _():
             for i in range(1, nd):
                 misc2(i, lax.rem(doc + nd - i, nd)).wait_recv()
             total = misc2_in[0].astype(F32)
             for i in range(1, nd):
                 total = total + misc2_in[i].astype(F32)
+            weights.halved()
+            values[0].halved()
             gains_ref[...] = total[rq : rq + 8, :]
             gq_ref[own_rows, :] = total[0:rq].astype(BF16)
             for i in range(1, nb):
@@ -1121,19 +1191,12 @@
         src = lax.rem(blk + nb - i, nb)
         misc3(i, pl.ds(pl.multiple_of(src * rq, rq), rq)).wait_recv()
 
-    total = direct_out[...].astype(F32)
-    for i in range(1, nd):
-        direct_copy(i).wait_recv()
-        total = total + dir_in[i - 1].astype(F32)
-    dsum_ref[...] = total
-
-    for n in range(D - 2, D):
-        pltpu.make_async_copy(acts.at[n % 2, 0:kc, 0:din], bg_hbm.at[n], bg_s.at[n % 2]).wait()
+    values[1].halved()
     weights.drain()
     for g in range(2):
         values[g].drain()
-        for s in range(pos):
-            v_mate(g)(s).wait_send()
+    for s in range(pos):
+        v_mate(1)(s).wait_send()
     for i in range(1, nb):
         delta_copy(i, own_rows).wait_send()
         misc1(i, blk).wait_send()
@@ -1141,39 +1204,6 @@
     for i in range(1, nd):
         direct_copy(i).wait_send()
         misc2(i, doc).wait_send()
-
-    @pl.loop(0, parts)
-    def _(e):
-        mate_copy(e, p, c).wait_send()
-
-        @pl.when(p < pos - 1)
-        def _():
-            right_copy(e, 0, p).wait_send()
-
-        @pl.when(p > 0)
-        def _():
-            left_copy(e, 0, p).wait_send()
-
-        for hop in range(pos - 1):
-            j = p - 1 - hop
-
-            @pl.when(j >= 0)
-            def _():
-                mate_copy(e, j, c).wait_send()
-                if hop + 1 < pos - 1:
-                    @pl.when(p < pos - 1)
-                    def _():
-                        right_copy(e, hop + 1, j).wait_send()
-
-            i = p + 1 + hop
-
-            @pl.when(i < pos)
-            def _():
-                mate_copy(e, i, c).wait_send()
-                if hop + 1 < pos - 1:
-                    @pl.when(p > 0)
-                    def _():
-                        left_copy(e, hop + 1, i).wait_send()
 
 
 def backward(
@@ -1190,9 +1220,9 @@
     anywhere = pl.BlockSpec(memory_space=pl.ANY)
     dma = pltpu.SemaphoreType.DMA
     scratch = (
-        shard_sum_scratch(nd, nb, 3 * pos, wunit, 2 * dl // nb, whalf)
-        + shard_sum_scratch(nd, nb, pos, vunit, 2 * din // nb, vhalf)
-        + shard_sum_scratch(nd, nb, pos, vunit, 2 * din // nb, vhalf)
+        shard_sum_scratch(nd, nb, 3 * pos, wunit, 2 * dl // nb, whalf, False)
+        + shard_sum_scratch(nd, nb, pos, vunit, 2 * din // nb, vhalf, True)
+        + shard_sum_scratch(nd, nb, pos, vunit, 2 * din // nb, vhalf, True)
         + [
             pltpu.VMEM((max(2 * dl, D * kc), dl), BF16),
             pltpu.VMEM((D, kc, din), BF16),
@@ -1202,8 +1232,6 @@
             pltpu.VMEM((D, HEADS, LAT), F32),
             pltpu.VMEM((HEADS, LAT, DQK // 2), BF16),
             pltpu.VMEM((2, din, (DV + DQK) // 2), BF16),
-            pltpu.VMEM((kc, HEADS // 2 * LAT), BF16),
-            pltpu.VMEM((kc, DV // 2), F32),
             pltpu.VMEM((DQK, LAT), F32),
             pltpu.VMEM((max(3 * rows, din), dl), F32),
             pltpu.VMEM((2, rows, dl), F32),
@@ -1213,7 +1241,7 @@
             pltpu.VMEM((rows, dl), BF16),
             pltpu.VMEM((rows, dl), BF16),
             pltpu.VMEM((max(2 * dl, D * kc), (DV + DQK) // 2), BF16),
-            pltpu.VMEM((2, pos, 2 * din // nb, vhalf), BF16),
+            pltpu.VMEM((pos, 2 * din // nb, vhalf), BF16),
             pltpu.VMEM((1, din), F32),
             pltpu.VMEM((1, dl), F32),
             pltpu.VMEM((rq, dl), BF16),

time: 206 us -> 199 us (0.966)
  Pallas kernels: 205 us -> 197 us
    pallas_call x1, Pallas kernels: 118 us -> 110 us  [backward(): pl.pallas_call(functools.partial(backward_kernel, nb, nd, wunit, vunit),...]
where the time goes in v6:
time: 199 us; the launch traced here: 198 us
  Pallas kernels  197 us (99%)
    pallas_call x1, Pallas kernels, backward(): pl.pallas_call(functools.partial(backward_kernel, nb, nd, wunit, vunit),...  110 us
    pallas_call x1, Pallas kernels, forward(): pl.pallas_call(functools.partial(forward_kernel, nb), out_shape=(jax.Shap...  78.6 us
    pallas_call x1, Pallas kernels, finish(): pl.pallas_call(functools.partial(finish_kernel, nb), out_shape=tuple((jax...  8.36 us

profile of v6, /device:TPU:0, one launch (start us, length us, event | category | flops | bytes accessed | tf_op | source)
XLA Modules:
  0.0 197.8 jit_solution(7753356846453514859)
XLA Ops:
  0.6 78.6 %forward.1 = (bf16[8,32,1280]{2,1,0:T(8,128)(2,1)}, f32[8,8,256]{2,1,0:T(8,128)}, bf16[8,256,256]{2,1,0:T(8,128)(2,1)}, bf16[8,256,1280]{2,1,0:T(8,128)(2,1)}, b...) custom-call(bf16[8,256,768]{2,1,0:T(8,128)(2,1)} %refs_0_.1, bf16[1280,256]{1,0:T(8,128)(2,1)} %wq_ref.1, ...), custom_call_target="tpu_custom_call" | custom-call | tf_op jit(solution)/shard_map/forward/pallas_call | solution.py:383
  79.3 110.0 %backward.1 = (f32[256,1280]{1,0:T(8,128)}, bf16[8,256,768]{2,1,0:T(8,128)(2,1)}, bf16[3,320,640]{2,1,0:T(8,128)(2,1)}, bf16[1,192,384]{2,1,0:T(8,128)(2,1)}, bf...) custom-call(bf16[8,256,768]{2,1,0:T(8,128)(2,1)} %refs_0_.1, ...), custom_call_target="tpu_custom_call" | custom-call | tf_op jit(solution)/shard_map/backward/pallas_call | solution.py:1262
  189.3 8.4 %finish.1 = (f32[256,1280]{1,0:T(8,128)}, f32[8,256,768]{2,1,0:T(8,128)}, f32[32,1280]{1,0:T(8,128)}, f32[1,160]{1,0:T(1,128)}, f32[1,96]{1,0:T(1,128)}, /*index...) custom-call(f32[256,1280]{1,0:T(8,128)} %get-tuple-element.45.rows_h, ...), custom_call_target="tpu_custom_call" | custom-call | tf_op jit(solution)/shard_map/finish/pallas_call | solution.py:1372

commit v7 on v6

--- a/solution.py
+++ b/solution.py
@@ -274,12 +274,17 @@
         logs_t = jnp.transpose(jnp.concatenate([logs] * (128 // HEADS), axis=0))
         bias = bias_ref[pl.ds(n, 1), :]
         kn = k_ref[n]
-        acc[...] = jnp.zeros_like(acc)
         for h in range(HEADS):
             s = dot_nt(qm[h], kn) * SCORE2 + bias
             prob = jnp.exp2(s - logs_t[:, h : h + 1]).astype(BF16)
             cols = slice(window(h), window(h) + 256)
-            acc[:, cols] += dot_nn(prob, v_ref[n, :, cols] * value_mask(h, kc))
+            out = dot_nn(prob, v_ref[n, :, cols] * value_mask(h, kc))
+            at = window(h)
+            if h % (HEADS // 2) == 0:
+                acc[:, at : at + 128] = out[:, 0:128]
+            else:
+                acc[:, at : at + 128] += out[:, 0:128]
+            acc[:, at + 128 : at + 256] = out[:, 128:256]
         for j in range(nb):
             part[n, j % 2, j // 2] = acc[rq * j : rq * (j + 1), :].astype(BF16)
         mate_copy(n).start()

time: 199 us -> 199 us (level)
  no operation moved by 1% of the time
where the time goes in v7:
time: 199 us; the launch traced here: 198 us
  Pallas kernels  197 us (99%)
    pallas_call x1, Pallas kernels, backward(): pl.pallas_call(functools.partial(backward_kernel, nb, nd, wunit, vunit),...  110 us
    pallas_call x1, Pallas kernels, forward(): pl.pallas_call(functools.partial(forward_kernel, nb), out_shape=(jax.Shap...  78.6 us
    pallas_call x1, Pallas kernels, finish(): pl.pallas_call(functools.partial(finish_kernel, nb), out_shape=tuple((jax...  8.36 us

profile of v7, /device:TPU:0, one launch (start us, length us, event | category | flops | bytes accessed | tf_op | source)
XLA Modules:
  0.0 197.8 jit_solution(12574885140571031582)
XLA Ops:
  0.6 78.6 %forward.1 = (bf16[8,32,1280]{2,1,0:T(8,128)(2,1)}, f32[8,8,256]{2,1,0:T(8,128)}, bf16[8,256,256]{2,1,0:T(8,128)(2,1)}, bf16[8,256,1280]{2,1,0:T(8,128)(2,1)}, b...) custom-call(bf16[8,256,768]{2,1,0:T(8,128)(2,1)} %refs_0_.1, bf16[1280,256]{1,0:T(8,128)(2,1)} %wq_ref.1, ...), custom_call_target="tpu_custom_call" | custom-call | tf_op jit(solution)/shard_map/forward/pallas_call | solution.py:388
  79.3 110.0 %backward.1 = (f32[256,1280]{1,0:T(8,128)}, bf16[8,256,768]{2,1,0:T(8,128)(2,1)}, bf16[3,320,640]{2,1,0:T(8,128)(2,1)}, bf16[1,192,384]{2,1,0:T(8,128)(2,1)}, bf...) custom-call(bf16[8,256,768]{2,1,0:T(8,128)(2,1)} %refs_0_.1, ...), custom_call_target="tpu_custom_call" | custom-call | tf_op jit(solution)/shard_map/backward/pallas_call | solution.py:1267
  189.3 8.4 %finish.1 = (f32[256,1280]{1,0:T(8,128)}, f32[8,256,768]{2,1,0:T(8,128)}, f32[32,1280]{1,0:T(8,128)}, f32[1,160]{1,0:T(1,128)}, f32[1,96]{1,0:T(1,128)}, /*index...) custom-call(f32[256,1280]{1,0:T(8,128)} %get-tuple-element.45.rows_h, ...), custom_call_target="tpu_custom_call" | custom-call | tf_op jit(solution)/shard_map/finish/pallas_call | solution.py:1377
